TPU v7x, 32 devices: a whole 2x2x4 slice. The times are simulated.
32 devices in a mesh: clip: 16 (over z, y, core), map: 2 (over x).
Axes of the slice: x: 2, y: 2, z: 4, core: 2. Of those that a mesh axis runs over, the one named last changes fastest.
Arguments:
- patches: bfloat16 [2, 32, 32, 196, 768], P(None, 'clip', 'map'), may hold values from -6 to 6
- keep: int32 [2, 32, 32, 196], P(None, 'clip', 'map'), may hold values 0 or 1
- tl_gain: bfloat16 [768], P('clip'), may hold values from 0.099609375 to 1.8984375
- tl_bias: bfloat16 [768], P('clip'), may hold values from -3 to 3
- map_w1: bfloat16 [768, 64], P('clip'), may hold values from -0.21875 to 0.21875
- map_b1: bfloat16 [64], P('clip'), may hold values from -3 to 3
- map_w2: bfloat16 [64, 8], P('clip'), may hold values from -1.5 to 1.5
- map_b2: bfloat16 [8], replicated, may hold values from -3 to 3
- ln1_gain: bfloat16 [768], P('clip'), may hold values from 0.099609375 to 1.8984375
- ln1_bias: bfloat16 [768], P('clip'), may hold values from -3 to 3
- qkv_weight: bfloat16 [768, 2304], P('clip'), may hold values from -0.21875 to 0.21875
- qv_bias: bfloat16 [2, 768], P(None, 'clip'), may hold values from -3 to 3
- out_weight: bfloat16 [768, 768], P('clip'), may hold values from -0.625 to 0.625
- out_bias: bfloat16 [768], P('clip'), may hold values from -3 to 3
- ln2_gain: bfloat16 [768], P('clip'), may hold values from 0.099609375 to 1.8984375
- ln2_bias: bfloat16 [768], P('clip'), may hold values from -3 to 3
- fc1_weight: bfloat16 [768, 3072], P('clip'), may hold values from -0.21875 to 0.21875
- fc1_bias: bfloat16 [3072], P('clip'), may hold values from -3 to 3
- fc2_weight: bfloat16 [3072, 768], P('clip'), may hold values from -0.15625 to 0.15625
- fc2_bias: bfloat16 [768], P('clip'), may hold values from -3 to 3
- cotangent: bfloat16 [2, 32, 256, 768], P(None, ('clip', 'map')), may hold values from -6 to 6
Outputs:
- layer_out: bfloat16 [2, 32, 256, 768], P(None, ('clip', 'map'))
- patch_grad: bfloat16 [2, 32, 32, 196, 768], P(None, 'clip', 'map')
- tl_gain_grad: float32 [768], P('clip')
- tl_bias_grad: float32 [768], P('clip')
- map_w1_grad: float32 [768, 64], P('clip')
- map_b1_grad: float32 [64], P('clip')
- map_w2_grad: float32 [64, 8], P('clip')
- map_b2_grad: float32 [8], replicated
- ln1_gain_grad: float32 [768], P('clip')
- ln1_bias_grad: float32 [768], P('clip')
- qkv_weight_grad: float32 [768, 2304], P('clip')
- qv_bias_grad: float32 [2, 768], P(None, 'clip')
- out_weight_grad: float32 [768, 768], P('clip')
- out_bias_grad: float32 [768], P('clip')
- ln2_gain_grad: float32 [768], P('clip')
- ln2_bias_grad: float32 [768], P('clip')
- fc1_weight_grad: float32 [768, 3072], P('clip')
- fc1_bias_grad: float32 [3072], P('clip')
- fc2_weight_grad: float32 [3072, 768], P('clip')
- fc2_bias_grad: float32 [768], P('clip')
Inputs may be any that keep to these rules, and one draw needn't show every extreme that they name: `keep`: 1 keeps a patch, 0 drops it.
All inputs are finite; a program needn't handle non-finite values. No bound on the sum of `keep` on one device may be relied on, other than what follows from the above.
Results may differ from a plain program's by a relative error of at most 0.03.
Values may be sent and summed in bfloat16 or wider, within the bound.
A program may use at most 320 MiB of HBM per device.

v0:
```python
import jax
import jax.numpy as jnp
from jax import lax
from jax.sharding import PartitionSpec as P

HEADS = 12
HEAD = 64
MAPS = 8


EPSILON = 1e-06


def normalize(values_in, gain_in, shift_in):
    center = jnp.mean(values_in, axis=-1, keepdims=True)
    centered = values_in - center
    spread = jnp.mean(centered * centered, axis=-1, keepdims=True)
    return centered * lax.rsqrt(spread + EPSILON) * gain_in + shift_in


def gelu_tanh(value_in):
    return (
        0.5
        * value_in
        * (
            1.0
            + jnp.tanh(0.7978845608028654 * (value_in + 0.044715 * value_in * value_in * value_in))
        )
    )


def softmax_rows(scores):
    peak = jnp.max(scores, axis=-1, keepdims=True)
    expo = jnp.exp(scores - peak)
    return expo / jnp.sum(expo, axis=-1, keepdims=True)


def gather_weights(shards):
    return (
        lax.all_gather(shards[0], "clip", axis=0, tiled=True),
        lax.all_gather(shards[1], "clip", axis=0, tiled=True),
        lax.all_gather(shards[2], "clip", axis=0, tiled=True),
        lax.all_gather(shards[3], "clip", axis=0, tiled=True),
        lax.all_gather(shards[4], "clip", axis=0, tiled=True),
        lax.all_gather(shards[5], "clip", axis=0, tiled=True),
        lax.all_gather(shards[6], "clip", axis=0, tiled=True),
        lax.all_gather(shards[7], "clip", axis=0, tiled=True),
        lax.all_gather(shards[8], "clip", axis=1, tiled=True),
        lax.all_gather(shards[9], "clip", axis=0, tiled=True),
        lax.all_gather(shards[10], "clip", axis=0, tiled=True),
        lax.all_gather(shards[11], "clip", axis=0, tiled=True),
        lax.all_gather(shards[12], "clip", axis=0, tiled=True),
        lax.all_gather(shards[13], "clip", axis=0, tiled=True),
        lax.all_gather(shards[14], "clip", axis=0, tiled=True),
        lax.all_gather(shards[15], "clip", axis=0, tiled=True),
        lax.all_gather(shards[16], "clip", axis=0, tiled=True),
    )


def reduce_grads(grads):
    return (
        lax.psum_scatter(
            grads[0].astype(jnp.bfloat16), "clip", scatter_dimension=0, tiled=True
        ).astype(jnp.float32),
        lax.psum_scatter(
            grads[1].astype(jnp.bfloat16), "clip", scatter_dimension=0, tiled=True
        ).astype(jnp.float32),
        lax.psum_scatter(
            grads[2].astype(jnp.bfloat16), "clip", scatter_dimension=0, tiled=True
        ).astype(jnp.float32),
        lax.psum_scatter(
            grads[3].astype(jnp.bfloat16), "clip", scatter_dimension=0, tiled=True
        ).astype(jnp.float32),
        lax.psum_scatter(
            grads[4].astype(jnp.bfloat16), "clip", scatter_dimension=0, tiled=True
        ).astype(jnp.float32),
        lax.psum_scatter(
            grads[5].astype(jnp.bfloat16), "clip", scatter_dimension=0, tiled=True
        ).astype(jnp.float32),
        lax.psum_scatter(
            grads[6].astype(jnp.bfloat16), "clip", scatter_dimension=0, tiled=True
        ).astype(jnp.float32),
        lax.psum_scatter(
            grads[7].astype(jnp.bfloat16), "clip", scatter_dimension=0, tiled=True
        ).astype(jnp.float32),
        lax.psum_scatter(
            grads[8].astype(jnp.bfloat16), "clip", scatter_dimension=1, tiled=True
        ).astype(jnp.float32),
        lax.psum_scatter(
            grads[9].astype(jnp.bfloat16), "clip", scatter_dimension=0, tiled=True
        ).astype(jnp.float32),
        lax.psum_scatter(
            grads[10].astype(jnp.bfloat16), "clip", scatter_dimension=0, tiled=True
        ).astype(jnp.float32),
        lax.psum_scatter(
            grads[11].astype(jnp.bfloat16), "clip", scatter_dimension=0, tiled=True
        ).astype(jnp.float32),
        lax.psum_scatter(
            grads[12].astype(jnp.bfloat16), "clip", scatter_dimension=0, tiled=True
        ).astype(jnp.float32),
        lax.psum_scatter(
            grads[13].astype(jnp.bfloat16), "clip", scatter_dimension=0, tiled=True
        ).astype(jnp.float32),
        lax.psum_scatter(
            grads[14].astype(jnp.bfloat16), "clip", scatter_dimension=0, tiled=True
        ).astype(jnp.float32),
        lax.psum_scatter(
            grads[15].astype(jnp.bfloat16), "clip", scatter_dimension=0, tiled=True
        ).astype(jnp.float32),
        lax.psum_scatter(
            grads[16].astype(jnp.bfloat16), "clip", scatter_dimension=0, tiled=True
        ).astype(jnp.float32),
    )


def column_sum(values_in):
    return jnp.sum(values_in.astype(jnp.float32), axis=0)


def as_float(values_in):
    return values_in.astype(jnp.float32)


def run_batch(full, map_b2, batch_patches, batch_keep, batch_cot):
    (
        tl_gain,
        tl_bias,
        map_w1,
        map_b1,
        map_w2,
        ln1_gain,
        ln1_bias,
        qkv_weight,
        qv_bias,
        out_weight,
        out_bias,
        ln2_gain,
        ln2_bias,
        fc1_weight,
        fc1_bias,
        fc2_weight,
        fc2_bias,
    ) = full
    group, frames_dev, count, width = batch_patches.shape
    frame_rows = group * frames_dev
    patch_rows = frame_rows * count
    pool_scale = count ** (-0.5)
    head_scale = HEAD ** (-0.5)
    flat_patches = batch_patches.reshape(patch_rows, width)
    frame_patches = batch_patches.reshape(frame_rows, count, width)
    keep_rows = batch_keep.reshape(patch_rows, 1).astype(jnp.float32)
    tl_normed, norm0_back = jax.vjp(
        normalize, flat_patches.astype(jnp.float32), as_float(tl_gain), as_float(tl_bias)
    )
    tl_low = tl_normed.astype(jnp.bfloat16)
    map_pre = jnp.dot(tl_low, map_w1, preferred_element_type=jnp.float32) + as_float(map_b1)
    map_act, gelu0_back = jax.vjp(gelu_tanh, map_pre)
    act0_low = map_act.astype(jnp.bfloat16)
    map_logit = jnp.dot(act0_low, map_w2, preferred_element_type=jnp.float32) + as_float(map_b2)

    def select_fn(logit_in):
        return jax.nn.sigmoid(logit_in) * keep_rows

    selection, select_back = jax.vjp(select_fn, map_logit)
    sel_low = selection.astype(jnp.bfloat16).reshape(frame_rows, count, MAPS)
    pooled = (
        jnp.einsum("npk,npd->nkd", sel_low, frame_patches, preferred_element_type=jnp.float32)
        * pool_scale
    )
    pooled_low = pooled.astype(jnp.bfloat16).reshape(group, frames_dev, MAPS, width)
    owned = lax.all_to_all(pooled_low, "map", split_axis=0, concat_axis=1, tiled=True)
    clips_dev = owned.shape[0]
    seq_len = owned.shape[1] * MAPS
    token_rows = clips_dev * seq_len
    tokens = owned.reshape(token_rows, width).astype(jnp.float32)
    normed1, norm1_back = jax.vjp(normalize, tokens, as_float(ln1_gain), as_float(ln1_bias))
    n1_low = normed1.astype(jnp.bfloat16)
    bias_three = jnp.concatenate(
        [as_float(qv_bias[0]), jnp.zeros((width,), jnp.float32), as_float(qv_bias[1])]
    )
    joined = jnp.dot(n1_low, qkv_weight, preferred_element_type=jnp.float32) + bias_three
    joined_low = joined.astype(jnp.bfloat16)
    queries = joined_low[:, :width].reshape(clips_dev, seq_len, HEADS, HEAD)
    keys_all = joined_low[:, width : 2 * width].reshape(clips_dev, seq_len, HEADS, HEAD)
    values_all = joined_low[:, 2 * width :].reshape(clips_dev, seq_len, HEADS, HEAD)
    scores = (
        jnp.einsum("cqhe,ckhe->chqk", queries, keys_all, preferred_element_type=jnp.float32)
        * head_scale
    )
    soft_out, soft_back = jax.vjp(softmax_rows, scores)
    soft_low = soft_out.astype(jnp.bfloat16)
    attended = jnp.einsum(
        "chqk,ckhe->cqhe", soft_low, values_all, preferred_element_type=jnp.float32
    )
    att_low = attended.astype(jnp.bfloat16).reshape(token_rows, width)
    branch = jnp.dot(att_low, out_weight, preferred_element_type=jnp.float32) + as_float(out_bias)
    mixed_rows = tokens + branch
    normed2, norm2_back = jax.vjp(normalize, mixed_rows, as_float(ln2_gain), as_float(ln2_bias))
    n2_low = normed2.astype(jnp.bfloat16)
    inner_pre = jnp.dot(n2_low, fc1_weight, preferred_element_type=jnp.float32) + as_float(fc1_bias)
    inner_act, gelu1_back = jax.vjp(gelu_tanh, inner_pre)
    act1_low = inner_act.astype(jnp.bfloat16)
    outer_out = jnp.dot(act1_low, fc2_weight, preferred_element_type=jnp.float32) + as_float(
        fc2_bias
    )
    layer_rows = (mixed_rows + outer_out).astype(jnp.bfloat16).reshape(clips_dev, seq_len, width)
    grad_out = batch_cot.reshape(token_rows, width).astype(jnp.float32)
    grad_outer = grad_out.astype(jnp.bfloat16)
    fc2_bias_grad = column_sum(grad_outer)
    fc2_weight_grad = jnp.dot(act1_low.T, grad_outer, preferred_element_type=jnp.float32)
    grad_act1 = jnp.dot(grad_outer, fc2_weight.T, preferred_element_type=jnp.float32)
    grad_inner = gelu1_back(grad_act1)[0].astype(jnp.bfloat16)
    fc1_bias_grad = column_sum(grad_inner)
    fc1_weight_grad = jnp.dot(n2_low.T, grad_inner, preferred_element_type=jnp.float32)
    grad_normed2 = jnp.dot(grad_inner, fc1_weight.T, preferred_element_type=jnp.float32)
    grad_mixed_ln, ln2_gain_grad, ln2_bias_grad = norm2_back(grad_normed2)
    grad_mixed = grad_out + grad_mixed_ln
    grad_branch = grad_mixed.astype(jnp.bfloat16)
    out_bias_grad = column_sum(grad_branch)
    out_weight_grad = jnp.dot(att_low.T, grad_branch, preferred_element_type=jnp.float32)
    grad_attended = jnp.dot(grad_branch, out_weight.T, preferred_element_type=jnp.float32)
    grad_att_low = grad_attended.astype(jnp.bfloat16).reshape(clips_dev, seq_len, HEADS, HEAD)
    grad_probs = jnp.einsum(
        "cqhe,ckhe->chqk", grad_att_low, values_all, preferred_element_type=jnp.float32
    )
    grad_values = jnp.einsum(
        "chqk,cqhe->ckhe", soft_low, grad_att_low, preferred_element_type=jnp.float32
    )
    grad_scores = soft_back(grad_probs)[0].astype(jnp.bfloat16)
    grad_queries = (
        jnp.einsum("chqk,ckhe->cqhe", grad_scores, keys_all, preferred_element_type=jnp.float32)
        * head_scale
    )
    grad_keys = (
        jnp.einsum("chqk,cqhe->ckhe", grad_scores, queries, preferred_element_type=jnp.float32)
        * head_scale
    )
    grad_joined = jnp.concatenate(
        [
            grad_queries.reshape(token_rows, width),
            grad_keys.reshape(token_rows, width),
            grad_values.reshape(token_rows, width),
        ],
        axis=1,
    ).astype(jnp.bfloat16)
    qkv_weight_grad = jnp.dot(n1_low.T, grad_joined, preferred_element_type=jnp.float32)
    joined_sums = column_sum(grad_joined)
    qv_bias_grad = jnp.stack([joined_sums[:width], joined_sums[2 * width :]])
    grad_normed1 = jnp.dot(grad_joined, qkv_weight.T, preferred_element_type=jnp.float32)
    grad_tok_ln, ln1_gain_grad, ln1_bias_grad = norm1_back(grad_normed1)
    grad_tokens = (
        (grad_mixed + grad_tok_ln)
        .astype(jnp.bfloat16)
        .reshape(clips_dev, seq_len // MAPS, MAPS, width)
    )
    grad_pooled = lax.all_to_all(
        grad_tokens, "map", split_axis=1, concat_axis=0, tiled=True
    ).reshape(frame_rows, MAPS, width)
    grad_select = (
        jnp.einsum("nkd,npd->npk", grad_pooled, frame_patches, preferred_element_type=jnp.float32)
        * pool_scale
    )
    grad_from_pool = (
        jnp.einsum("npk,nkd->npd", sel_low, grad_pooled, preferred_element_type=jnp.float32)
        * pool_scale
    )
    grad_logit = select_back(grad_select.reshape(patch_rows, MAPS))[0].astype(jnp.bfloat16)
    map_b2_grad = column_sum(grad_logit)
    map_w2_grad = jnp.dot(act0_low.T, grad_logit, preferred_element_type=jnp.float32)
    grad_act0 = jnp.dot(grad_logit, map_w2.T, preferred_element_type=jnp.float32)
    grad_map_pre = gelu0_back(grad_act0)[0].astype(jnp.bfloat16)
    map_b1_grad = column_sum(grad_map_pre)
    map_w1_grad = jnp.dot(tl_low.T, grad_map_pre, preferred_element_type=jnp.float32)
    grad_tl_normed = jnp.dot(grad_map_pre, map_w1.T, preferred_element_type=jnp.float32)
    grad_in_ln, tl_gain_grad, tl_bias_grad = norm0_back(grad_tl_normed)
    patch_grad = (grad_in_ln + grad_from_pool.reshape(patch_rows, width)).astype(jnp.bfloat16)
    patch_grad = patch_grad.reshape(group, frames_dev, count, width)
    grads = (
        tl_gain_grad,
        tl_bias_grad,
        map_w1_grad,
        map_b1_grad,
        map_w2_grad,
        ln1_gain_grad,
        ln1_bias_grad,
        qkv_weight_grad,
        qv_bias_grad,
        out_weight_grad,
        out_bias_grad,
        ln2_gain_grad,
        ln2_bias_grad,
        fc1_weight_grad,
        fc1_bias_grad,
        fc2_weight_grad,
        fc2_bias_grad,
    )
    return (layer_rows, patch_grad, grads, map_b2_grad)


def add_tuples(first_tuple, second_tuple):
    return tuple(
        (first_item + second_item for first_item, second_item in zip(first_tuple, second_tuple))
    )


def on_device(
    patches,
    keep,
    tl_gain,
    tl_bias,
    map_w1,
    map_b1,
    map_w2,
    map_b2,
    ln1_gain,
    ln1_bias,
    qkv_weight,
    qv_bias,
    out_weight,
    out_bias,
    ln2_gain,
    ln2_bias,
    fc1_weight,
    fc1_bias,
    fc2_weight,
    fc2_bias,
    cotangent,
):
    shards = (
        tl_gain,
        tl_bias,
        map_w1,
        map_b1,
        map_w2,
        ln1_gain,
        ln1_bias,
        qkv_weight,
        qv_bias,
        out_weight,
        out_bias,
        ln2_gain,
        ln2_bias,
        fc1_weight,
        fc1_bias,
        fc2_weight,
        fc2_bias,
    )
    batches = patches.shape[0]
    layer_list = []
    patch_list = []
    reduced = None
    bias_total = None
    for batch_index in range(batches):
        full = gather_weights(shards)
        layer_rows, patch_grad, grads, bias_grad = run_batch(
            full, map_b2, patches[batch_index], keep[batch_index], cotangent[batch_index]
        )
        layer_list.append(layer_rows)
        patch_list.append(patch_grad)
        shard_part = reduce_grads(grads)
        reduced = shard_part if reduced is None else add_tuples(reduced, shard_part)
        bias_total = bias_grad if bias_total is None else bias_total + bias_grad
    final = (
        lax.psum(reduced[0].astype(jnp.bfloat16), "map").astype(jnp.float32),
        lax.psum(reduced[1].astype(jnp.bfloat16), "map").astype(jnp.float32),
        lax.psum(reduced[2].astype(jnp.bfloat16), "map").astype(jnp.float32),
        lax.psum(reduced[3].astype(jnp.bfloat16), "map").astype(jnp.float32),
        lax.psum(reduced[4].astype(jnp.bfloat16), "map").astype(jnp.float32),
        lax.psum(reduced[5].astype(jnp.bfloat16), "map").astype(jnp.float32),
        lax.psum(reduced[6].astype(jnp.bfloat16), "map").astype(jnp.float32),
        lax.psum(reduced[7].astype(jnp.bfloat16), "map").astype(jnp.float32),
        lax.psum(reduced[8].astype(jnp.bfloat16), "map").astype(jnp.float32),
        lax.psum(reduced[9].astype(jnp.bfloat16), "map").astype(jnp.float32),
        lax.psum(reduced[10].astype(jnp.bfloat16), "map").astype(jnp.float32),
        lax.psum(reduced[11].astype(jnp.bfloat16), "map").astype(jnp.float32),
        lax.psum(reduced[12].astype(jnp.bfloat16), "map").astype(jnp.float32),
        lax.psum(reduced[13].astype(jnp.bfloat16), "map").astype(jnp.float32),
        lax.psum(reduced[14].astype(jnp.bfloat16), "map").astype(jnp.float32),
        lax.psum(reduced[15].astype(jnp.bfloat16), "map").astype(jnp.float32),
        lax.psum(reduced[16].astype(jnp.bfloat16), "map").astype(jnp.float32),
    )
    bias_final = lax.psum(bias_total, ("clip", "map"))
    layer_out = jnp.stack(layer_list)
    patch_out = jnp.stack(patch_list)
    return (
        layer_out,
        patch_out,
        final[0],
        final[1],
        final[2],
        final[3],
        final[4],
        bias_final,
        final[5],
        final[6],
        final[7],
        final[8],
        final[9],
        final[10],
        final[11],
        final[12],
        final[13],
        final[14],
        final[15],
        final[16],
    )


def solution(mesh):
    in_specs = (
        P(None, "clip", "map", None, None),
        P(None, "clip", "map", None),
        P("clip"),
        P("clip"),
        P("clip", None),
        P("clip"),
        P("clip", None),
        P(),
        P("clip"),
        P("clip"),
        P("clip", None),
        P(None, "clip"),
        P("clip", None),
        P("clip"),
        P("clip"),
        P("clip"),
        P("clip", None),
        P("clip"),
        P("clip", None),
        P("clip"),
        P(None, ("clip", "map"), None, None),
    )
    out_specs = (
        P(None, ("clip", "map"), None, None),
        P(None, "clip", "map", None, None),
        P("clip"),
        P("clip"),
        P("clip", None),
        P("clip"),
        P("clip", None),
        P(),
        P("clip"),
        P("clip"),
        P("clip", None),
        P(None, "clip"),
        P("clip", None),
        P("clip"),
        P("clip"),
        P("clip"),
        P("clip", None),
        P("clip"),
        P("clip", None),
        P("clip"),
    )
    return jax.shard_map(
        on_device, mesh=mesh, in_specs=in_specs, out_specs=out_specs, check_vma=False
    )
```

profile of v0, /device:TPU:0, one launch (start us, length us, event | category | flops | bytes accessed | tf_op | source)
XLA Modules:
  0.0 1275.5 jit_solution(16430404640105778007)
XLA Ops:
  23.7 63.7 %all-reduce.33 = (bf16[768]{0:T(1024)(128)(2,1)S(1)}, bf16[768]{0:T(1024)(128)(2,1)S(1)}, bf16[64]{0:T(256)(128)(2,1)S(1)}, bf16[768]{0:T(1024)(128)(2,1)S(1)}, ...) all-reduce(bf16[768]{0:T(1024)(128)(2,1)S(1)} %dynamic-update-slice, ...), channel_id=1, replica_groups=mesh['clip'=16,'map'=2] {'clip'}, use_global_device_ids=true, to_apply=%add.1 | all-reduce | flops 8512 | bytes 34048
  101.3 20.4 %fusion.128 = (bf16[1,2,16,196,768]{4,2,3,1,0:T(8,128)(2,1)}, f32[1,2,16,196,768]{4,2,3,1,0:T(8,128)}, f32[1,2,16,196,768]{4,2,3,1,0:T(8,128)S(1)}, bf16[1,2,16,196,768]{4,2,3,1,0:T(8,128)(2,1)}) fusion(bf16[2,2,16,196,768]{4,2,3,1,0:T(8,128)(2,1)} %param.21), kind=kLoop, calls=%fused_computation.313 | loop fusion | flops 9633792 | bytes 77070336 | tf_op jit(solution)/shard_map/slice | solution.py:356
  135.2 19.2 %reshape.700 = f32[6272,768]{1,0:T(8,128)} reshape(f32[1,2,16,196,768]{4,3,2,1,0:T(8,128)} %copy.141) | data formatting | bytes 38535168 | tf_op jit(solution)/shard_map/convert_element_type | solution.py:153
  154.4 20.3 %copy.152 = f32[1,2,16,196,768]{4,3,2,1,0:T(8,128)} copy(f32[1,2,16,196,768]{4,2,3,1,0:T(8,128)} %get-tuple-element.182) | data formatting | bytes 38535168 | tf_op jit(solution)/shard_map/convert_element_type | solution.py:153
  174.8 19.2 %reshape.704 = f32[6272,768]{1,0:T(8,128)} reshape(f32[1,2,16,196,768]{4,3,2,1,0:T(8,128)} %copy.152) | data formatting | bytes 38535168 | tf_op jit(solution)/shard_map/convert_element_type | solution.py:153
  211.3 19.8 %all_gather.70 = bf16[768,64]{1,0:T(8,128)(2,1)S(1)} all-gather(bf16[48,64]{1,0:T(8,128)(2,1)S(1)} %copy-done.144), channel_id=1, replica_groups=mesh['clip'=16,'map'=2] {'clip'}, dimensions={0}, use_global_device_ids=true | all-gather | bytes 104448 | tf_op jit(solution)/shard_map/all_gather | solution.py:42
  231.2 18.2 %add_convert_fusion.3 = (bf16[6272,768]{1,0:T(8,128)(2,1)}, bf16[6272,768]{1,0:T(8,128)(2,1)S(1)}) fusion(f32[6272,768]{1,0:T(8,128)} %reshape.700, f32[768]{0:T(1024)S(1)} %convert_element_type.580, f32[768]{0:T(1024)S(1)} %convert_element_type.579, f32[6272]{0:T(1024)S(1)} %rsqrt.60, f32[6272]{0:T(1024)S(1)} %div.183, f32[6272]{0:T(1024)S(1)} %rsqrt.63, ...), kind=kLoop, calls=%fused_computation.11 | loop fusion | flops 48168960 | bytes 57909248 | tf_op jit(solution)/shard_map/convert_element_type | solution.py:155
  478.2 53.0 %reduce-scatter.39.cloned.1.call-done = bf16[48,2]{1,0:T(8,128)(2,1)} async-done(((bf16[768,2]{1,0:T(8,128)(2,1)}), bf16[48,2]{1,0:T(8,128)(2,1)}) %reduce-scatter.39.cloned.1.call-update) | async-done | bytes 208
  570.8 19.4 %reshape.691 = f32[6272,768]{1,0:T(8,128)} reshape(f32[32,196,768]{2,1,0:T(8,128)} %broadcast_multiply_fusion.1) | data formatting | bytes 38535168 | tf_op jit(solution)/shard_map/reshape | solution.py:276
  594.1 33.3 %multiply_reduce_fusion.1 = (bf16[768]{0:T(1024)(128)(2,1)S(1)}, f32[6272]{0:T(1024)}, bf16[768]{0:T(1024)(128)(2,1)S(1)}, bf16[768]{0:T(1024)(128)(2,1)}, f32[6...) fusion(f32[6272,768]{1,0:T(8,128)} %reshape.700, f32[6272]{0:T(1024)S(1)} %copy-done.77, ...), kind=kOutput, calls=%fused_computation.4 | convolution fusion | flops 693617408 | bytes 78131200 | tf_op jit(solution)/shard_map/dot_general | solution.py:274
  630.2 35.9 %fusion.118 = (f32[6272]{0:T(1024)}, f32[6272,768]{1,0:T(8,128)}, f32[6272]{0:T(1024)S(1)}, f32[6272,768]{1,0:T(8,128)}) fusion(f32[6272]{0:T(1024)} %multiply_multiply_fusion.9, f32[6272,768]{1,0:T(8,128)S(1)} %bitcast.241, f32[6272]{0:T(1024)S(1)} %copy-done.81, f32[6272]{0:T(1024)S(1)} %copy-done.77, f32[6272,768]{1,0:T(8,128)} %get-tuple-element.245, ...), kind=kLoop, calls=%fused_computation.305 | loop fusion | flops 67424000 | bytes 115809280 | tf_op jit(solution)/shard_map/transpose(jvp())/reduce_sum | solution.py:16
  666.9 17.7 %add_convert_fusion.1 = bf16[6272,768]{1,0:T(8,128)(2,1)} fusion(f32[6272,768]{1,0:T(8,128)} %reshape.691, f32[6272,768]{1,0:T(8,128)} %get-tuple-element.162, f32[6272]{0:T(1024)S(1)} %negate_multiply_fusion.1), kind=kLoop, calls=%fused_computation.7 | loop fusion | flops 14450688 | bytes 48194048 | tf_op jit(solution)/shard_map/convert_element_type | solution.py:276
  705.9 19.2 %reshape.699 = f32[6272,768]{1,0:T(8,128)} reshape(f32[32,196,768]{2,1,0:T(8,128)} %broadcast_multiply_fusion) | data formatting | bytes 38535168 | tf_op jit(solution)/shard_map/reshape | solution.py:276
  725.1 17.8 %add_convert_fusion = bf16[6272,768]{1,0:T(8,128)(2,1)} fusion(f32[6272,768]{1,0:T(8,128)} %reshape.699, f32[6272,768]{1,0:T(8,128)} %get-tuple-element.208, f32[6272]{0:T(1024)S(1)} %negate_multiply_fusion), kind=kLoop, calls=%fused_computation.5 | loop fusion | flops 14450688 | bytes 48194048 | tf_op jit(solution)/shard_map/convert_element_type | solution.py:276
  757.9 59.5 %all-reduce.32 = (bf16[768]{0:T(1024)(128)(2,1)S(1)}, bf16[768]{0:T(1024)(128)(2,1)S(1)}, bf16[768]{0:T(1024)(128)(2,1)S(1)}, bf16[768]{0:T(1024)(128)(2,1)S(1)}...) all-reduce(bf16[768]{0:T(1024)(128)(2,1)S(1)} %copy-done.163, ...), channel_id=1, replica_groups=mesh['clip'=16,'map'=2] {'clip'}, use_global_device_ids=true, to_apply=%add.9 | all-reduce | flops 20352 | bytes 81408
  832.9 17.7 %pad_maximum_fusion = bf16[2,2,16,196,768]{4,3,2,1,0:T(8,128)(2,1)} fusion(bf16[1,2,16,196,768]{4,3,2,1,0:T(8,128)(2,1)} %stack_reshape.15, bf16[1,2,16,196,768]{4,3,2,1,0:T(8,128)(2,1)} %stack_reshape.14), kind=kLoop, calls=%fused_computation.2 | loop fusion | flops 9633792 | bytes 38535168 | tf_op jit(solution)/shard_map/stack | solution.py:384
  850.6 37.4 %psum.131 = f32[8]{0:T(128)} all-reduce(f32[8]{0:T(128)S(1)} %add.482), channel_id=1, replica_groups=mesh['clip'=16,'map'=2] {'clip','map'}, use_global_device_ids=true, to_apply=%region_57.0 | all-reduce | flops 8 | bytes 64 | tf_op jit(solution)/shard_map/psum | solution.py:382
  888.1 25.0 %copy.176 = bf16[2,2,16,196,768]{4,2,3,1,0:T(8,128)(2,1)} copy(bf16[2,2,16,196,768]{4,3,2,1,0:T(8,128)(2,1)} %pad_maximum_fusion) | data formatting | bytes 38535168
  922.4 30.4 %reduce-scatter.31.cloned.1.call-done = bf16[48,3072]{1,0:T(8,128)(2,1)} async-done(((bf16[768,3072]{1,0:T(8,128)(2,1)}), bf16[48,3072]{1,0:T(8,128)(2,1)}) %reduce-scatter.31.cloned.1.call-update) | async-done | bytes 294928 | tf_op jit(solution)/shard_map/reduce_scatter | solution.py:101
  954.7 76.6 %reduce-scatter.33.cloned.1.call-done = bf16[192,768]{1,0:T(8,128)(2,1)} async-done(((bf16[3072,768]{1,0:T(8,128)(2,1)}), bf16[192,768]{1,0:T(8,128)(2,1)}) %reduce-scatter.33.cloned.1.call-update) | async-done | bytes 294928 | tf_op jit(solution)/shard_map/reduce_scatter | solution.py:107
  1031.3 78.9 %reduce-scatter.35.cloned.1.call-done = bf16[192,768]{1,0:T(8,128)(2,1)} async-done(((bf16[3072,768]{1,0:T(8,128)(2,1)}), bf16[192,768]{1,0:T(8,128)(2,1)}) %reduce-scatter.35.cloned.1.call-update) | async-done | bytes 294928 | tf_op jit(solution)/shard_map/reduce_scatter | solution.py:107
  1118.3 47.9 %reduce-scatter.17.cloned.1.call-done = bf16[48,64]{1,0:T(8,128)(2,1)} async-done(((bf16[768,64]{1,0:T(8,128)(2,1)}), bf16[48,64]{1,0:T(8,128)(2,1)}) %reduce-scatter.17.cloned.1.call-update) | async-done | bytes 6160 | tf_op jit(solution)/shard_map/reduce_scatter | solution.py:68
  1166.2 56.0 %reduce-scatter.19.cloned.1.call-done = bf16[48,64]{1,0:T(8,128)(2,1)} async-done(((bf16[768,64]{1,0:T(8,128)(2,1)}), bf16[48,64]{1,0:T(8,128)(2,1)}) %reduce-scatter.19.cloned.1.call-update) | async-done | bytes 6160 | tf_op jit(solution)/shard_map/reduce_scatter | solution.py:68
  1238.2 23.6 %all-reduce.38.cloned.1.call-done = (bf16[48,2304]{1,0:T(8,128)(2,1)}, bf16[48,768]{1,0:T(8,128)(2,1)}, bf16[48,3072]{1,0:T(8,128)(2,1)}, bf16[192,768]{1,0:T(8,128)(2,1)}) async-done(((bf16[48,2304]{1,0:T(8,128)(2,1)}, bf16[48,768]{1,0:T(8,128)(2,1)}, bf16[48,3072]{1,0:T(8,128)(2,1)}, bf16[192,768]{1,0:T(8,128)(2,1)}), (bf16[48,2304]{1,0:T(8,128)(2,1)}, bf16[48,768]{1,0:T(8,128)(2,1)}, ...) | async-done | bytes 884752 | tf_op jit(solution)/shard_map/psum | solution.py:371
  (702 shorter events, 424.4 us)
Async XLA Ops:
  7.2 328.8 %all-gather.7.cloned.1.call-start = ((), (), s32[]{:S(2)}) async-start(), calls=%async_computation.16 | async-start | bytes 3760128 | tf_op jit(solution)/shard_map/all_gather | solution.py:47
  7.9 348.6 %all-gather.9.cloned.1.call-start = ((), (), s32[]{:S(2)}) async-start(), calls=%async_computation.17 | async-start | bytes 1253376 | tf_op jit(solution)/shard_map/all_gather | solution.py:49
  8.7 359.5 %all-gather.11.cloned.1.call-start = ((), (), s32[]{:S(2)}) async-start(), calls=%async_computation.18 | async-start | bytes 5013504 | tf_op jit(solution)/shard_map/all_gather | solution.py:53
  18.6 212.6 %copy-start.80 = (f32[6272]{0:T(1024)}, f32[6272]{0:T(1024)S(1)}, u32[]{:S(2)}) copy-start(f32[6272]{0:T(1024)S(1)} %div.183) | copy-start | bytes 75268
  19.0 212.2 %copy-start.82 = (f32[6272]{0:T(1024)}, f32[6272]{0:T(1024)S(1)}, u32[]{:S(2)}) copy-start(f32[6272]{0:T(1024)S(1)} %div.194) | copy-start | bytes 75268
  272.9 50.5 %all-to-all-start.1 = ((bf16[2,16,8,768]{3,2,1,0:T(8,128)(2,1)}), bf16[2,16,8,768]{3,2,1,0:T(8,128)(2,1)S(1)}, u32[]{:S(2)}, u32[]{:S(2)}) async-start(bf16[2,16,8,768]{3,2,1,0:T(8,128)(2,1)} %bitcast.19), calls=%async_computation.1 | async-start | bytes 786432 | tf_op jit(solution)/shard_map/all_to_all | solution.py:171
  276.4 101.3 %all-gather.13.cloned.1.call-start = ((), (), s32[]{:S(2)}) async-start(), calls=%async_computation.19 | async-start | bytes 5013504 | tf_op jit(solution)/shard_map/all_gather | solution.py:55
  323.4 11.0 all-to-all-start
  326.9 150.5 %reduce-scatter.37.cloned.1.call-start = ((), (), s32[]{:S(2)}) async-start(), calls=%async_computation.30 | async-start | bytes 208896
  423.3 107.9 %reduce-scatter.39.cloned.1.call-start = ((), (), s32[]{:S(2)}) async-start(), calls=%async_computation.31 | async-start | bytes 208896
  425.8 493.2 %reduce-scatter.25.cloned.1.call-start = ((), (), s32[]{:S(2)}) async-start(), calls=%async_computation.24 | async-start | bytes 1253376 | tf_op jit(solution)/shard_map/reduce_scatter | solution.py:89
  427.4 491.6 %reduce-scatter.27.cloned.1.call-start = ((), (), s32[]{:S(2)}) async-start(), calls=%async_computation.25 | async-start | bytes 1253376 | tf_op jit(solution)/shard_map/reduce_scatter | solution.py:89
  429.0 491.7 %reduce-scatter.21.cloned.1.call-start = ((), (), s32[]{:S(2)}) async-start(), calls=%async_computation.22 | async-start | bytes 3760128 | tf_op jit(solution)/shard_map/reduce_scatter | solution.py:83
  432.0 488.6 %reduce-scatter.23.cloned.1.call-start = ((), (), s32[]{:S(2)}) async-start(), calls=%async_computation.23 | async-start | bytes 3760128 | tf_op jit(solution)/shard_map/reduce_scatter | solution.py:83
  436.2 486.2 %reduce-scatter.29.cloned.1.call-start = ((), (), s32[]{:S(2)}) async-start(), calls=%async_computation.26 | async-start | bytes 5013504 | tf_op jit(solution)/shard_map/reduce_scatter | solution.py:101
  442.4 510.4 %reduce-scatter.31.cloned.1.call-start = ((), (), s32[]{:S(2)}) async-start(), calls=%async_computation.27 | async-start | bytes 5013504 | tf_op jit(solution)/shard_map/reduce_scatter | solution.py:101
  448.7 582.6 %reduce-scatter.33.cloned.1.call-start = ((), (), s32[]{:S(2)}) async-start(), calls=%async_computation.28 | async-start | bytes 5013504 | tf_op jit(solution)/shard_map/reduce_scatter | solution.py:107
  467.6 64.9 %all-to-all-start.2 = ((bf16[1,32,8,768]{3,2,0,1:T(8,128)(2,1)}), bf16[1,32,8,768]{3,2,0,1:T(8,128)(2,1)S(1)}, u32[]{:S(2)}, u32[]{:S(2)}) async-start(bf16[1,32,8,768]{3,2,0,1:T(8,128)(2,1)} %get-tuple-element.193), calls=%async_computation.2 | async-start | bytes 786432 | tf_op jit(solution)/shard_map/all_to_all | solution.py:256
  471.0 639.2 %reduce-scatter.35.cloned.1.call-start = ((), (), s32[]{:S(2)}) async-start(), calls=%async_computation.29 | async-start | bytes 5013504 | tf_op jit(solution)/shard_map/reduce_scatter | solution.py:107
  532.5 10.7 all-to-all-start.3
  536.0 630.3 %reduce-scatter.17.cloned.1.call-start = ((), (), s32[]{:S(2)}) async-start(), calls=%async_computation.20 | async-start | bytes 208896 | tf_op jit(solution)/shard_map/reduce_scatter | solution.py:68
  832.9 389.4 %reduce-scatter.19.cloned.1.call-start = ((), (), s32[]{:S(2)}) async-start(), calls=%async_computation.21 | async-start | bytes 208896 | tf_op jit(solution)/shard_map/reduce_scatter | solution.py:68
  913.1 348.6 %all-reduce.38.cloned.1.call-start = ((), (), s32[]{:S(2)}) async-start(), calls=%async_computation.32 | async-start | bytes 1769472 | tf_op jit(solution)/shard_map/psum | solution.py:371
  918.9 193.1 %copy-start.12 = (f32[256,768]{1,0:T(8,128)S(1)}, f32[256,768]{1,0:T(8,128)}, u32[]{:S(2)}) copy-start(f32[256,768]{1,0:T(8,128)} %copy-done.8) | copy-start | bytes 2359300
  (203 other events, 2305.3 us)
Sparse Core Ops, SparseCore 0:
  10.3 49.9 all-gather.6
  62.6 37.3 all-gather.8
  102.3 52.3 all-gather.10
  279.2 51.1 all-gather.12
  423.4 51.1 reduce-scatter.36
  478.5 52.6 reduce-scatter.38
  534.8 57.1 reduce-scatter.24
  595.7 57.0 reduce-scatter.26
  656.7 67.0 reduce-scatter.20
  727.5 67.4 reduce-scatter.22
  798.9 75.0 reduce-scatter.28
  878.2 74.6 reduce-scatter.30
  956.7 74.5 reduce-scatter.32
  1035.5 74.6 reduce-scatter.34
  1113.6 52.6 reduce-scatter.16
  1169.6 52.5 reduce-scatter.18
  1225.7 36.0 all-reduce.37
where the time goes:
time: 1280 us
  waiting for transfers between devices  376 us (29%)
  blocking collectives  223 us (17%)
  matrix products  220 us (17%)
  local copies, waits for them, and re-layouts  218 us (17%)
  other arithmetic  202 us (16%)
  between operations  20.7 us (2%)
  starting transfers between devices  16 us (1%)
    reduce_scatter x2, waiting for transfers between devices, reduce_grads(): lax.psum_scatter(grads[15].astype(jnp.bfloat16), 'clip', scatter_dimensio...  156 us
    unnamed x2, blocking collectives  123 us
    reduce_scatter x2, waiting for transfers between devices, reduce_grads(): lax.psum_scatter(grads[2].astype(jnp.bfloat16), 'clip', scatter_dimension...  104 us
    convert_element_type x4, local copies, waits for them, and re-layouts, run_batch(): flat_patches.astype(jnp.float32)  72.3 us
    unnamed x19, waiting for transfers between devices  55.4 us
    unnamed x439, local copies, waits for them, and re-layouts  45.6 us
    dot_general x2, matrix products, run_batch(): jnp.dot(grad_map_pre, map_w1.T, preferred_element_type=jnp.float32)  42.6 us
    reshape x2, local copies, waits for them, and re-layouts, run_batch(): grad_from_pool.reshape(patch_rows, width)  38.6 us
  transfers between devices with their start and end apart: 21, of which 8 were waited for; matrix products, arithmetic and copies ran while one was open for 45% of the time, Pallas kernels for 0%

commit v1 on v0

v1 whole, which is shorter than its diff:
```python
import functools

import jax
import jax.numpy as jnp
from jax import lax
from jax.experimental import pallas as pl
from jax.experimental.pallas import tpu as pltpu
from jax.sharding import PartitionSpec as P

HEAD = 64
MAPS = 8
LANES = 128
EPS = 1e-06
GC = 0.7978845608028654
GA = 0.044715
BF = jnp.bfloat16
F32 = jnp.float32
VLIM = 61 * 1024 * 1024


def dot(a, b):
    return lax.dot_general(a, b, (((1,), (0,)), ((), ())), preferred_element_type=F32)


def dot_nt(a, b):
    return lax.dot_general(a, b, (((1,), (1,)), ((), ())), preferred_element_type=F32)


def dot_tn(a, b):
    return lax.dot_general(a, b, (((0,), (0,)), ((), ())), preferred_element_type=F32)


def gelu_parts(x):
    x2 = x * x
    t = jnp.tanh(GC * x * (1.0 + GA * x2))
    act = 0.5 * x * (1.0 + t)
    slope = 0.5 * (1.0 + t) + 0.5 * x * (1.0 - t * t) * (GC * (1.0 + 3.0 * GA * x2))
    return act, slope


def col(x, n):
    return pl.ds(pl.multiple_of(x, n), n)


def patch_fwd_kernel(
    blocks, per, rb, width, v_ref, w1_ref, w1s_ref, w2_ref, b2_ref, kx_ref, pool_ref, aux_ref, sel_ref, der_ref,
    vbuf, acc, rmat, delta, vsem,
):
    frames = rb // (kx_ref.shape[1] - 4)

    @pl.loop(0, blocks)
    def _(i):
        pltpu.make_async_copy(v_ref.at[pl.ds(i * rb, rb)], vbuf.at[pl.ds(i * rb, rb)], vsem.at[i]).start()

    r2 = lax.broadcasted_iota(jnp.int32, rmat.shape, 0)
    c2 = lax.broadcasted_iota(jnp.int32, rmat.shape, 1)
    rmat[...] = jnp.where(r2 // frames == c2, 1.0, 0.0).astype(BF)
    r1 = lax.broadcasted_iota(jnp.int32, delta.shape, 0)
    c1 = lax.broadcasted_iota(jnp.int32, delta.shape, 1)
    delta[...] = jnp.where(r1 % frames == c1 // MAPS, 1.0, 0.0)

    @pl.loop(0, blocks)
    def _(i):
        rows = pl.ds(pl.multiple_of(i * rb, 16), rb)
        pltpu.make_async_copy(v_ref.at[pl.ds(i * rb, rb)], vbuf.at[pl.ds(i * rb, rb)], vsem.at[i]).wait()
        v = vbuf[rows, :]
        mm = dot(v, w1_ref[...])
        mean = mm[:, 64:65] * (1.0 / width)
        sq = jnp.zeros((rb, LANES), F32)
        for k in range(width // LANES):
            c = v[:, k * LANES : (k + 1) * LANES].astype(F32) - mean
            sq = sq + c * c
        rstd = lax.rsqrt(jnp.sum(sq, axis=-1, keepdims=True) * (1.0 / width) + EPS)
        pre = rstd * (mm - mean * w1s_ref[0:1, :]) + w1s_ref[1:2, :]
        act, _ = gelu_parts(pre)
        logit = dot(act.astype(BF)[:, :64], w2_ref[...]) + b2_ref[...]
        sig = 1.0 / (1.0 + jnp.exp(-logit))
        mask = dot(rmat[...], kx_ref[i]) * delta[...]
        sm = sig * mask
        sel = sm.astype(BF)
        sel_ref[rows, :] = sel
        der_ref[rows, :] = (sm * (1.0 - sig)).astype(BF)
        lane = lax.broadcasted_iota(jnp.int32, (rb, LANES), 1)
        aux_ref[rows, :] = jnp.where(lane < 64, pre, jnp.where(lane < 96, mean, rstd))
        part = dot_tn(sel, v)

        @pl.when(i % per == 0)
        def _():
            acc[...] = part

        @pl.when(i % per != 0)
        def _():
            acc[...] += part

        @pl.when(i % per == per - 1)
        def _():
            pool_ref[i // per] = (acc[...] * ((rb // frames * per) ** -0.5)).astype(BF)


def patch_forward(v, w1aug, w1s, w2rep, b2rep, kx, groups, per):
    rows, width = v.shape
    blocks = kx.shape[0]
    rb = rows // blocks
    vm = pl.BlockSpec(memory_space=pltpu.VMEM)
    return pl.pallas_call(
        functools.partial(patch_fwd_kernel, blocks, per, rb, width),
        out_shape=(
            jax.ShapeDtypeStruct((groups, LANES, width), BF),
            jax.ShapeDtypeStruct((rows, LANES), F32),
            jax.ShapeDtypeStruct((rows, LANES), BF),
            jax.ShapeDtypeStruct((rows, LANES), BF),
        ),
        in_specs=[pl.BlockSpec(memory_space=pltpu.HBM)] + [vm] * 5,
        out_specs=(vm,) * 4,
        scratch_shapes=[
            pltpu.VMEM((rows, width), BF),
            pltpu.VMEM((LANES, width), F32),
            pltpu.VMEM((rb, kx.shape[1]), BF),
            pltpu.VMEM((rb, LANES), F32),
            pltpu.SemaphoreType.DMA((blocks,)),
        ],
        compiler_params=pltpu.CompilerParams(vmem_limit_bytes=VLIM),
    )(v, w1aug, w1s, w2rep, b2rep, kx)


def ln_stats(t):
    mean = jnp.mean(t, axis=-1, keepdims=True)
    c = t - mean
    rstd = lax.rsqrt(jnp.mean(c * c, axis=-1, keepdims=True) + EPS)
    return c * rstd, rstd


def token_kernel(
    tok, cot, wq, wo, w1, w2, vec, b1,
    out_ref, gq_ref, go_ref, g1_ref, g2_ref, gtok_ref, gvec_ref, gb1_ref,
    n1, joined, probs, att, mixed, n2, act, slope, gacc, gmix, gbr, gatt, gj, tr,
):
    n, d = tok.shape
    ff = w1.shape[1]
    seq = 256
    micros = n // seq
    pairs = d // LANES
    ch = 64
    cb = 256
    chunks = n // ch
    lane = lax.broadcasted_iota(jnp.int32, (1, LANES), 1)
    first = lane < HEAD

    def rows_of(i):
        return pl.ds(pl.multiple_of(i * ch, ch), ch)

    def transpose_into(src):
        @pl.loop(0, n // 128)
        def _(i):
            r = pl.ds(pl.multiple_of(i * 128, 128), 128)
            tr[:, r] = src[r, :].astype(F32).T.astype(BF)

    gvec_ref[...] = jnp.zeros(gvec_ref.shape, F32)

    def add_row(i, val):
        gvec_ref[i : i + 1, :] += jnp.sum(val, axis=0, keepdims=True)

    @pl.loop(0, chunks)
    def _(i):
        xh, _ = ln_stats(tok[rows_of(i), :].astype(F32))
        n1[rows_of(i), :] = (xh * vec[0:1, :] + vec[1:2, :]).astype(BF)

    for blk in range(3):
        @pl.loop(0, d // cb)
        def _(j):
            o = pl.multiple_of(blk * d + j * cb, cb)
            r = dot(n1[...], wq[:, pl.ds(o, cb)])
            if blk == 0:
                r = r + vec[2:3, col(j * cb, cb)]
            if blk == 2:
                r = r + vec[3:4, col(j * cb, cb)]
            joined[:, pl.ds(o, cb)] = r.astype(BF)

    def heads_of(ref, i, base):
        m, pr = i // pairs, i % pairs
        r = pl.ds(pl.multiple_of(m * seq, seq), seq)
        return ref[r, pl.ds(pl.multiple_of(base + pr * LANES, LANES), LANES)]

    def put_heads(ref, i, base, val):
        m, pr = i // pairs, i % pairs
        r = pl.ds(pl.multiple_of(m * seq, seq), seq)
        ref[r, pl.ds(pl.multiple_of(base + pr * LANES, LANES), LANES)] = val

    zero = jnp.zeros((seq, LANES), BF)

    @pl.loop(0, micros * pairs)
    def _(i):
        q = (heads_of(joined, i, 0).astype(F32) * (HEAD**-0.5)).astype(BF)
        k = heads_of(joined, i, d)
        v = heads_of(joined, i, 2 * d)
        total = jnp.zeros((seq, LANES), F32)
        for e in range(2):
            mine = first if e == 0 else jnp.logical_not(first)
            s = dot_nt(jnp.where(mine, q, zero), k)
            ex = jnp.exp(s - jnp.max(s, axis=-1, keepdims=True))
            p = ex / jnp.sum(ex, axis=-1, keepdims=True)
            probs[i * 2 + e] = p
            total = total + dot(p.astype(BF), jnp.where(mine, v, zero))
        put_heads(att, i, 0, total.astype(BF))

    @pl.loop(0, d // cb)
    def _(j):
        c = col(j * cb, cb)
        mixed[:, c] = tok[:, c].astype(F32) + (dot(att[...], wo[:, c]) + vec[4:5, c])

    @pl.loop(0, chunks)
    def _(i):
        xh, _ = ln_stats(mixed[rows_of(i), :])
        n2[rows_of(i), :] = (xh * vec[5:6, :] + vec[6:7, :]).astype(BF)

    @pl.loop(0, ff // cb)
    def _(j):
        c = col(j * cb, cb)
        a, s = gelu_parts(dot(n2[...], w1[:, c]) + b1[0:1, c])
        act[:, c] = a.astype(BF)
        slope[:, c] = s.astype(BF)

    @pl.loop(0, ff // cb)
    def _(j):
        c = col(j * cb, cb)
        g2_ref[c, :] = dot_tn(act[:, c], cot[...]).astype(BF)

    @pl.loop(0, d // cb)
    def _(j):
        c = col(j * cb, cb)
        out_ref[:, c] = (mixed[:, c] + (dot(act[...], w2[:, c]) + vec[7:8, c])).astype(BF)

    transpose_into(n2)

    @pl.loop(0, ff // cb)
    def _(j):
        c = col(j * cb, cb)
        g = (dot_nt(cot[...], w2[c, :]) * slope[:, c].astype(F32)).astype(BF)
        act[:, c] = g
        gb1_ref[0:1, c] = jnp.sum(g.astype(F32), axis=0, keepdims=True)
        g1_ref[:, c] = dot(tr[...], g).astype(BF)

    @pl.loop(0, d // cb)
    def _(j):
        c = col(j * cb, cb)
        gacc[:, c] = dot_nt(act[...], w1[c, :])

    @pl.loop(0, chunks)
    def _(i):
        r = rows_of(i)
        xh, rstd = ln_stats(mixed[r, :])
        e = gacc[r, :]
        add_row(5, e * xh)
        add_row(6, e)
        eg = e * vec[5:6, :]
        back = eg - jnp.mean(eg, axis=-1, keepdims=True) - xh * jnp.mean(eg * xh, axis=-1, keepdims=True)
        c = cot[r, :].astype(F32)
        g = c + back * rstd
        gmix[r, :] = g
        low = g.astype(BF)
        gbr[r, :] = low
        add_row(4, low.astype(F32))
        add_row(7, c)

    transpose_into(att)

    @pl.loop(0, d // cb)
    def _(j):
        c = col(j * cb, cb)
        go_ref[:, c] = dot(tr[...], gbr[:, c]).astype(BF)
        gatt[:, c] = dot_nt(gbr[...], wo[c, :]).astype(BF)

    @pl.loop(0, micros * pairs)
    def _(i):
        q = (heads_of(joined, i, 0).astype(F32) * (HEAD**-0.5)).astype(BF)
        k = heads_of(joined, i, d)
        v = heads_of(joined, i, 2 * d)
        ga = heads_of(gatt, i, 0)
        gq = jnp.zeros((seq, LANES), F32)
        gk = jnp.zeros((seq, LANES), F32)
        gv = jnp.zeros((seq, LANES), F32)
        for e in range(2):
            mine = first if e == 0 else jnp.logical_not(first)
            p = probs[i * 2 + e]
            ga_e = jnp.where(mine, ga, zero)
            gp = dot_nt(ga_e, v)
            pg = p * gp
            gs = (pg - p * jnp.sum(pg, axis=-1, keepdims=True)).astype(BF)
            gv = gv + dot_tn(p.astype(BF), ga_e)
            gq = gq + dot(gs, jnp.where(mine, k, zero))
            gk = gk + dot_tn(gs, jnp.where(mine, q, zero))
        put_heads(gj, i, 0, (gq * (HEAD**-0.5)).astype(BF))
        put_heads(gj, i, d, gk.astype(BF))
        put_heads(gj, i, 2 * d, gv.astype(BF))

    transpose_into(n1)

    @pl.loop(0, 3 * d // cb)
    def _(j):
        c = col(j * cb, cb)
        gq_ref[:, c] = dot(tr[...], gj[:, c]).astype(BF)

    @pl.loop(0, d // cb)
    def _(j):
        c = col(j * cb, cb)
        gacc[:, c] = dot_nt(gj[...], wq[c, :])

    @pl.loop(0, chunks)
    def _(i):
        r = rows_of(i)
        xh, rstd = ln_stats(tok[r, :].astype(F32))
        e = gacc[r, :]
        add_row(0, e * xh)
        add_row(1, e)
        add_row(2, gj[r, 0:d].astype(F32))
        add_row(3, gj[r, 2 * d : 3 * d].astype(F32))
        eg = e * vec[0:1, :]
        back = eg - jnp.mean(eg, axis=-1, keepdims=True) - xh * jnp.mean(eg * xh, axis=-1, keepdims=True)
        gtok_ref[r, :] = (gmix[r, :] + back * rstd).astype(BF)


def token_layer(tok, cot, wq, wo, w1, w2, vec, b1):
    n, d = tok.shape
    ff = w1.shape[1]
    vm = pl.BlockSpec(memory_space=pltpu.VMEM)
    sds = jax.ShapeDtypeStruct
    heads = (n // 256) * (d // HEAD)
    return pl.pallas_call(
        token_kernel,
        out_shape=(
            sds((n, d), BF), sds((d, 3 * d), BF), sds((d, d), BF), sds((d, ff), BF), sds((ff, d), BF), sds((n, d), BF),
            sds((8, d), F32), sds((1, ff), F32),
        ),
        in_specs=[vm] * 8,
        out_specs=(vm,) * 8,
        scratch_shapes=[
            pltpu.VMEM((n, d), BF),
            pltpu.VMEM((n, 3 * d), BF),
            pltpu.VMEM((heads, 256, 256), F32),
            pltpu.VMEM((n, d), BF),
            pltpu.VMEM((n, d), F32),
            pltpu.VMEM((n, d), BF),
            pltpu.VMEM((n, ff), BF),
            pltpu.VMEM((n, ff), BF),
            pltpu.VMEM((n, d), F32),
            pltpu.VMEM((n, d), F32),
            pltpu.VMEM((n, d), BF),
            pltpu.VMEM((n, d), BF),
            pltpu.VMEM((n, 3 * d), BF),
            pltpu.VMEM((d, n), BF),
        ],
        compiler_params=pltpu.CompilerParams(vmem_limit_bytes=VLIM),
    )(tok, cot, wq, wo, w1, w2, vec, b1)


def patch_bwd_kernel(
    blocks, per, rb, width, v_ref, aux_hbm, sel_ref, der_hbm, gt_ref, w1s_ref, w2_ref,
    co_hbm, x_ref, w2g_ref, row_ref,
    vbuf, aux_ref, der_ref, co_ref, vsem, asem, dsem, csem,
):
    def copies(i):
        r = pl.ds(i * rb, rb)
        return (
            pltpu.make_async_copy(v_ref.at[r], vbuf.at[r], vsem.at[i]),
            pltpu.make_async_copy(aux_hbm.at[r], aux_ref.at[r], asem.at[i]),
            pltpu.make_async_copy(der_hbm.at[r], der_ref.at[r], dsem.at[i]),
        )

    def put(i):
        r = pl.ds(i * rb, rb)
        return pltpu.make_async_copy(co_ref.at[r], co_hbm.at[r], csem.at[i])

    @pl.loop(0, blocks)
    def _(i):
        for c in copies(i):
            c.start()

    x_ref[...] = jnp.zeros(x_ref.shape, F32)
    w2g_ref[...] = jnp.zeros(w2g_ref.shape, F32)
    row_ref[...] = jnp.zeros(row_ref.shape, F32)
    lane = lax.broadcasted_iota(jnp.int32, (rb, LANES), 1)

    @pl.loop(0, blocks)
    def _(i):
        rows = pl.ds(pl.multiple_of(i * rb, 16), rb)
        for c in copies(i):
            c.wait()
        v = vbuf[rows, :]
        aux = aux_ref[rows, :]
        mean = aux[:, 64:65]
        rstd = aux[:, 127:128]
        g = dot_nt(v, gt_ref[i // per])
        gl_f = g * der_ref[rows, :].astype(F32)
        gl = gl_f.astype(BF)
        ga = dot_nt(gl, w2_ref[...])
        pre = jnp.where(lane < 64, aux, 0.0)
        act, slope = gelu_parts(pre)
        gmp = (ga * slope).astype(BF).astype(F32)
        u = (gmp * rstd).astype(BF)
        uf = u.astype(F32)
        m1 = jnp.sum(gmp * w1s_ref[0:1, :], axis=-1, keepdims=True) * (1.0 / width)
        m2 = jnp.sum(gmp * (pre - w1s_ref[1:2, :]), axis=-1, keepdims=True) * (1.0 / width)
        w2g_ref[...] += dot_tn(act.astype(BF)[:, :64], gl)
        x_ref[...] += dot_tn(u[:, :64], v)
        row_ref[0:1, :] += jnp.sum(gl_f, axis=0, keepdims=True)
        row_ref[1:2, :] += jnp.sum(gmp, axis=0, keepdims=True)
        row_ref[2:3, :] += jnp.sum(uf * mean, axis=0, keepdims=True)
        c1 = -rstd * m1
        s = -rstd * rstd * m2
        c1h, sh, mh = (t.astype(BF).astype(F32) for t in (c1, s, mean))
        ex = jnp.where(lane < 64, uf, 0.0)
        for pos, val in enumerate((c1h, c1 - c1h, sh, s - sh, mh, mean - mh)):
            ex = jnp.where(lane == 64 + pos, val, ex)
        co_ref[rows, :] = ex.astype(BF)
        put(i).start()

    @pl.loop(0, blocks)
    def _(i):
        put(i).wait()


def patch_backward(v, aux, sel, der, gts, w1s, w2rep, blocks, per):
    rows, width = v.shape
    rb = rows // blocks
    vm = pl.BlockSpec(memory_space=pltpu.VMEM)
    hb = pl.BlockSpec(memory_space=pltpu.HBM)
    sds = jax.ShapeDtypeStruct
    return pl.pallas_call(
        functools.partial(patch_bwd_kernel, blocks, per, rb, width),
        out_shape=(sds((rows, LANES), BF), sds((64, width), F32), sds((64, LANES), F32), sds((8, LANES), F32)),
        in_specs=[hb, hb, hb, hb, vm, vm, vm],
        out_specs=(hb, vm, vm, vm),
        scratch_shapes=[
            pltpu.VMEM((rows, width), BF),
            pltpu.VMEM((rows, LANES), F32),
            pltpu.VMEM((rows, LANES), BF),
            pltpu.VMEM((rows, LANES), BF),
        ] + [pltpu.SemaphoreType.DMA((blocks,))] * 4,
        compiler_params=pltpu.CompilerParams(vmem_limit_bytes=VLIM),
    )(v, aux, sel, der, gts, w1s, w2rep)


def patch_out_kernel(v_ref, sel_ref, co_ref, gt_ref, bt_ref, o_ref):
    co = co_ref[...]
    ex = co.astype(F32)
    s = ex[:, 66:67] + ex[:, 67:68]
    mean = ex[:, 68:69] + ex[:, 69:70]
    left = jnp.concatenate([sel_ref[...], co], axis=1)
    right = jnp.concatenate([gt_ref[0], bt_ref[...]], axis=0)
    mm = dot(left, right)
    for k in range(v_ref.shape[1] // LANES):
        c = slice(k * LANES, (k + 1) * LANES)
        o_ref[:, c] = (mm[:, c] + (v_ref[:, c].astype(F32) - mean) * s).astype(BF)


def patch_out(v, sel, co, gts, bt, blocks, per):
    rows, width = v.shape
    rb = rows // blocks
    row = pl.BlockSpec((rb, width), lambda i: (i, 0))
    thin = pl.BlockSpec((rb, LANES), lambda i: (i, 0))
    return pl.pallas_call(
        patch_out_kernel,
        grid=(blocks,),
        out_shape=jax.ShapeDtypeStruct((rows, width), BF),
        in_specs=[
            row, thin, thin,
            pl.BlockSpec((1, LANES, width), lambda i: (i // per, 0, 0)),
            pl.BlockSpec((LANES, width), lambda i: (0, 0)),
        ],
        out_specs=row,
        compiler_params=pltpu.CompilerParams(vmem_limit_bytes=VLIM),
    )(v, sel, co, gts, bt)


def on_device(
    patches, keep, tl_gain, tl_bias, map_w1, map_b1, map_w2, map_b2, ln1_gain, ln1_bias, qkv_weight, qv_bias,
    out_weight, out_bias, ln2_gain, ln2_bias, fc1_weight, fc1_bias, fc2_weight, fc2_bias, cotangent,
):
    micros, group, frames, count, width = patches.shape
    groups = micros * group
    shard = tl_gain.shape[0]
    me = lax.axis_index("clip")
    per = 7
    blocks = groups * per
    pb = count // per
    rb = pb * frames
    v = jnp.transpose(patches, (0, 1, 3, 2, 4)).reshape(groups * count * frames, width)
    kx = jnp.transpose(keep, (0, 1, 3, 2)).reshape(blocks, pb, frames)
    kx = jnp.repeat(kx, MAPS, axis=2).astype(BF)
    kx = jnp.pad(kx, ((0, 0), (0, 4), (0, LANES - frames * MAPS)))
    gather = functools.partial(lax.all_gather, axis_name="clip", tiled=True)
    gain, bias, w1, b1, w2 = (gather(t).astype(F32) for t in (tl_gain, tl_bias, map_w1, map_b1, map_w2))
    gw1 = (gain[:, None] * w1).astype(BF)
    w1aug = jnp.concatenate([gw1, jnp.ones((width, 1), BF), jnp.zeros((width, 63), BF)], axis=1)
    csum = jnp.sum(gw1.astype(F32), axis=0)
    w1s = jnp.zeros((8, LANES), F32).at[0, :64].set(csum).at[1, :64].set(b1 + bias @ w1)
    w2rep = jnp.tile(w2.astype(BF), (1, LANES // MAPS))
    b2rep = jnp.tile(map_b2.astype(F32), LANES // MAPS)[None]
    bt = jnp.concatenate([gw1.T, jnp.ones((2, width), BF), jnp.zeros((62, width), BF)], axis=0)
    pool, aux, sel, der = patch_forward(v, w1aug, w1s, w2rep, b2rep, kx, groups, per)
    pool = pool[:, : frames * MAPS].reshape(micros, group, frames * MAPS, width)
    tok = lax.all_to_all(pool, "map", split_axis=1, concat_axis=2, tiled=True)
    tok = tok.reshape(-1, width)
    vecs = jnp.stack([ln1_gain, ln1_bias, qv_bias[0], qv_bias[1], out_bias, ln2_gain, ln2_bias, fc2_bias])
    vec = gather(vecs, axis=1).astype(F32)
    fb = gather(fc1_bias).astype(F32)[None]
    wq, wo, wf1, wf2 = (gather(t) for t in (qkv_weight, out_weight, fc1_weight, fc2_weight))
    out, gq, go, g1, g2, gtok, gvec, gb1 = token_layer(tok, cotangent.reshape(tok.shape), wq, wo, wf1, wf2, vec, fb)
    gts = lax.all_to_all(
        gtok.reshape(micros, 1, -1, width), "map", split_axis=2, concat_axis=1, tiled=True
    ).reshape(groups, frames * MAPS, width)
    gts = (gts.astype(F32) * count**-0.5).astype(BF)
    gts = jnp.pad(gts, ((0, 0), (0, LANES - frames * MAPS), (0, 0)))
    w2n = jnp.pad(w2rep, ((0, 64), (0, 0)))
    co, xt, w2g, row = patch_backward(v, aux, sel, der, gts, w1s, w2n, blocks, per)
    pg = patch_out(v, sel, co, gts, bt, blocks, per)
    pg = jnp.transpose(pg.reshape(micros, group, count, frames, width), (0, 1, 3, 2, 4))
    x = (xt - row[2, :64][:, None]).T
    w2g = jnp.sum(w2g.reshape(64, LANES // MAPS, MAPS), axis=1)
    b2g = jnp.sum(row[0].reshape(LANES // MAPS, MAPS), axis=0)

    def scatter(t, axis=0):
        t = lax.psum_scatter(t.astype(BF), "clip", scatter_dimension=axis, tiled=True)
        return lax.psum(t, "map").astype(F32)

    xs = scatter(x)
    gb = lax.psum(row[1, :64], ("clip", "map"))
    b2g = lax.psum(b2g, ("clip", "map"))
    gvec = scatter(gvec, 1)
    gains, biases, w1l = tl_gain.astype(F32), tl_bias.astype(F32), map_w1.astype(F32)
    n_map = shard * 64 // width
    return (
        out.reshape(cotangent.shape),
        pg,
        jnp.sum(w1l * xs, axis=1),
        w1l @ gb,
        gains[:, None] * xs + biases[:, None] * gb[None],
        lax.dynamic_slice(gb, (me * n_map,), (n_map,)),
        scatter(w2g),
        b2g,
        gvec[0],
        gvec[1],
        scatter(gq),
        gvec[2:4],
        scatter(go),
        gvec[4],
        gvec[5],
        gvec[6],
        scatter(g1),
        scatter(gb1[0]),
        scatter(g2),
        gvec[7],
    )


def solution(mesh):
    weights = (
        P("clip"), P("clip"), P("clip", None), P("clip"), P("clip", None), P(), P("clip"), P("clip"), P("clip", None),
        P(None, "clip"), P("clip", None), P("clip"), P("clip"), P("clip"), P("clip", None), P("clip"), P("clip", None),
        P("clip"),
    )
    tokens = P(None, ("clip", "map"), None, None)
    frames = P(None, "clip", "map", None, None)
    return jax.shard_map(
        on_device,
        mesh=mesh,
        in_specs=(frames, P(None, "clip", "map", None)) + weights + (tokens,),
        out_specs=(tokens, frames) + weights,
        check_vma=False,
    )
```

time: 1280 us -> 787 us (0.61)
  matrix products: 220 us -> 0.78 us
  local copies, waits for them, and re-layouts: 218 us -> 24.4 us
  Pallas kernels: 0 us -> 189 us
  other arithmetic: 202 us -> 13.9 us
  waiting for transfers between devices: 376 us -> 308 us
    dot_general x54 -> x2, matrix products: 220 us -> 0.78 us  [the longest x1 0.64 us: on_device(): w1l @ gb]
    pallas_call x0 -> x4, Pallas kernels: none -> 189 us  [the longest x1 78.3 us: token_layer(): pl.pallas_call(token_kernel, out_shape=(sds((n, d), BF), sds((d, 3 * d),...]
    reduce_sum x22 -> x3, other arithmetic: 75.4 us -> 0.17 us  [the longest x1 0.12 us: on_device(): csum = jnp.sum(gw1.astype(F32), axis=0)]
    convert_element_type x8, local copies, waits for them, and re-layouts: 76.4 us -> 1.6 us  [the longest x5 0.8 us: on_device(): kx = jnp.repeat(kx, MAPS, axis=2).astype(BF)]
    convert_element_type x51 -> x15, other arithmetic: 79.5 us -> 11.7 us  [the longest x7 8.06 us: scatter(): return lax.psum(t, 'map').astype(F32)]
    unnamed x19 -> x13, waiting for transfers between devices: 55.4 us -> 5.24 us
    reshape x6 -> x2, local copies, waits for them, and re-layouts: 39.6 us -> 3.8 us  [the longest x1 2.09 us: on_device(): pool = pool[:, :frames * MAPS].reshape(micros, group, frames * MAPS, width)]
    unnamed x439 -> x49, local copies, waits for them, and re-layouts: 45.6 us -> 9.88 us
  transfers between devices with their start and end apart: 21 -> 13, of which waited for: 8 -> 6; matrix products, arithmetic and copies ran while one was open for 45% -> 4% of each run, Pallas kernels for 0% -> 14%
where the time goes in v1:
time: 787 us; the launch traced here: 785 us
  waiting for transfers between devices  308 us (39%)
  blocking collectives  224 us (28%)
  Pallas kernels  189 us (24%)
  local copies, waits for them, and re-layouts  24.4 us (3%)
  between operations  17.4 us (2%)
  other arithmetic  13.9 us (2%)
    reduce_scatter x4, waiting for transfers between devices, scatter(): lax.psum_scatter(t.astype(BF), 'clip', scatter_dimension=axis, tiled=True)  280 us
    unnamed x2, blocking collectives  121 us
    pallas_call x1, Pallas kernels, token_layer(): pl.pallas_call(token_kernel, out_shape=(sds((n, d), BF), sds((d, 3 * d),...  78.3 us
    pallas_call x1, Pallas kernels, patch_forward(): pl.pallas_call(functools.partial(patch_fwd_kernel, blocks, per, rb, width...  48.4 us
    all_gather x2, blocking collectives, on_device(): gather(t).astype(F32)  37.8 us
    psum x1, blocking collectives, on_device(): gb = lax.psum(row[1, :64], ('clip', 'map'))  37.2 us
    pallas_call x1, Pallas kernels, patch_backward(): pl.pallas_call(functools.partial(patch_bwd_kernel, blocks, per, rb, width...  34.3 us
    pallas_call x1, Pallas kernels, patch_out(): pl.pallas_call(patch_out_kernel, grid=(blocks,), out_shape=jax.ShapeDtype...  28.3 us
  transfers between devices with their start and end apart: 13, of which 6 were waited for; matrix products, arithmetic and copies ran while one was open for 4% of the time, Pallas kernels for 14%

profile of v1, /device:TPU:0, one launch (start us, length us, event | category | flops | bytes accessed | tf_op | source)
XLA Modules:
  0.0 784.8 jit_solution(10864881343386570778)
XLA Ops:
  16.7 63.3 %all-reduce.11 = (bf16[768]{0:T(1024)(128)(2,1)S(1)}, bf16[768]{0:T(1024)(128)(2,1)S(1)}, bf16[64]{0:T(256)(128)(2,1)S(1)}, bf16[3072]{0:T(1024)(128)(2,1)S(1)}) all-reduce(bf16[768]{0:T(1024)(128)(2,1)S(1)} %dynamic-update-slice.4, bf16[768]{0:T(1024)(128)(2,1)S(1)} %dynamic-update-slice.6, ...), channel_id=1, replica_groups=mesh['clip'=16,'map'=2] {'clip'}, use_global_device_ids=true, to_apply=%add.3 | all-reduce | flops 4672 | bytes 18688
  79.9 18.5 %all_gather.34 = bf16[768,64]{1,0:T(8,128)(2,1)S(1)} all-gather(bf16[48,64]{1,0:T(8,128)(2,1)} %param.29), channel_id=1, replica_groups=mesh['clip'=16,'map'=2] {'clip'}, dimensions={0}, use_global_device_ids=true | all-gather | bytes 104448 | tf_op jit(solution)/shard_map/all_gather | solution.py:492
  99.8 19.3 %all-gather = bf16[16,4,8]{2,1,0:T(4,128)(2,1)S(1)} all-gather(bf16[1,4,8]{2,1,0:T(4,128)(2,1)} %bitcast.110), channel_id=1, replica_groups=mesh['clip'=16,'map'=2] {'clip'}, dimensions={0}, use_global_device_ids=true | all-gather | bytes 1088 | tf_op jit(solution)/shard_map/all_gather | solution.py:492
  123.8 48.4 %shard_map.356 = (bf16[4,128,768]{2,1,0:T(8,128)(2,1)}, f32[12544,128]{1,0:T(8,128)}, bf16[12544,128]{1,0:T(8,128)(2,1)}, bf16[12544,128]{1,0:T(8,128)(2,1)}) custom-call(bf16[12544,768]{1,0:T(8,128)(2,1)} %bitcast.92, bf16[768,128]{1,0:T(8,128)(2,1)} %copy.83.w1_ref, f32[8,128]{1,0:T(8,128)} %copy-done.3, bf16[64,128]{1,0:T(8,128)(2,1)} %copy.84.w2_ref, ...), custom_call_target="tpu_custom_call" | custom-call | tf_op jit(solution)/shard_map/pallas_call | solution.py:105
  172.3 2.1 copy.85
  174.3 3.5 all-to-all-start
  178.6 18.2 %all-gather.1 = bf16[16,48,8]{1,2,0:T(8,128)(2,1)S(1)} all-gather(bf16[1,48,8]{1,2,0:T(8,128)(2,1)S(1)} %bitcast.108), channel_id=1, replica_groups=mesh['clip'=16,'map'=2] {'clip'}, dimensions={0}, use_global_device_ids=true | all-gather | bytes 13056 | tf_op jit(solution)/shard_map/all_gather | solution.py:505
  198.4 11.8 %all-gather.13.cloned.1.call-done.w2 = bf16[3072,768]{1,0:T(8,128)(2,1)} async-done(((bf16[192,768]{1,0:T(8,128)(2,1)}), bf16[3072,768]{1,0:T(8,128)(2,1)}) %all-gather.13.cloned.1.call-update) | async-done | bytes 4718608 | tf_op jit(solution)/shard_map/all_gather | solution.py:507
  210.2 78.3 %shard_map.357 = (bf16[512,768]{1,0:T(8,128)(2,1)}, bf16[768,2304]{1,0:T(8,128)(2,1)}, bf16[768,768]{1,0:T(8,128)(2,1)}, bf16[768,3072]{1,0:T(8,128)(2,1)}, bf16...) custom-call(bf16[512,768]{1,0:T(8,128)(2,1)} %bitcast.98, ...), custom_call_target="tpu_custom_call" | custom-call | tf_op jit(solution)/shard_map/pallas_call | solution.py:328
  293.3 1.7 copy.88
  295.0 3.5 all-to-all-start.1
  299.4 10.6 %all-to-all-done.1 = bf16[2,1,256,768]{3,0,1,2:T(2,128)(2,1)S(1)} async-done(((bf16[2,1,256,768]{3,0,1,2:T(2,128)(2,1)}), bf16[2,1,256,768]{3,0,1,2:T(2,128)(2,1)S(1)}, u32[]{:S(2)}, u32[]{:S(2)}) %all-to-all-start.1) | async-done | bytes 786464 | tf_op jit(solution)/shard_map/all_to_all | solution.py:509
  311.1 34.3 %shard_map.358 = (bf16[12544,128]{1,0:T(8,128)(2,1)}, f32[64,768]{1,0:T(8,128)}, f32[64,128]{1,0:T(8,128)}, f32[8,128]{1,0:T(8,128)}) custom-call(bf16[12544,768]{1,0:T(8,128)(2,1)} %bitcast.93, f32[12544,128]{1,0:T(8,128)} %get-tuple-element.63.aux_hbm, bf16[12544,128]{1,0:T(8,128)(2,1)} %get-tuple-element.62.sel_ref, ...), custom_call_target="tpu_custom_call" | custom-call | tf_op jit(solution)/shard_map/pallas_call | solution.py:428
  351.1 52.0 %reduce-scatter.13.cloned.1.call-done = bf16[48,768]{1,0:T(8,128)(2,1)} async-done(((bf16[768,768]{1,0:T(8,128)(2,1)}), bf16[48,768]{1,0:T(8,128)(2,1)}) %reduce-scatter.13.cloned.1.call-update) | async-done | bytes 73744 | tf_op jit(solution)/shard_map/reduce_scatter | solution.py:523
  403.1 70.9 %reduce-scatter.11.cloned.1.call-done = bf16[48,2304]{1,0:T(8,128)(2,1)} async-done(((bf16[768,2304]{1,0:T(8,128)(2,1)}), bf16[48,2304]{1,0:T(8,128)(2,1)}) %reduce-scatter.11.cloned.1.call-update) | async-done | bytes 221200 | tf_op jit(solution)/shard_map/reduce_scatter | solution.py:523
  474.0 78.3 %reduce-scatter.15.cloned.1.call-done = bf16[48,3072]{1,0:T(8,128)(2,1)} async-done(((bf16[768,3072]{1,0:T(8,128)(2,1)}), bf16[48,3072]{1,0:T(8,128)(2,1)}) %reduce-scatter.15.cloned.1.call-update) | async-done | bytes 294928 | tf_op jit(solution)/shard_map/reduce_scatter | solution.py:523
  552.3 79.0 %reduce-scatter.17.cloned.1.call-done = bf16[192,768]{1,0:T(8,128)(2,1)} async-done(((bf16[3072,768]{1,0:T(8,128)(2,1)}), bf16[192,768]{1,0:T(8,128)(2,1)}) %reduce-scatter.17.cloned.1.call-update) | async-done | bytes 294928 | tf_op jit(solution)/shard_map/reduce_scatter | solution.py:523
  633.1 58.0 %all-reduce.10 = (bf16[64,8]{1,0:T(8,128)(2,1)S(1)}, bf16[3072]{0:T(1024)(128)(2,1)S(1)}) all-reduce(bf16[64,8]{1,0:T(8,128)(2,1)S(1)} %copy.93, bf16[3072]{0:T(1024)(128)(2,1)S(1)} %convert_reduce_fusion.1), channel_id=3, replica_groups=mesh['clip'=16,'map'=2] {'clip'}, use_global_device_ids=true, to_apply=%region_6.7.clone | all-reduce | flops 3584 | bytes 14336
  691.2 37.2 %all-reduce.9 = (f32[64]{0:T(128)S(1)}, f32[8]{0:T(128)}) all-reduce(f32[64]{0:T(128)S(1)} %get-tuple-element.182, f32[8]{0:T(128)S(1)} %reduce_sum.39), channel_id=1, replica_groups=mesh['clip'=16,'map'=2] {'clip','map'}, use_global_device_ids=true, to_apply=%region_4.5 | all-reduce | flops 72 | bytes 576 | tf_op jit(solution)/shard_map/psum | solution.py:527
  729.0 28.3 %shard_map.359 = bf16[12544,768]{1,0:T(8,128)(2,1)} custom-call(bf16[12544,768]{1,0:T(8,128)(2,1)} %bitcast.94, bf16[12544,128]{1,0:T(8,128)(2,1)} %get-tuple-element.62.sel_ref, bf16[12544,128]{1,0:T(8,128)(2,1)} %get-tuple-element.66.co_ref, bf16[4,128,768]{2,1,0:T(8,128)(2,1)} %bitcast.97, bf16[128,768]{1,0:T(8,128)(2,1)} %maximum_maximum_fusion.1.bt_ref), custom_call_target="tpu_custom_call" | custom-call | tf_op jit(solution)/shard_map/pallas_call | solution.py:461
  758.7 9.1 %all-reduce.12 = (bf16[48,64]{0,1:T(8,128)(2,1)S(1)}, bf16[4,8]{1,0:T(4,128)(2,1)S(1)}, bf16[8,48]{1,0:T(8,128)(2,1)S(1)}, bf16[192]{0:T(256)(128)(2,1)S(1)}) all-reduce(bf16[48,64]{0,1:T(8,128)(2,1)S(1)} %copy.97, bf16[4,8]{1,0:T(4,128)(2,1)S(1)} %constant_dynamic-slice_fusion, ...), channel_id=1, replica_groups=mesh['clip'=16,'map'=2] {'map'}, use_global_device_ids=true, to_apply=%region_2.3 | all-reduce | flops 3680 | bytes 14720 | tf_op jit(solution)/shard_map/psum | solution.py:524
  771.3 1.8 convert_element_type.128
  773.1 1.8 convert_element_type.132
  774.9 1.7 convert_element_type.126
  (133 shorter events, 35.6 us)
Async XLA Ops:
  7.2 114.4 %copy-start.5 = (bf16[8]{0:T(256)(128)(2,1)S(1)}, bf16[8]{0:T(256)(128)(2,1)}, u32[]{:S(2)}) copy-start(bf16[8]{0:T(256)(128)(2,1)} %param.32) | copy-start | bytes 52
  7.2 191.2 %all-gather.9.cloned.1.call-start = ((), (), s32[]{:S(2)}) async-start(), calls=%async_computation.9 | async-start | bytes 1253376 | tf_op jit(solution)/shard_map/all_gather | solution.py:507
  7.9 190.5 %all-gather.7.cloned.1.call-start = ((), (), s32[]{:S(2)}) async-start(), calls=%async_computation.8 | async-start | bytes 3760128 | tf_op jit(solution)/shard_map/all_gather | solution.py:507
  8.7 189.8 %all-gather.11.cloned.1.call-start = ((), (), s32[]{:S(2)}) async-start(), calls=%async_computation.10 | async-start | bytes 5013504 | tf_op jit(solution)/shard_map/all_gather | solution.py:507
  9.4 200.8 %all-gather.13.cloned.1.call-start = ((), (), s32[]{:S(2)}) async-start(), calls=%async_computation.11 | async-start | bytes 5013504 | tf_op jit(solution)/shard_map/all_gather | solution.py:507
  123.8 54.8 %copy-start.6 = (bf16[48]{0:T(256)(128)(2,1)S(1)}, bf16[48]{0:T(256)(128)(2,1)}, u32[]{:S(2)}) copy-start(bf16[48]{0:T(256)(128)(2,1)} %param.33) | copy-start | bytes 292
  123.8 54.8 %copy-start.7 = (bf16[48]{0:T(256)(128)(2,1)S(1)}, bf16[48]{0:T(256)(128)(2,1)}, u32[]{:S(2)}) copy-start(bf16[48]{0:T(256)(128)(2,1)} %param.34) | copy-start | bytes 292
  123.8 54.8 %copy-start.8 = (bf16[2,48]{1,0:T(2,128)(2,1)S(1)}, bf16[2,48]{1,0:T(2,128)(2,1)}, u32[]{:S(2)}) copy-start(bf16[2,48]{1,0:T(2,128)(2,1)} %param.36) | copy-start | bytes 580
  123.8 54.8 %copy-start.9 = (bf16[48]{0:T(256)(128)(2,1)S(1)}, bf16[48]{0:T(256)(128)(2,1)}, u32[]{:S(2)}) copy-start(bf16[48]{0:T(256)(128)(2,1)} %param.38) | copy-start | bytes 292
  123.8 54.8 %copy-start.10 = (bf16[48]{0:T(256)(128)(2,1)S(1)}, bf16[48]{0:T(256)(128)(2,1)}, u32[]{:S(2)}) copy-start(bf16[48]{0:T(256)(128)(2,1)} %param.39) | copy-start | bytes 292
  123.8 54.8 %copy-start.11 = (bf16[48]{0:T(256)(128)(2,1)S(1)}, bf16[48]{0:T(256)(128)(2,1)}, u32[]{:S(2)}) copy-start(bf16[48]{0:T(256)(128)(2,1)} %param.40) | copy-start | bytes 292
  123.8 54.8 %copy-start.12 = (bf16[48]{0:T(256)(128)(2,1)S(1)}, bf16[48]{0:T(256)(128)(2,1)}, u32[]{:S(2)}) copy-start(bf16[48]{0:T(256)(128)(2,1)} %param.44) | copy-start | bytes 292
  174.3 23.1 %all-to-all-start = ((bf16[2,2,128,768]{3,2,0,1:T(8,128)(2,1)}), bf16[2,2,128,768]{3,2,0,1:T(8,128)(2,1)S(1)}, u32[]{:S(2)}, u32[]{:S(2)}) async-start(bf16[2,2,128,768]{3,2,0,1:T(8,128)(2,1)} %copy.85), calls=%async_computation | async-start | bytes 1572864 | tf_op jit(solution)/shard_map/all_to_all | solution.py:502
  177.9 172.4 %reduce-scatter.21.cloned.1.call-start = ((), (), s32[]{:S(2)}) async-start(), calls=%async_computation.17 | async-start | bytes 208896
  290.1 113.0 %reduce-scatter.13.cloned.1.call-start = ((), (), s32[]{:S(2)}) async-start(), calls=%async_computation.13 | async-start | bytes 1253376 | tf_op jit(solution)/shard_map/reduce_scatter | solution.py:523
  290.7 183.3 %reduce-scatter.11.cloned.1.call-start = ((), (), s32[]{:S(2)}) async-start(), calls=%async_computation.12 | async-start | bytes 3760128 | tf_op jit(solution)/shard_map/reduce_scatter | solution.py:523
  291.4 260.9 %reduce-scatter.15.cloned.1.call-start = ((), (), s32[]{:S(2)}) async-start(), calls=%async_computation.14 | async-start | bytes 5013504 | tf_op jit(solution)/shard_map/reduce_scatter | solution.py:523
  292.2 339.1 %reduce-scatter.17.cloned.1.call-start = ((), (), s32[]{:S(2)}) async-start(), calls=%async_computation.15 | async-start | bytes 5013504 | tf_op jit(solution)/shard_map/reduce_scatter | solution.py:523
  295.0 15.0 %all-to-all-start.1 = ((bf16[2,1,256,768]{3,0,1,2:T(2,128)(2,1)}), bf16[2,1,256,768]{3,0,1,2:T(2,128)(2,1)S(1)}, u32[]{:S(2)}, u32[]{:S(2)}) async-start(bf16[2,1,256,768]{3,0,1,2:T(2,128)(2,1)} %copy.88), calls=%async_computation.1 | async-start | bytes 1572864 | tf_op jit(solution)/shard_map/all_to_all | solution.py:509
  298.6 459.4 %reduce-scatter.19.cloned.1.call-start = ((), (), s32[]{:S(2)}) async-start(), calls=%async_computation.16 | async-start | bytes 208896
  311.1 37.8 %copy-start.13 = (bf16[48]{0:T(256)(128)(2,1)S(1)}, bf16[48]{0:T(256)(128)(2,1)}, u32[]{:S(2)}) copy-start(bf16[48]{0:T(256)(128)(2,1)} %param.27) | copy-start | bytes 292
  311.1 37.9 %copy-start.14 = (bf16[48]{0:T(256)(128)(2,1)S(1)}, bf16[48]{0:T(256)(128)(2,1)}, u32[]{:S(2)}) copy-start(bf16[48]{0:T(256)(128)(2,1)} %param.28) | copy-start | bytes 292
  311.1 39.2 %copy-start.4 = (f32[1,3072]{1,0:T(1,128)S(1)}, f32[1,3072]{1,0:T(1,128)}, u32[]{:S(2)}) copy-start(f32[1,3072]{1,0:T(1,128)} %get-tuple-element.74) | copy-start | bytes 36868
  348.0 423.3 %all-reduce.16.cloned.1.call-start = ((), (), s32[]{:S(2)}) async-start(), calls=%async_computation.18 | async-start | bytes 1769472 | tf_op jit(solution)/shard_map/psum | solution.py:524
  (4 other events, 45.9 us)
Sparse Core Ops, SparseCore 0:
  10.3 41.1 all-gather.8
  53.8 46.9 all-gather.6
  103.2 52.8 all-gather.10
  158.2 52.0 all-gather.12
  290.2 52.2 reduce-scatter.20
  346.0 57.1 reduce-scatter.12
  407.0 66.9 reduce-scatter.10
  477.9 74.3 reduce-scatter.14
  556.6 74.6 reduce-scatter.16
  635.2 52.6 reduce-scatter.18
  690.4 36.5 all-reduce.15

commit v2 on v1

--- a/solution.py
+++ b/solution.py
@@ -42,15 +42,213 @@
     return pl.ds(pl.multiple_of(x, n), n)
 
 
-def patch_fwd_kernel(
-    blocks, per, rb, width, v_ref, w1_ref, w1s_ref, w2_ref, b2_ref, kx_ref, pool_ref, aux_ref, sel_ref, der_ref,
-    vbuf, acc, rmat, delta, vsem,
+MESH = pl.DeviceIdType.MESH
+
+
+class Place:
+    def __init__(self, n, m):
+        self.n, self.m, self.na = n, m, n // 4
+        self.clip, self.map = lax.axis_index("clip"), lax.axis_index("map")
+        self.a, self.b, self.c = self.clip // 4, (self.clip // 2) % 2, self.clip % 2
+        self.half = self.map % 2
+        self.twin = self.map + 1 - 2 * self.half
+        self.core_dev = (self.shard(self.a, self.b, 1 - self.c), self.map)
+        self.y_dev = (self.shard(self.a, 1 - self.b, self.c), self.map)
+        self.x_dev = (self.clip, self.twin)
+
+    def shard(self, a, b, c):
+        return (a * 2 + b) * 2 + c
+
+    def back(self, k):
+        return lax.rem(self.a + self.na - k, self.na)
+
+    def ahead(self, k):
+        return lax.rem(self.a + k, self.na)
+
+    def greet(self):
+        bar = pltpu.get_barrier_semaphore()
+        for k in range(1, self.n):
+            pl.semaphore_signal(bar, inc=1, device_id=(lax.rem(self.clip + k, self.n), self.map), device_id_type=MESH)
+        for k in range(1, self.m):
+            pl.semaphore_signal(bar, inc=1, device_id=(self.clip, lax.rem(self.map + k, self.m)), device_id_type=MESH)
+        pl.semaphore_wait(bar, self.n + self.m - 2)
+
+
+def remote(src, dst, send, recv, dev):
+    return pltpu.make_async_remote_copy(
+        src_ref=src, dst_ref=dst, send_sem=send, recv_sem=recv, device_id=dev, device_id_type=MESH
+    )
+
+
+class Gather:
+    def __init__(self, place, chunks, sends, recvs):
+        self.p, self.chunks, self.sends, self.recvs = place, chunks, sends, recvs
+        self.started = []
+
+    def block(self, i, s, half):
+        ref, panels, rows, pitch, skip, _ = self.chunks[i]
+        r = pl.ds(pl.multiple_of(s * pitch + skip, 8), rows)
+        c = slice(None) if half is None else pl.ds(pl.multiple_of(half * (ref.shape[-1] // 2), LANES), ref.shape[-1] // 2)
+        return ref.at[r, c] if panels is None else ref.at[panels, r, c]
+
+    def send(self, i, at, dev, s, half):
+        b = self.block(i, s, half)
+        j = i * self.per() + at
+        remote(b, b, self.sends.at[j], self.recvs.at[j], dev).start()
+        self.started.append((i, j, half is None))
+
+    def wait(self, i, at, s, half):
+        b = self.block(i, s, half)
+        j = i * self.per() + at
+        remote(b, b, self.sends.at[j], self.recvs.at[j], self.p.core_dev).wait_recv()
+
+    def per(self):
+        return 11 * self.p.na
+
+    def at_z(self, k):
+        return k - 1
+
+    def at_y(self, k):
+        return self.p.na - 1 + k
+
+    def at_x(self, side, k):
+        return (2 + side) * self.p.na + k
+
+    def at_diag_y(self, k):
+        return 4 * self.p.na + k
+
+    def at_core(self, e):
+        return 5 * self.p.na + e
+
+    def own(self, i):
+        p = self.p
+        for k in range(1, p.na):
+            self.send(i, self.at_z(k), (p.shard(p.ahead(k), p.b, p.c), p.map), p.clip, p.half)
+        self.send(i, self.at_y(0), p.y_dev, p.clip, None)
+        self.send(i, self.at_core(0), p.core_dev, p.clip, None)
+
+    def by_x(self, i):
+        return self.chunks[i][5]
+
+    def from_z(self, i, k):
+        p = self.p
+        s = p.shard(p.back(k), p.b, p.c)
+        self.wait(i, self.at_z(k), s, p.half)
+        self.send(i, self.at_x(0, k), p.x_dev, s, p.half)
+        self.send(i, self.at_y(k), p.y_dev, s, p.half)
+        self.send(i, self.at_core(k), p.core_dev, s, p.half)
+
+    def from_y(self, i, k):
+        p = self.p
+        if k == 0:
+            s = p.shard(p.a, 1 - p.b, p.c)
+            self.wait(i, self.at_y(0), s, None)
+            self.send(i, self.at_core(p.na), p.core_dev, s, None)
+            return
+        s = p.shard(p.back(k), 1 - p.b, p.c)
+        self.wait(i, self.at_y(k), s, p.half)
+        if self.by_x(i):
+            self.send(i, self.at_x(1, k), p.x_dev, s, p.half)
+        self.send(i, self.at_core(p.na + k), p.core_dev, s, p.half)
+
+    def from_x(self, i, side, k):
+        p = self.p
+        b = p.b if side == 0 else 1 - p.b
+        s = p.shard(p.back(k), b, p.c)
+        by_x = self.by_x(i)
+        self.wait(i, self.at_x(side, k) if by_x or side == 0 else self.at_diag_y(k), s, 1 - p.half)
+        if side == 0 and not by_x:
+            self.send(i, self.at_diag_y(k), p.y_dev, s, 1 - p.half)
+        self.send(i, self.at_core((2 + side) * p.na + k), p.core_dev, s, 1 - p.half)
+
+    def from_core(self, i):
+        p, o = self.p, 1 - self.p.c
+        self.wait(i, self.at_core(0), p.shard(p.a, p.b, o), None)
+        self.wait(i, self.at_core(p.na), p.shard(p.a, 1 - p.b, o), None)
+        for k in range(1, p.na):
+            for side in range(2):
+                s = p.shard(p.back(k), p.b if side == 0 else 1 - p.b, o)
+                self.wait(i, self.at_core(p.na * side + k), s, p.half)
+                self.wait(i, self.at_core((2 + side) * p.na + k), s, 1 - p.half)
+
+    def finish(self):
+        for i in range(len(self.chunks)):
+            self.from_core(i)
+        for i, j, full in self.started:
+            b = self.block(i, self.p.clip, None if full else self.p.half)
+            remote(b, b, self.sends.at[j], self.recvs.at[j], self.p.core_dev).wait_send()
+
+    def events(self):
+        n, ks = len(self.chunks), range(1, self.p.na)
+        call = functools.partial
+        out = [call(self.own, i) for i in range(AHEAD)]
+        for i in range(n + 2):
+            if i < n:
+                for k in ks:
+                    out.append(call(self.from_z, i, k))
+                    if k == self.p.na - 2 and i + AHEAD < n:
+                        out.append(call(self.own, i + AHEAD))
+                out.append(call(self.from_y, i, 0))
+            if 0 <= i - 1 < n:
+                out += [call(self.from_y, i - 1, k) for k in ks]
+                out += [call(self.from_x, i - 1, 0, k) for k in ks]
+            if 0 <= i - 2 < n:
+                out += [call(self.from_x, i - 2, 1, k) for k in ks]
+        return out
+
+
+def forward_kernel(
+    n, m, blocks, per, count, v_ref, kx_ref, b2_ref, pa_ref, pb_ref, wq_ref, wo_ref, w1_ref, w2_ref,
+    wa_ref, wb_ref, tok_ref, aux_ref, sel_ref, der_ref, vec_ref, fb_ref, wt_ref, small_ref,
+    vbuf, acc, pool, rmat, delta, pag, pbg, w1v, w2v, ss, vsem, lsem, gsend, grecv, psend, precv, tsend, trecv,
 ):
+    rows, width = v_ref.shape
+    rb = rows // blocks
     frames = rb // (kx_ref.shape[1] - 4)
+    fm = tok_ref.shape[2]
+    me = Place(n, m)
+    shard = width // n
+    ff = w1_ref.shape[1]
+    fsh = ff // n
 
     @pl.loop(0, blocks)
     def _(i):
         pltpu.make_async_copy(v_ref.at[pl.ds(i * rb, rb)], vbuf.at[pl.ds(i * rb, rb)], vsem.at[i]).start()
+
+    own = pl.ds(pl.multiple_of(me.clip * shard, 8), shard)
+    local = []
+    for p in range(3):
+        local.append((wq_ref.at[:, pl.ds(p * width, width)], wa_ref.at[p, own]))
+    local.append((wo_ref, wa_ref.at[3, own]))
+    for p in range(ff // width):
+        local.append((w1_ref.at[:, pl.ds(p * width, width)], wa_ref.at[4 + p, own]))
+    local.append((w2_ref, wb_ref.at[pl.ds(pl.multiple_of(me.clip * fsh, 8), fsh)]))
+    local.append((pa_ref, pag.at[me.clip]))
+    local.append((pb_ref, pbg.at[me.clip]))
+    local = [pltpu.make_async_copy(s, d, lsem.at[i]) for i, (s, d) in enumerate(local)]
+    for d in local:
+        d.start()
+    me.greet()
+    small = []
+    for k in range(1, n):
+        dev = (lax.rem(me.clip + k, n), me.map)
+        small.append(remote(pa_ref, pag.at[me.clip], psend.at[0, k], precv.at[0, k], dev))
+        small[-1].start()
+    for d in local:
+        d.wait()
+    chunks = [(wa_ref, pl.ds(2 * q, 2), shard, shard, 0, True) for q in range(4)]
+    chunks += [(wb_ref, None, fsh // 2, fsh, q * (fsh // 2), q == 0) for q in range(2)]
+    g = Gather(me, chunks, gsend, grecv)
+    todo = g.events()
+    slots = [[] for _ in range(blocks + 1)]
+    for at, f in enumerate(todo[AHEAD:]):
+        slots[min(int(at * STEP * blocks / len(todo)), blocks)].append(f)
+    for f in todo[:AHEAD]:
+        f()
+    for k in range(1, n):
+        dev = (lax.rem(me.clip + k, n), me.map)
+        small.append(remote(pb_ref, pbg.at[me.clip], psend.at[1, k], precv.at[1, k], dev))
+        small[-1].start()
 
     r2 = lax.broadcasted_iota(jnp.int32, rmat.shape, 0)
     c2 = lax.broadcasted_iota(jnp.int32, rmat.shape, 1)
@@ -59,29 +257,73 @@
     c1 = lax.broadcasted_iota(jnp.int32, delta.shape, 1)
     delta[...] = jnp.where(r1 % frames == c1 // MAPS, 1.0, 0.0)
 
+    for k in range(1, n):
+        s = lax.rem(me.clip + n - k, n)
+        remote(pa_ref, pag.at[s], psend.at[0, k], precv.at[0, k], me.core_dev).wait_recv()
+    par = pa_ref.shape[0]
+    flat = pag[...].reshape(n * par, LANES)
+    q2 = 64 // n
+
+    def pick(lo, count_rows, want_s, want_j):
+        r = lax.broadcasted_iota(jnp.int32, (count_rows, 1), 0) + lo
+        kk = lax.broadcasted_iota(jnp.int32, (1, n * par), 1)
+        s, j = kk // par, kk % par
+        sel = jnp.logical_and(s == want_s(r), j == want_j(r))
+        return dot(jnp.where(sel, 1.0, 0.0).astype(BF), flat)
+
+    lane = lax.broadcasted_iota(jnp.int32, (1, LANES), 1)
+    for q in range(width // 128):
+        got = pick(q * 128, 128, lambda r: r // shard, lambda r: r % shard)
+        got = jnp.where(lane < 64, got, jnp.where(lane == 64, 1.0, 0.0))
+        w1v[q * 128 : (q + 1) * 128, :] = got.astype(BF)
+        wt_ref[0:64, q * 128 : (q + 1) * 128] = got.T[0:64, :].astype(BF)
+    tail = lax.broadcasted_iota(jnp.int32, (64, width), 0)
+    wt_ref[64:128, :] = jnp.where(tail < 2, 1.0, 0.0).astype(BF)
+    got = pick(0, 64, lambda r: r // q2, lambda r: shard + 1 + r % q2)
+    w2v[...] = got.astype(BF)
+    small_ref[...] = jnp.zeros(small_ref.shape, F32)
+    small_ref[8:72, :] = got
+    r = lax.broadcasted_iota(jnp.int32, (8, 1), 0)
+    kk = lax.broadcasted_iota(jnp.int32, (1, n * par), 1) % par
+    sums = dot(jnp.where(jnp.logical_or(jnp.logical_and(r == 0, kk < shard), jnp.logical_and(r == 1, kk == shard)), 1.0, 0.0).astype(BF), flat)
+    csum = jnp.where(lane < 64, sums[0:1, :], 0.0)
+    cadd = jnp.where(lane < 64, pltpu.roll(sums, 64, 1)[0:1, :] + sums[1:2, :], 0.0)
+    ss[0:1, :] = csum
+    ss[1:2, :] = cadd
+    small_ref[0:1, :] = csum
+    small_ref[1:2, :] = cadd
+
     @pl.loop(0, blocks)
     def _(i):
-        rows = pl.ds(pl.multiple_of(i * rb, 16), rb)
+        for at, fs in enumerate(slots[:blocks]):
+            if fs:
+
+                @pl.when(i == at)
+                def _():
+                    for f in fs:
+                        f()
+
+        rr = pl.ds(pl.multiple_of(i * rb, 16), rb)
         pltpu.make_async_copy(v_ref.at[pl.ds(i * rb, rb)], vbuf.at[pl.ds(i * rb, rb)], vsem.at[i]).wait()
-        v = vbuf[rows, :]
-        mm = dot(v, w1_ref[...])
+        v = vbuf[rr, :]
+        mm = dot(v, w1v[...])
         mean = mm[:, 64:65] * (1.0 / width)
         sq = jnp.zeros((rb, LANES), F32)
         for k in range(width // LANES):
             c = v[:, k * LANES : (k + 1) * LANES].astype(F32) - mean
             sq = sq + c * c
         rstd = lax.rsqrt(jnp.sum(sq, axis=-1, keepdims=True) * (1.0 / width) + EPS)
-        pre = rstd * (mm - mean * w1s_ref[0:1, :]) + w1s_ref[1:2, :]
+        pre = rstd * (mm - mean * ss[0:1, :]) + ss[1:2, :]
         act, _ = gelu_parts(pre)
-        logit = dot(act.astype(BF)[:, :64], w2_ref[...]) + b2_ref[...]
+        logit = dot(act.astype(BF)[:, :64], w2v[...]) + b2_ref[...]
         sig = 1.0 / (1.0 + jnp.exp(-logit))
         mask = dot(rmat[...], kx_ref[i]) * delta[...]
         sm = sig * mask
         sel = sm.astype(BF)
-        sel_ref[rows, :] = sel
-        der_ref[rows, :] = (sm * (1.0 - sig)).astype(BF)
-        lane = lax.broadcasted_iota(jnp.int32, (rb, LANES), 1)
-        aux_ref[rows, :] = jnp.where(lane < 64, pre, jnp.where(lane < 96, mean, rstd))
+        sel_ref[rr, :] = sel
+        der_ref[rr, :] = (sm * (1.0 - sig)).astype(BF)
+        ln = lax.broadcasted_iota(jnp.int32, (rb, LANES), 1)
+        aux_ref[rr, :] = jnp.where(ln < 64, pre, jnp.where(ln < 96, mean, rstd))
         part = dot_tn(sel, v)
 
         @pl.when(i % per == 0)
@@ -94,33 +336,97 @@
 
         @pl.when(i % per == per - 1)
         def _():
-            pool_ref[i // per] = (acc[...] * ((rb // frames * per) ** -0.5)).astype(BF)
-
-
-def patch_forward(v, w1aug, w1s, w2rep, b2rep, kx, groups, per):
+            pool[i // per] = (acc[...] * (count**-0.5)).astype(BF)
+
+    micros = tok_ref.shape[0]
+    out = []
+    for mi in range(micros):
+        for k in range(1, m):
+            j = lax.rem(me.map + k, m)
+            d = remote(
+                pool.at[mi * m + j, pl.ds(0, fm)], tok_ref.at[mi, me.map], tsend.at[mi * m + k], trecv.at[mi * m + k], (me.clip, j)
+            )
+            d.start()
+            out.append(d)
+        mine = pltpu.make_async_copy(pool.at[mi * m + me.map, pl.ds(0, fm)], tok_ref.at[mi, me.map], tsend.at[mi * m])
+        mine.start()
+        mine.wait()
+    for f in slots[blocks]:
+        f()
+    for k in range(1, n):
+        s = lax.rem(me.clip + n - k, n)
+        remote(pb_ref, pbg.at[s], psend.at[1, k], precv.at[1, k], me.core_dev).wait_recv()
+    wide = pb_ref.shape[1]
+    each = wide // shard
+    for q in range(width // wide):
+        t = pbg[q * each].astype(F32)
+        for s in range(q * each + 1, (q + 1) * each):
+            t = t + pbg[s].astype(F32)
+        vec_ref[:, q * wide : (q + 1) * wide] = t[0:8, :]
+    each = wide // fsh
+    for q in range(ff // wide):
+        t = pbg[q * each].astype(F32)
+        for s in range(q * each + 1, (q + 1) * each):
+            t = t + pbg[s].astype(F32)
+        fb_ref[:, q * wide : (q + 1) * wide] = t[8:9, :]
+    for mi in range(micros):
+        for k in range(1, m):
+            j = lax.rem(me.map + m - k, m)
+            remote(
+                pool.at[mi * m + j, pl.ds(0, fm)], tok_ref.at[mi, j], tsend.at[mi * m + k], trecv.at[mi * m + k], me.core_dev
+            ).wait_recv()
+    g.finish()
+    for d in small + out:
+        d.wait_send()
+
+
+STEP = 1.0
+AHEAD = 3
+
+
+def forward(n, m, v, kx, b2rep, pa, pb, wq, wo, w1, w2, micros, frames, per, count):
     rows, width = v.shape
     blocks = kx.shape[0]
     rb = rows // blocks
+    ff = w1.shape[1]
+    groups = blocks // per
+    copies = 6 * 11 * (n // 4)
+    sds = jax.ShapeDtypeStruct
     vm = pl.BlockSpec(memory_space=pltpu.VMEM)
+    hb = pl.BlockSpec(memory_space=pltpu.HBM)
+    dma = pltpu.SemaphoreType.DMA
     return pl.pallas_call(
-        functools.partial(patch_fwd_kernel, blocks, per, rb, width),
+        functools.partial(forward_kernel, n, m, blocks, per, count),
         out_shape=(
-            jax.ShapeDtypeStruct((groups, LANES, width), BF),
-            jax.ShapeDtypeStruct((rows, LANES), F32),
-            jax.ShapeDtypeStruct((rows, LANES), BF),
-            jax.ShapeDtypeStruct((rows, LANES), BF),
+            sds((8, width, width), BF),
+            sds((ff, width), BF),
+            sds((micros, m, frames * MAPS, width), BF),
+            sds((rows, LANES), F32),
+            sds((rows, LANES), BF),
+            sds((rows, LANES), BF),
+            sds((8, width), F32),
+            sds((1, ff), F32),
+            sds((LANES, width), BF),
+            sds((72, LANES), F32),
         ),
-        in_specs=[pl.BlockSpec(memory_space=pltpu.HBM)] + [vm] * 5,
-        out_specs=(vm,) * 4,
+        in_specs=[hb, vm, vm, vm, vm, hb, hb, hb, hb],
+        out_specs=(hb, hb, hb) + (vm,) * 7,
         scratch_shapes=[
             pltpu.VMEM((rows, width), BF),
             pltpu.VMEM((LANES, width), F32),
+            pltpu.VMEM((groups, LANES, width), BF),
             pltpu.VMEM((rb, kx.shape[1]), BF),
             pltpu.VMEM((rb, LANES), F32),
-            pltpu.SemaphoreType.DMA((blocks,)),
+            pltpu.VMEM((n,) + pa.shape, BF),
+            pltpu.VMEM((n,) + pb.shape, BF),
+            pltpu.VMEM((width, LANES), BF),
+            pltpu.VMEM((64, LANES), BF),
+            pltpu.VMEM((8, LANES), F32),
+            dma((blocks,)), dma((16,)), dma((copies,)), dma((copies,)), dma((2, n)), dma((2, n)),
+            dma((micros * m,)), dma((micros * m,)),
         ],
-        compiler_params=pltpu.CompilerParams(vmem_limit_bytes=VLIM),
-    )(v, w1aug, w1s, w2rep, b2rep, kx)
+        compiler_params=pltpu.CompilerParams(vmem_limit_bytes=VLIM, collective_id=0, has_side_effects=True),
+    )(v, kx, b2rep, pa, pb, wq, wo, w1, w2)
 
 
 def ln_stats(t):
@@ -131,12 +437,13 @@
 
 
 def token_kernel(
-    tok, cot, wq, wo, w1, w2, vec, b1,
-    out_ref, gq_ref, go_ref, g1_ref, g2_ref, gtok_ref, gvec_ref, gb1_ref,
+    tok, cot, wa, w2, vec, b1,
+    out_ref, ga_ref, g2_ref, gtok_ref, gvec_ref, gb1_ref,
     n1, joined, probs, att, mixed, n2, act, slope, gacc, gmix, gbr, gatt, gj, tr,
 ):
     n, d = tok.shape
-    ff = w1.shape[1]
+    ff = w2.shape[0]
+    per = d // 256
     seq = 256
     micros = n // seq
     pairs = d // LANES
@@ -169,7 +476,7 @@
         @pl.loop(0, d // cb)
         def _(j):
             o = pl.multiple_of(blk * d + j * cb, cb)
-            r = dot(n1[...], wq[:, pl.ds(o, cb)])
+            r = dot(n1[...], wa[blk, :, col(j * cb, cb)])
             if blk == 0:
                 r = r + vec[2:3, col(j * cb, cb)]
             if blk == 2:
@@ -206,7 +513,7 @@
     @pl.loop(0, d // cb)
     def _(j):
         c = col(j * cb, cb)
-        mixed[:, c] = tok[:, c].astype(F32) + (dot(att[...], wo[:, c]) + vec[4:5, c])
+        mixed[:, c] = tok[:, c].astype(F32) + (dot(att[...], wa[3, :, c]) + vec[4:5, c])
 
     @pl.loop(0, chunks)
     def _(i):
@@ -216,7 +523,7 @@
     @pl.loop(0, ff // cb)
     def _(j):
         c = col(j * cb, cb)
-        a, s = gelu_parts(dot(n2[...], w1[:, c]) + b1[0:1, c])
+        a, s = gelu_parts(dot(n2[...], wa[4 + j // per, :, col((j % per) * cb, cb)]) + b1[0:1, c])
         act[:, c] = a.astype(BF)
         slope[:, c] = s.astype(BF)
 
@@ -238,12 +545,15 @@
         g = (dot_nt(cot[...], w2[c, :]) * slope[:, c].astype(F32)).astype(BF)
         act[:, c] = g
         gb1_ref[0:1, c] = jnp.sum(g.astype(F32), axis=0, keepdims=True)
-        g1_ref[:, c] = dot(tr[...], g).astype(BF)
+        ga_ref[4 + j // per, :, col((j % per) * cb, cb)] = dot(tr[...], g).astype(BF)
 
     @pl.loop(0, d // cb)
     def _(j):
         c = col(j * cb, cb)
-        gacc[:, c] = dot_nt(act[...], w1[c, :])
+        total = jnp.zeros((n, cb), F32)
+        for q in range(ff // d):
+            total = total + dot_nt(act[:, q * d : (q + 1) * d], wa[4 + q, c, :])
+        gacc[:, c] = total
 
     @pl.loop(0, chunks)
     def _(i):
@@ -267,8 +577,8 @@
     @pl.loop(0, d // cb)
     def _(j):
         c = col(j * cb, cb)
-        go_ref[:, c] = dot(tr[...], gbr[:, c]).astype(BF)
-        gatt[:, c] = dot_nt(gbr[...], wo[c, :]).astype(BF)
+        ga_ref[3, :, c] = dot(tr[...], gbr[:, c]).astype(BF)
+        gatt[:, c] = dot_nt(gbr[...], wa[3, c, :]).astype(BF)
 
     @pl.loop(0, micros * pairs)
     def _(i):
@@ -298,12 +608,15 @@
     @pl.loop(0, 3 * d // cb)
     def _(j):
         c = col(j * cb, cb)
-        gq_ref[:, c] = dot(tr[...], gj[:, c]).astype(BF)
+        ga_ref[j // per, :, col((j % per) * cb, cb)] = dot(tr[...], gj[:, c]).astype(BF)
 
     @pl.loop(0, d // cb)
     def _(j):
         c = col(j * cb, cb)
-        gacc[:, c] = dot_nt(gj[...], wq[c, :])
+        total = jnp.zeros((n, cb), F32)
+        for q in range(3):
+            total = total + dot_nt(gj[:, q * d : (q + 1) * d], wa[q, c, :])
+        gacc[:, c] = total
 
     @pl.loop(0, chunks)
     def _(i):
@@ -319,20 +632,20 @@
         gtok_ref[r, :] = (gmix[r, :] + back * rstd).astype(BF)
 
 
-def token_layer(tok, cot, wq, wo, w1, w2, vec, b1):
+def token_layer(tok, cot, wa, w2, vec, b1):
     n, d = tok.shape
-    ff = w1.shape[1]
+    ff = w2.shape[0]
     vm = pl.BlockSpec(memory_space=pltpu.VMEM)
     sds = jax.ShapeDtypeStruct
     heads = (n // 256) * (d // HEAD)
     return pl.pallas_call(
         token_kernel,
         out_shape=(
-            sds((n, d), BF), sds((d, 3 * d), BF), sds((d, d), BF), sds((d, ff), BF), sds((ff, d), BF), sds((n, d), BF),
+            sds((n, d), BF), sds(wa.shape, BF), sds((ff, d), BF), sds((n, d), BF),
             sds((8, d), F32), sds((1, ff), F32),
         ),
-        in_specs=[vm] * 8,
-        out_specs=(vm,) * 8,
+        in_specs=[vm] * 6,
+        out_specs=(vm,) * 6,
         scratch_shapes=[
             pltpu.VMEM((n, d), BF),
             pltpu.VMEM((n, 3 * d), BF),
@@ -350,14 +663,193 @@
             pltpu.VMEM((d, n), BF),
         ],
         compiler_params=pltpu.CompilerParams(vmem_limit_bytes=VLIM),
-    )(tok, cot, wq, wo, w1, w2, vec, b1)
-
-
-def patch_bwd_kernel(
-    blocks, per, rb, width, v_ref, aux_hbm, sel_ref, der_hbm, gt_ref, w1s_ref, w2_ref,
-    co_hbm, x_ref, w2g_ref, row_ref,
-    vbuf, aux_ref, der_ref, co_ref, vsem, asem, dsem, csem,
+    )(tok, cot, wa, w2, vec, b1)
+
+
+class Reduce:
+    def __init__(self, place, chunks, own, rc, rx, ry, rz, rf, lsem, sends, recvs):
+        self.p, self.chunks, self.own, self.rc, self.rx, self.ry, self.rz, self.rf = place, chunks, own, rc, rx, ry, rz, rf
+        self.lsem, self.sends, self.recvs = lsem, sends, recvs
+
+    def sem(self, i, at):
+        j = i * 8 * self.p.na + at
+        return self.sends.at[j], self.recvs.at[j]
+
+    def send(self, i, at, src, dst, dev):
+        s, r = self.sem(i, at)
+        remote(src, dst, s, r, dev).start()
+
+    def grad(self, i, k, side, core):
+        p = self.p
+        ref, panels, rows, pitch, skip, _ = self.chunks[i]
+        s = p.shard(p.back(k), p.b if side == 0 else 1 - p.b, core)
+        return ref.at[panels, pl.ds(pl.multiple_of(s * pitch + skip, 8), rows)]
+
+    def cols(self, half):
+        w = self.chunks[0][0].shape[-1] // 2
+        return pl.ds(pl.multiple_of(half * w, LANES), w)
+
+    def mine(self):
+        return self.cols(self.p.half)
+
+    def other(self):
+        return self.cols(1 - self.p.half)
+
+    def core_copies(self, i):
+        p = self.p
+        return [
+            (2 * k + side, self.grad(i, k, side, 1 - p.c), self.rc[i].at[2 * k + side], p.core_dev)
+            for k in range(p.na) for side in range(2)
+        ]
+
+    def local_copies(self, i):
+        p = self.p
+        return [
+            pltpu.make_async_copy(self.grad(i, k, side, p.c), self.own[i].at[2 * k + side], self.lsem.at[i, 2 * k + side])
+            for k in range(p.na) for side in range(2)
+        ]
+
+    def x_copies(self, i):
+        p, base = self.p, 2 * self.p.na
+        sides = range(2) if self.chunks[i][5] else range(1)
+        return [
+            (base + 2 * k + side, self.own[i].at[2 * k + side, :, :, self.other()], self.rx[i].at[2 * (k - 1) + side], p.x_dev)
+            for k in range(1, p.na) for side in sides
+        ]
+
+    def y_copies(self, i):
+        p, base = self.p, 4 * self.p.na
+        out = []
+        for k in range(p.na):
+            src, dst = self.own[i].at[2 * k + 1], self.ry[i].at[k]
+            if self.chunks[i][5] and k:
+                src, dst = src.at[:, :, self.mine()], dst.at[:, :, self.mine()]
+            out.append((base + k, src, dst, p.y_dev))
+        return out
+
+    def z_copies(self, i):
+        p, base = self.p, 5 * self.p.na
+        return [
+            (base + k, self.own[i].at[2 * k, :, :, self.mine()], self.rz[i].at[k - 1], (p.shard(p.back(k), p.b, p.c), p.map))
+            for k in range(1, p.na)
+        ]
+
+    def last_copies(self, i):
+        return [(6 * self.p.na, self.own[i].at[0], self.rf[i], self.p.x_dev)]
+
+    def start(self, i, copies):
+        for at, src, dst, dev in copies:
+            self.send(i, at, src, dst, dev)
+
+    def wait(self, i, copies):
+        for at, src, dst, dev in copies:
+            s, r = self.sem(i, at)
+            remote(dst, dst, s, r, self.p.core_dev).wait_recv()
+
+    def add(self, ref, at, cols, inc):
+        a = ref[at, :, :, cols]
+        ref[at, :, :, cols] = (a.astype(F32) + inc.astype(F32)).astype(BF)
+
+    def stage0(self, i):
+        for c in self.local_copies(i):
+            c.start()
+        self.start(i, self.core_copies(i))
+
+    def stage1(self, i):
+        for c in self.local_copies(i):
+            c.wait()
+        self.wait(i, self.core_copies(i))
+
+        @pl.loop(0, 2 * self.p.na)
+        def _(j):
+            self.own[i][j] = (self.own[i][j].astype(F32) + self.rc[i][j].astype(F32)).astype(BF)
+
+        self.start(i, self.x_copies(i) if self.chunks[i][5] else self.y_copies(i))
+
+    def add_x(self, i):
+        self.wait(i, self.x_copies(i))
+        both = self.chunks[i][5]
+
+        @pl.loop(0, self.p.na - 1)
+        def _(k):
+            for side in range(2 if both else 1):
+                self.add(self.own[i], 2 * k + 2 + side, self.mine(), self.rx[i][2 * k + side])
+
+    def add_y(self, i):
+        self.wait(i, self.y_copies(i))
+        if not self.chunks[i][5]:
+
+            @pl.loop(0, self.p.na)
+            def _(k):
+                self.own[i][2 * k] = (self.own[i][2 * k].astype(F32) + self.ry[i][k].astype(F32)).astype(BF)
+
+            return
+        self.own[i][0] = (self.own[i][0].astype(F32) + self.ry[i][0].astype(F32)).astype(BF)
+
+        @pl.loop(1, self.p.na)
+        def _(k):
+            self.add(self.own[i], 2 * k, self.mine(), self.ry[i][k, :, :, self.mine()])
+
+    def stage2(self, i):
+        if self.chunks[i][5]:
+            self.add_x(i)
+            self.start(i, self.y_copies(i))
+        else:
+            self.add_y(i)
+            self.start(i, self.x_copies(i))
+
+    def stage3(self, i):
+        if self.chunks[i][5]:
+            self.add_y(i)
+        else:
+            self.add_x(i)
+        self.start(i, self.z_copies(i))
+
+    def stage4(self, i):
+        self.wait(i, self.z_copies(i))
+        c = self.mine()
+        t = self.own[i][0, :, :, c].astype(F32)
+        for k in range(self.p.na - 1):
+            t = t + self.rz[i][k].astype(F32)
+        self.own[i][0, :, :, c] = t.astype(BF)
+        self.start(i, self.last_copies(i))
+
+    def stage5(self, i, put):
+        self.wait(i, self.last_copies(i))
+        put(i, self.own[i][0].astype(F32) + self.rf[i][...].astype(F32))
+
+    def events(self, put):
+        call, n = functools.partial, len(self.chunks)
+        out = []
+        for t in range(n + 4):
+            for s in range(5, 0, -1):
+                i = t - (s - 1)
+                if 0 <= i < n:
+                    out.append(call(self.stage5, i, put) if s == 5 else call(getattr(self, "stage%d" % s), i))
+        return out
+
+    def finish(self):
+        for i in range(len(self.chunks)):
+            for c in (self.core_copies, self.x_copies, self.y_copies, self.z_copies, self.last_copies):
+                for at, src, dst, dev in c(i):
+                    s, r = self.sem(i, at)
+                    remote(src, src, s, r, self.p.core_dev).wait_send()
+
+
+def backward_kernel(
+    n, m, blocks, per, count, v_ref, aux_hbm, der_hbm, gtok_ref, ga_ref, gb_ref, w1s_ref, w2_ref, vecs_ref,
+    co_hbm, gt_ref, oa_ref, ob_ref, win_ref, tot_ref,
+    vbuf, aux_ref, der_ref, co_ref, gin, x_ref, w2g_ref, row_ref,
+    own_a, rc_a, rx_a, ry_a, rz_a, rf_a, own_b, rc_b, rx_b, ry_b, rz_b, rf_b,
+    ms, mc, mx, my, mz, md, tc, tx, ty, tz, td, te,
+    vsem, asem, dsem, csem, lsem, rsend, rrecv, tsend, trecv, ssend, srecv,
 ):
+    rows, width = v_ref.shape
+    rb = rows // blocks
+    me = Place(n, m)
+    shard, fsh = width // n, gb_ref.shape[1] // n
+    micros, _, fm, _ = gtok_ref.shape
+
     def copies(i):
         r = pl.ds(i * rb, rb)
         return (
@@ -370,6 +862,37 @@
         r = pl.ds(i * rb, rb)
         return pltpu.make_async_copy(co_ref.at[r], co_hbm.at[r], csem.at[i])
 
+    me.greet()
+    out = []
+    for mi in range(micros):
+        for k in range(1, m):
+            j = lax.rem(me.map + k, m)
+            d = remote(gtok_ref.at[mi, j], gin.at[mi, me.map], tsend.at[mi * m + k], trecv.at[mi * m + k], (me.clip, j))
+            d.start()
+            out.append(d)
+        out.append(pltpu.make_async_copy(gtok_ref.at[mi, me.map], gin.at[mi, me.map], tsend.at[mi * m]))
+        out[-1].start()
+
+    chunks = [(gb_ref, pl.ds(0, 1), fsh // 2, fsh, q * (fsh // 2), q == 0) for q in range(2)]
+    chunks += [(ga_ref, pl.ds(2 * q, 2), shard, shard, 0, q % 2 == 0) for q in (2, 3, 0, 1)]
+
+    def both(b, a):
+        return [b.at[0], b.at[1]] + [a.at[q] for q in range(4)]
+
+    red = Reduce(
+        me, chunks, both(own_b, own_a), both(rc_b, rc_a), both(rx_b, rx_a), both(ry_b, ry_a), both(rz_b, rz_a),
+        both(rf_b, rf_a), lsem, rsend, rrecv,
+    )
+    for i in range(6):
+        red.stage0(i)
+
+    def put_out(i, val):
+        if i < 2:
+            ob_ref[i * (fsh // 2) : (i + 1) * (fsh // 2), :] = val[0]
+        else:
+            q = (2, 3, 0, 1)[i - 2]
+            oa_ref[2 * q : 2 * q + 2] = val
+
     @pl.loop(0, blocks)
     def _(i):
         for c in copies(i):
@@ -380,17 +903,47 @@
     row_ref[...] = jnp.zeros(row_ref.shape, F32)
     lane = lax.broadcasted_iota(jnp.int32, (rb, LANES), 1)
 
+    todo = red.events(put_out)
+    slots = [[] for _ in range(blocks + 1)]
+    for at, f in enumerate(todo[2:]):
+        slots[min(int(at * RSTEP * blocks / len(todo)), blocks)].append(f)
+    todo[0]()
+    todo[1]()
+    for mi in range(micros):
+        for k in range(1, m):
+            j = lax.rem(me.map + m - k, m)
+            remote(gtok_ref.at[mi, j], gin.at[mi, j], tsend.at[mi * m + k], trecv.at[mi * m + k], me.core_dev).wait_recv()
+    for mi in range(micros):
+        for k in range(m):
+            d = out[mi * m + k]
+            if k < m - 1:
+                d.wait_send()
+            else:
+                d.wait()
+    gt_ref[...] = jnp.zeros(gt_ref.shape, BF)
+    for mi in range(micros):
+        for j in range(m):
+            gt_ref[mi * m + j, 0:fm, :] = (gin[mi, j].astype(F32) * count**-0.5).astype(BF)
+
     @pl.loop(0, blocks)
     def _(i):
-        rows = pl.ds(pl.multiple_of(i * rb, 16), rb)
+        for at, fs in enumerate(slots[:blocks]):
+            if fs:
+
+                @pl.when(i == at)
+                def _():
+                    for f in fs:
+                        f()
+
+        rr = pl.ds(pl.multiple_of(i * rb, 16), rb)
         for c in copies(i):
             c.wait()
-        v = vbuf[rows, :]
-        aux = aux_ref[rows, :]
+        v = vbuf[rr, :]
+        aux = aux_ref[rr, :]
         mean = aux[:, 64:65]
         rstd = aux[:, 127:128]
         g = dot_nt(v, gt_ref[i // per])
-        gl_f = g * der_ref[rows, :].astype(F32)
+        gl_f = g * der_ref[rr, :].astype(F32)
         gl = gl_f.astype(BF)
         ga = dot_nt(gl, w2_ref[...])
         pre = jnp.where(lane < 64, aux, 0.0)
@@ -411,33 +964,144 @@
         ex = jnp.where(lane < 64, uf, 0.0)
         for pos, val in enumerate((c1h, c1 - c1h, sh, s - sh, mh, mean - mh)):
             ex = jnp.where(lane == 64 + pos, val, ex)
-        co_ref[rows, :] = ex.astype(BF)
+        co_ref[rr, :] = ex.astype(BF)
         put(i).start()
+
+    shift = row_ref[...].T[0:64, 2:3]
+    ms[0:64, :] = (x_ref[...] - shift).astype(BF)
+    ms[64:96, :] = jnp.concatenate([vecs_ref[...], jnp.zeros((16, width), F32)], axis=0).astype(BF)
+    td[0:64, :] = w2g_ref[...]
+    td[64:72, :] = row_ref[...]
+    td[72:80, :] = jnp.zeros((8, LANES), F32)
+
+    def both_ways(at, dev, msrc, mdst, tsrc, tdst):
+        a = remote(msrc, mdst, ssend.at[0, at], srecv.at[0, at], dev)
+        b = remote(tsrc, tdst, ssend.at[1, at], srecv.at[1, at], dev)
+        a.start()
+        b.start()
+        return a, b
+
+    a, b = both_ways(0, me.core_dev, ms, mc, td, tc)
+    for f in slots[blocks]:
+        f()
+    a.wait()
+    b.wait()
+    ms[...] = (ms[...].astype(F32) + mc[...].astype(F32)).astype(BF)
+    td[...] += tc[...]
+    mr = pl.ds(pl.multiple_of(me.c * 48, 16), 48)
+    tr = pl.ds(pl.multiple_of(me.c * 40, 8), 40)
+    for at, dev, mb, tb in ((1, me.x_dev, mx, tx), (2, me.y_dev, my, ty)):
+        a, b = both_ways(at, dev, ms.at[mr], mb, td.at[tr], tb)
+        a.wait()
+        b.wait()
+        ms[mr, :] = (ms[mr, :].astype(F32) + mb[...].astype(F32)).astype(BF)
+        td[tr, :] += tb[...]
+
+    def window(z):
+        lo = jnp.minimum(z * (width // me.na) // LANES * LANES, width - 256)
+        return pl.ds(pl.multiple_of(lo, LANES), 256)
+
+    sent = []
+    for k in range(1, me.na):
+        z = me.back(k)
+        sent += both_ways(
+            2 + k, (me.shard(z, me.b, me.c), me.map), ms.at[mr, window(z)], mz.at[me.a], td.at[tr], tz.at[me.a]
+        )
+    mz[me.a] = ms[mr, window(me.a)]
+    tz[me.a] = td[tr, :]
+    for k in range(1, me.na):
+        z = me.ahead(k)
+        remote(mz.at[z], mz.at[z], ssend.at[0, 2 + k], srecv.at[0, 2 + k], me.core_dev).wait_recv()
+        remote(tz.at[z], tz.at[z], ssend.at[1, 2 + k], srecv.at[1, 2 + k], me.core_dev).wait_recv()
+    for d in sent:
+        d.wait_send()
+    t = mz[0].astype(F32)
+    s = tz[0]
+    for z in range(1, me.na):
+        t = t + mz[z].astype(F32)
+        s = s + tz[z]
+    md[mr, :] = t
+    td[tr, :] = s
+    a, b = both_ways(me.na + 2, me.core_dev, md.at[mr], md.at[mr], td.at[tr], te)
+    o = 1 - me.c
+    mo, to = pl.ds(pl.multiple_of(o * 48, 16), 48), pl.ds(pl.multiple_of(o * 40, 8), 40)
+    remote(md.at[mo], md.at[mo], ssend.at[0, me.na + 2], srecv.at[0, me.na + 2], me.core_dev).wait_recv()
+    b.wait()
+    a.wait_send()
+    td[to, :] = te[...]
+    win_ref[...] = md[...]
+    tot_ref[...] = td[...]
 
     @pl.loop(0, blocks)
     def _(i):
         put(i).wait()
 
-
-def patch_backward(v, aux, sel, der, gts, w1s, w2rep, blocks, per):
+    red.finish()
+
+
+RSTEP = 1.0
+
+
+def backward(n, m, v, aux, der, gtok, ga, gb, w1s, w2n, vecs, blocks, per, count):
     rows, width = v.shape
     rb = rows // blocks
+    na, shard, fsh = n // 4, width // n, gb.shape[1] // n
+    micros, _, fm, _ = gtok.shape
     vm = pl.BlockSpec(memory_space=pltpu.VMEM)
     hb = pl.BlockSpec(memory_space=pltpu.HBM)
     sds = jax.ShapeDtypeStruct
+    dma = pltpu.SemaphoreType.DMA
+    half = width // 2
+
+    def bufs(c, np, r):
+        return [
+            pltpu.VMEM((c, 2 * na, np, r, width), BF),
+            pltpu.VMEM((c, 2 * na, np, r, width), BF),
+            pltpu.VMEM((c, 2 * na - 2, np, r, half), BF),
+            pltpu.VMEM((c, na, np, r, width), BF),
+            pltpu.VMEM((c, na - 1, np, r, half), BF),
+            pltpu.VMEM((c, np, r, width), BF),
+        ]
+
     return pl.pallas_call(
-        functools.partial(patch_bwd_kernel, blocks, per, rb, width),
-        out_shape=(sds((rows, LANES), BF), sds((64, width), F32), sds((64, LANES), F32), sds((8, LANES), F32)),
-        in_specs=[hb, hb, hb, hb, vm, vm, vm],
-        out_specs=(hb, vm, vm, vm),
+        functools.partial(backward_kernel, n, m, blocks, per, count),
+        out_shape=(
+            sds((rows, LANES), BF), sds((micros * m, LANES, width), BF), sds((8, shard, width), F32),
+            sds((fsh, width), F32), sds((96, 256), F32), sds((80, LANES), F32),
+        ),
+        in_specs=[hb] * 6 + [vm] * 3,
+        out_specs=(hb,) + (vm,) * 5,
         scratch_shapes=[
             pltpu.VMEM((rows, width), BF),
             pltpu.VMEM((rows, LANES), F32),
             pltpu.VMEM((rows, LANES), BF),
             pltpu.VMEM((rows, LANES), BF),
-        ] + [pltpu.SemaphoreType.DMA((blocks,))] * 4,
-        compiler_params=pltpu.CompilerParams(vmem_limit_bytes=VLIM),
-    )(v, aux, sel, der, gts, w1s, w2rep)
+            pltpu.VMEM(gtok.shape, BF),
+            pltpu.VMEM((64, width), F32),
+            pltpu.VMEM((64, LANES), F32),
+            pltpu.VMEM((8, LANES), F32),
+        ]
+        + bufs(4, 2, shard)
+        + bufs(2, 1, fsh // 2)
+        + [
+            pltpu.VMEM((96, width), BF),
+            pltpu.VMEM((96, width), BF),
+            pltpu.VMEM((48, width), BF),
+            pltpu.VMEM((48, width), BF),
+            pltpu.VMEM((na, 48, 256), BF),
+            pltpu.VMEM((96, 256), F32),
+            pltpu.VMEM((80, LANES), F32),
+            pltpu.VMEM((40, LANES), F32),
+            pltpu.VMEM((40, LANES), F32),
+            pltpu.VMEM((na, 40, LANES), F32),
+            pltpu.VMEM((80, LANES), F32),
+            pltpu.VMEM((40, LANES), F32),
+        ]
+        + [dma((blocks,))] * 4
+        + [dma((6, 2 * na)), dma((6 * 8 * na,)), dma((6 * 8 * na,)), dma((micros * m,)), dma((micros * m,))]
+        + [dma((2, na + 3)), dma((2, na + 3))],
+        compiler_params=pltpu.CompilerParams(vmem_limit_bytes=VLIM, collective_id=1, has_side_effects=True),
+    )(v, aux, der, gtok, ga, gb, w1s, w2n, vecs)
 
 
 def patch_out_kernel(v_ref, sel_ref, co_ref, gt_ref, bt_ref, o_ref):
@@ -488,67 +1152,64 @@
     kx = jnp.transpose(keep, (0, 1, 3, 2)).reshape(blocks, pb, frames)
     kx = jnp.repeat(kx, MAPS, axis=2).astype(BF)
     kx = jnp.pad(kx, ((0, 0), (0, 4), (0, LANES - frames * MAPS)))
-    gather = functools.partial(lax.all_gather, axis_name="clip", tiled=True)
-    gain, bias, w1, b1, w2 = (gather(t).astype(F32) for t in (tl_gain, tl_bias, map_w1, map_b1, map_w2))
-    gw1 = (gain[:, None] * w1).astype(BF)
-    w1aug = jnp.concatenate([gw1, jnp.ones((width, 1), BF), jnp.zeros((width, 63), BF)], axis=1)
-    csum = jnp.sum(gw1.astype(F32), axis=0)
-    w1s = jnp.zeros((8, LANES), F32).at[0, :64].set(csum).at[1, :64].set(b1 + bias @ w1)
-    w2rep = jnp.tile(w2.astype(BF), (1, LANES // MAPS))
+    n, m = width // shard, group
     b2rep = jnp.tile(map_b2.astype(F32), LANES // MAPS)[None]
-    bt = jnp.concatenate([gw1.T, jnp.ones((2, width), BF), jnp.zeros((62, width), BF)], axis=0)
-    pool, aux, sel, der = patch_forward(v, w1aug, w1s, w2rep, b2rep, kx, groups, per)
-    pool = pool[:, : frames * MAPS].reshape(micros, group, frames * MAPS, width)
-    tok = lax.all_to_all(pool, "map", split_axis=1, concat_axis=2, tiled=True)
+    gains, biases, w1l = tl_gain.astype(F32)[:, None], tl_bias.astype(F32)[:, None], map_w1.astype(F32)
+    q2 = map_w2.shape[0]
+    par = -(-(shard + 1 + q2) // 16) * 16
+    pa = jnp.concatenate([gains * w1l, biases * w1l], axis=1).astype(BF)
+    b1row = lax.dynamic_update_slice(jnp.zeros((1, LANES), BF), map_b1[None], (0, me * q2))
+    pa = jnp.concatenate([pa, b1row, jnp.tile(map_w2, (1, LANES // MAPS)), jnp.zeros((par - shard - 1 - q2, LANES), BF)])
+    wide = width // 2
+    fsh = fc1_bias.shape[0]
+    vecs = jnp.stack([ln1_gain, ln1_bias, qv_bias[0], qv_bias[1], out_bias, ln2_gain, ln2_bias, fc2_bias])
+    pb = lax.dynamic_update_slice(jnp.zeros((16, wide), BF), vecs, (0, (me * shard) % wide))
+    pb = lax.dynamic_update_slice(pb, fc1_bias[None], (8, (me * fsh) % wide))
+    wa, wb, tok, aux, sel, der, vec, fb, bt, small = forward(
+        n, m, v, kx, b2rep, pa, pb, qkv_weight, out_weight, fc1_weight, fc2_weight, micros, frames, per, count
+    )
     tok = tok.reshape(-1, width)
-    vecs = jnp.stack([ln1_gain, ln1_bias, qv_bias[0], qv_bias[1], out_bias, ln2_gain, ln2_bias, fc2_bias])
-    vec = gather(vecs, axis=1).astype(F32)
-    fb = gather(fc1_bias).astype(F32)[None]
-    wq, wo, wf1, wf2 = (gather(t) for t in (qkv_weight, out_weight, fc1_weight, fc2_weight))
-    out, gq, go, g1, g2, gtok, gvec, gb1 = token_layer(tok, cotangent.reshape(tok.shape), wq, wo, wf1, wf2, vec, fb)
-    gts = lax.all_to_all(
-        gtok.reshape(micros, 1, -1, width), "map", split_axis=2, concat_axis=1, tiled=True
-    ).reshape(groups, frames * MAPS, width)
-    gts = (gts.astype(F32) * count**-0.5).astype(BF)
-    gts = jnp.pad(gts, ((0, 0), (0, LANES - frames * MAPS), (0, 0)))
-    w2n = jnp.pad(w2rep, ((0, 64), (0, 0)))
-    co, xt, w2g, row = patch_backward(v, aux, sel, der, gts, w1s, w2n, blocks, per)
+    w1s = small[0:8]
+    w2n = jnp.pad(small[8:72].astype(BF), ((0, 64), (0, 0)))
+    ff = wb.shape[0]
+    out, ga, gb, gtok, gvec, gb1 = token_layer(tok, cotangent.reshape(tok.shape), wa, wb, vec, fb)
+    vecs = jnp.concatenate([gvec, jnp.swapaxes(gb1.reshape(n, -1, shard), 0, 1).reshape(-1, width)])
+    vecs = jnp.pad(vecs, ((0, 16 - vecs.shape[0]), (0, 0)))
+    co, gts, oa, ob, win, tot = backward(
+        n, m, v, aux, der, gtok.reshape(micros, m, -1, width), ga, gb[None], w1s, w2n, vecs, blocks, per, count
+    )
     pg = patch_out(v, sel, co, gts, bt, blocks, per)
     pg = jnp.transpose(pg.reshape(micros, group, count, frames, width), (0, 1, 3, 2, 4))
-    x = (xt - row[2, :64][:, None]).T
-    w2g = jnp.sum(w2g.reshape(64, LANES // MAPS, MAPS), axis=1)
-    b2g = jnp.sum(row[0].reshape(LANES // MAPS, MAPS), axis=0)
-
-    def scatter(t, axis=0):
-        t = lax.psum_scatter(t.astype(BF), "clip", scatter_dimension=axis, tiled=True)
-        return lax.psum(t, "map").astype(F32)
-
-    xs = scatter(x)
-    gb = lax.psum(row[1, :64], ("clip", "map"))
-    b2g = lax.psum(b2g, ("clip", "map"))
-    gvec = scatter(gvec, 1)
-    gains, biases, w1l = tl_gain.astype(F32), tl_bias.astype(F32), map_w1.astype(F32)
-    n_map = shard * 64 // width
+    if m > 2:
+        oa, ob, win, tot = (lax.psum(t, "map") * 0.5 for t in (oa, ob, win, tot))
+    lo = jnp.minimum(me // 4 * (width // (n // 4)) // LANES * LANES, width - 256)
+    win = lax.dynamic_slice(win, (0, me * shard - lo), (96, shard))
+    xs = win[:64].T
+    gvec = win[64:72]
+    fgrad = win[72 : 72 + ff // width].reshape(-1)
+    gb = tot[65, :64]
+    b2g = jnp.sum(tot[64].reshape(LANES // MAPS, MAPS), axis=0)
+    w2g = lax.dynamic_slice(tot, (me * q2, 0), (q2, LANES)).reshape(q2, LANES // MAPS, MAPS).sum(axis=1)
     return (
         out.reshape(cotangent.shape),
         pg,
         jnp.sum(w1l * xs, axis=1),
         w1l @ gb,
-        gains[:, None] * xs + biases[:, None] * gb[None],
-        lax.dynamic_slice(gb, (me * n_map,), (n_map,)),
-        scatter(w2g),
+        gains * xs + biases * gb[None],
+        lax.dynamic_slice(gb, (me * q2,), (q2,)),
+        w2g,
         b2g,
         gvec[0],
         gvec[1],
-        scatter(gq),
+        jnp.concatenate([oa[0], oa[1], oa[2]], axis=1),
         gvec[2:4],
-        scatter(go),
+        oa[3],
         gvec[4],
         gvec[5],
         gvec[6],
-        scatter(g1),
-        scatter(gb1[0]),
-        scatter(g2),
+        jnp.concatenate([oa[4 + q] for q in range(ff // width)], axis=1),
+        fgrad,
+        ob,
         gvec[7],
     )
 

time: 787 us -> 423 us (0.54)
  waiting for transfers between devices: 308 us -> 0 us
  blocking collectives: 224 us -> 0 us
  Pallas kernels: 189 us -> 390 us
  between operations: 17.4 us -> 0.85 us
    reduce_scatter x4 -> x0, waiting for transfers between devices: 280 us -> none  [scatter(): lax.psum_scatter(t.astype(BF), 'clip', scatter_dimension=axis, tiled=True)]
    pallas_call x3, Pallas kernels: 161 us -> 361 us  [the longest x1 156 us: backward(): pl.pallas_call(functools.partial(backward_kernel, n, m, blocks, per, coun...]
    unnamed x2 -> x0, blocking collectives: 121 us -> none
    all_gather x3 -> x0, blocking collectives: 56 us -> none  [the longest x2 37.8 us: on_device(): gather(t).astype(F32)]
    psum x2 -> x0, blocking collectives: 46.3 us -> none  [the longest x1 37.2 us: on_device(): gb = lax.psum(row[1, :64], ('clip', 'map'))]
    all_gather x4 -> x0, waiting for transfers between devices: 11.8 us -> none  [on_device(): gather(t)]
    all_to_all x2 -> x0, waiting for transfers between devices: 10.6 us -> none  [the longest x1 10.6 us: on_device(): lax.all_to_all(gtok.reshape(micros, 1, -1, width), 'map', split_axis=2, c...]
    convert_element_type x14 -> x2, other arithmetic: 10.9 us -> 1.32 us  [the longest x1 0.67 us: on_device(): tl_gain.astype(F32)[:, None]]
  transfers between devices with their start and end apart: 13 -> 0, of which waited for: 6 -> 0; matrix products, arithmetic and copies ran while one was open for 4% -> 0% of each run, Pallas kernels for 14% -> 0%
where the time goes in v2:
time: 423 us; the launch traced here: 422 us
  Pallas kernels  390 us (92%)
  local copies, waits for them, and re-layouts  19.8 us (5%)
  other arithmetic  9.85 us (2%)
    pallas_call x1, Pallas kernels, backward(): pl.pallas_call(functools.partial(backward_kernel, n, m, blocks, per, coun...  156 us
    pallas_call x1, Pallas kernels, forward(): pl.pallas_call(functools.partial(forward_kernel, n, m, blocks, per, count...  127 us
    pallas_call x1, Pallas kernels, token_layer(): pl.pallas_call(token_kernel, out_shape=(sds((n, d), BF), sds(wa.shape, BF...  78.5 us
    pallas_call x1, Pallas kernels, patch_out(): pl.pallas_call(patch_out_kernel, grid=(blocks,), out_shape=jax.ShapeDtype...  28.3 us

profile of v2, /device:TPU:0, one launch (start us, length us, event | category | flops | bytes accessed | tf_op | source)
XLA Modules:
  0.0 421.7 jit_solution(11473979703600526732)
XLA Ops:
  0.7 0.8 stack.28
  2.6 0.8 dynamic_update_slice.9
  3.4 0.8 copy.70
  5.7 0.7 tile.7
  6.6 0.7 maximum_maximum_fusion.pa_ref
  7.3 0.8 convert_bitcast_fusion
  9.0 0.7 pad.12.kx_ref
  10.9 126.7 %shard_map.356 = (bf16[8,768,768]{2,1,0:T(8,128)(2,1)}, bf16[3072,768]{1,0:T(8,128)(2,1)}, bf16[2,2,128,768]{3,2,1,0:T(8,128)(2,1)}, f32[12544,128]{1,0:T(8,128)...) custom-call(bf16[12544,768]{1,0:T(8,128)(2,1)} %bitcast.73, ...), custom_call_target="tpu_custom_call" | custom-call | tf_op jit(solution)/shard_map/pallas_call | solution.py:398
  137.6 78.5 %shard_map.357 = (bf16[512,768]{1,0:T(8,128)(2,1)}, bf16[8,768,768]{2,1,0:T(8,128)(2,1)}, bf16[3072,768]{1,0:T(8,128)(2,1)}, bf16[512,768]{1,0:T(8,128)(2,1)}, f32[8,768]{1,0:T(8,128)}, /*index=5*/f32[1,3072]{1,0:T(1,128)}) custom-call(bf16[512,768]{1,0:T(8,128)(2,1)} %bitcast.79, bf16[512,768]{1,0:T(8,128)(2,1)} %bitcast.78, ...), custom_call_target="tpu_custom_call" | custom-call | tf_op jit(solution)/shard_map/pallas_call | solution.py:641
  216.7 1.4 reduce.7
  218.3 1.4 select_maximum_fusion.vecs_ref
  220.8 156.3 %shard_map.358 = (bf16[12544,128]{1,0:T(8,128)(2,1)}, bf16[4,128,768]{2,1,0:T(8,128)(2,1)}, f32[8,48,768]{2,1,0:T(8,128)}, f32[192,768]{1,0:T(8,128)}, f32[96,256]{1,0:T(8,128)}, /*index=5*/f32[80,128]{1,0:T(8,128)}) custom-call(bf16[12544,768]{1,0:T(8,128)(2,1)} %bitcast.74, f32[12544,128]{1,0:T(8,128)} %get-tuple-element.49.aux_hbm, ...), custom_call_target="tpu_custom_call" | custom-call | tf_op jit(solution)/shard_map/pallas_call | solution.py:1066
  377.1 2.1 slice_bitcast_fusion.3
  379.2 0.9 pad_maximum_fusion
  380.1 0.8 pad_maximum_fusion.1
  381.5 1.4 multiply_add_fusion
  383.0 0.7 copy.75
  383.7 28.3 %shard_map.359 = bf16[12544,768]{1,0:T(8,128)(2,1)} custom-call(bf16[12544,768]{1,0:T(8,128)(2,1)} %bitcast.75, bf16[12544,128]{1,0:T(8,128)(2,1)} %get-tuple-element.48.sel_ref, bf16[12544,128]{1,0:T(8,128)(2,1)} %get-tuple-element.57.co_ref, bf16[4,128,768]{2,1,0:T(8,128)(2,1)} %get-tuple-element.58.gt_ref, bf16[128,768]{1,0:T(8,128)(2,1)} %get-tuple-element.59.bt_ref), custom_call_target="tpu_custom_call" | custom-call | tf_op jit(solution)/shard_map/pallas_call | solution.py:1125
  412.0 1.5 dynamic-slice_bitcast_fusion.1
  413.5 0.8 dynamic-slice.8
  414.9 1.3 dynamic-slice.4
  418.2 0.7 slice_reduce_fusion
  419.6 1.3 convolution_bitcast_fusion
  420.9 0.8 copy.82
  (43 shorter events, 10.6 us)
Async XLA Ops:
  2.6 8.3 %copy-start.2 = (bf16[16,384]{1,0:T(8,128)(2,1)}, bf16[16,384]{1,0:T(8,128)(2,1)S(1)}, u32[]{:S(2)}) copy-start(bf16[16,384]{1,0:T(8,128)(2,1)S(1)} %dynamic_update_slice.11.pb_ref) | copy-start | bytes 36868
  137.6 82.0 %copy-start.3 = (f32[72,128]{1,0:T(8,128)S(1)}, f32[72,128]{1,0:T(8,128)}, u32[]{:S(2)}) copy-start(f32[72,128]{1,0:T(8,128)} %get-tuple-element.54) | copy-start | bytes 110596
  383.7 35.9 %copy-start.1 = (bf16[48,64]{1,0:T(8,128)(2,1)S(1)}, bf16[48,64]{1,0:T(8,128)(2,1)}, u32[]{:S(2)}) copy-start(bf16[48,64]{1,0:T(8,128)(2,1)} %param.25) | copy-start | bytes 18436
  383.7 37.2 %copy-start = (f32[192,768]{1,0:T(8,128)S(1)}, f32[192,768]{1,0:T(8,128)}, u32[]{:S(2)}) copy-start(f32[192,768]{1,0:T(8,128)} %get-tuple-element.202) | copy-start | bytes 1769476

commit v3 on v2

--- a/solution.py
+++ b/solution.py
@@ -81,8 +81,8 @@
 
 
 class Gather:
-    def __init__(self, place, chunks, sends, recvs):
-        self.p, self.chunks, self.sends, self.recvs = place, chunks, sends, recvs
+    def __init__(self, place, chunks, shards, sends, recvs):
+        self.p, self.chunks, self.shards, self.sends, self.recvs = place, chunks, shards, sends, recvs
         self.started = []
 
     def block(self, i, s, half):
@@ -91,10 +91,10 @@
         c = slice(None) if half is None else pl.ds(pl.multiple_of(half * (ref.shape[-1] // 2), LANES), ref.shape[-1] // 2)
         return ref.at[r, c] if panels is None else ref.at[panels, r, c]
 
-    def send(self, i, at, dev, s, half):
+    def send(self, i, at, dev, s, half, src=None):
         b = self.block(i, s, half)
         j = i * self.per() + at
-        remote(b, b, self.sends.at[j], self.recvs.at[j], dev).start()
+        remote(b if src is None else src, b, self.sends.at[j], self.recvs.at[j], dev).start()
         self.started.append((i, j, half is None))
 
     def wait(self, i, at, s, half):
@@ -121,11 +121,14 @@
         return 5 * self.p.na + e
 
     def own(self, i):
-        p = self.p
+        p, src = self.p, self.shards[i]
+        w = src.shape[-1] // 2
+        c = pl.ds(pl.multiple_of(p.half * w, LANES), w)
+        part = src.at[:, c] if len(src.shape) == 2 else src.at[:, :, c]
         for k in range(1, p.na):
-            self.send(i, self.at_z(k), (p.shard(p.ahead(k), p.b, p.c), p.map), p.clip, p.half)
-        self.send(i, self.at_y(0), p.y_dev, p.clip, None)
-        self.send(i, self.at_core(0), p.core_dev, p.clip, None)
+            self.send(i, self.at_z(k), (p.shard(p.ahead(k), p.b, p.c), p.map), p.clip, p.half, part)
+        self.send(i, self.at_y(0), p.y_dev, p.clip, None, src)
+        self.send(i, self.at_core(0), p.core_dev, p.clip, None, src)
 
     def by_x(self, i):
         return self.chunks[i][5]
@@ -198,9 +201,9 @@
 
 
 def forward_kernel(
-    n, m, blocks, per, count, v_ref, kx_ref, b2_ref, pa_ref, pb_ref, wq_ref, wo_ref, w1_ref, w2_ref,
-    wa_ref, wb_ref, tok_ref, aux_ref, sel_ref, der_ref, vec_ref, fb_ref, wt_ref, small_ref,
-    vbuf, acc, pool, rmat, delta, pag, pbg, w1v, w2v, ss, vsem, lsem, gsend, grecv, psend, precv, tsend, trecv,
+    n, m, blocks, per, count, v_ref, kx_ref, b2_ref, pa_ref, pb_ref, wq_ref, wo_ref, w1_ref,
+    wa_ref, tok_ref, aux_ref, sel_ref, der_ref, vec_ref, fb_ref, wt_ref, small_ref,
+    vbuf, acc, pool, rmat, delta, pag, pbg, w1v, w2v, ss, ws_ref, vsem, lsem, gsend, grecv, psend, precv, tsend, trecv,
 ):
     rows, width = v_ref.shape
     rb = rows // blocks
@@ -211,18 +214,28 @@
     ff = w1_ref.shape[1]
     fsh = ff // n
 
+    micros = tok_ref.shape[0]
+
+    def load(blk, i):
+        r = pl.ds(blk * rb, rb)
+        return pltpu.make_async_copy(v_ref.at[r], vbuf.at[r], vsem.at[i])
+
+    def token_copy(gi, mi, j, back=False):
+        dst = tok_ref.at[mi, j] if back else tok_ref.at[mi, me.map]
+        return remote(pool.at[mi * m + j, pl.ds(0, fm)], dst, tsend.at[gi], trecv.at[gi], (me.clip, j))
+
     @pl.loop(0, blocks)
     def _(i):
-        pltpu.make_async_copy(v_ref.at[pl.ds(i * rb, rb)], vbuf.at[pl.ds(i * rb, rb)], vsem.at[i]).start()
+        gi = i // per
+        load(((gi % micros) * m + lax.rem(me.map + 1 + gi // micros, m)) * per + i % per, i).start()
 
     own = pl.ds(pl.multiple_of(me.clip * shard, 8), shard)
-    local = []
-    for p in range(3):
-        local.append((wq_ref.at[:, pl.ds(p * width, width)], wa_ref.at[p, own]))
-    local.append((wo_ref, wa_ref.at[3, own]))
-    for p in range(ff // width):
-        local.append((w1_ref.at[:, pl.ds(p * width, width)], wa_ref.at[4 + p, own]))
-    local.append((w2_ref, wb_ref.at[pl.ds(pl.multiple_of(me.clip * fsh, 8), fsh)]))
+    for q in range(3):
+        ws_ref[q] = wq_ref[:, q * width : (q + 1) * width]
+    ws_ref[3] = wo_ref[...]
+    for q in range(ff // width):
+        ws_ref[4 + q] = w1_ref[:, q * width : (q + 1) * width]
+    local = [(ws_ref, wa_ref.at[:, own])]
     local.append((pa_ref, pag.at[me.clip]))
     local.append((pb_ref, pbg.at[me.clip]))
     local = [pltpu.make_async_copy(s, d, lsem.at[i]) for i, (s, d) in enumerate(local)]
@@ -234,11 +247,11 @@
         dev = (lax.rem(me.clip + k, n), me.map)
         small.append(remote(pa_ref, pag.at[me.clip], psend.at[0, k], precv.at[0, k], dev))
         small[-1].start()
-    for d in local:
+    for d in local[1:]:
         d.wait()
-    chunks = [(wa_ref, pl.ds(2 * q, 2), shard, shard, 0, True) for q in range(4)]
-    chunks += [(wb_ref, None, fsh // 2, fsh, q * (fsh // 2), q == 0) for q in range(2)]
-    g = Gather(me, chunks, gsend, grecv)
+    chunks = [(wa_ref, pl.ds(2 * q, 2), shard, shard, 0, q != 2) for q in range(4)]
+    shards = [ws_ref.at[pl.ds(2 * q, 2)] for q in range(4)]
+    g = Gather(me, chunks, shards, gsend, grecv)
     todo = g.events()
     slots = [[] for _ in range(blocks + 1)]
     for at, f in enumerate(todo[AHEAD:]):
@@ -303,8 +316,12 @@
                     for f in fs:
                         f()
 
-        rr = pl.ds(pl.multiple_of(i * rb, 16), rb)
-        pltpu.make_async_copy(v_ref.at[pl.ds(i * rb, rb)], vbuf.at[pl.ds(i * rb, rb)], vsem.at[i]).wait()
+        gi = i // per
+        j = lax.rem(me.map + 1 + gi // micros, m)
+        gr = (gi % micros) * m + j
+        blk = gr * per + i % per
+        rr = pl.ds(pl.multiple_of(blk * rb, 16), rb)
+        load(blk, i).wait()
         v = vbuf[rr, :]
         mm = dot(v, w1v[...])
         mean = mm[:, 64:65] * (1.0 / width)
@@ -317,7 +334,7 @@
         act, _ = gelu_parts(pre)
         logit = dot(act.astype(BF)[:, :64], w2v[...]) + b2_ref[...]
         sig = 1.0 / (1.0 + jnp.exp(-logit))
-        mask = dot(rmat[...], kx_ref[i]) * delta[...]
+        mask = dot(rmat[...], kx_ref[blk]) * delta[...]
         sm = sig * mask
         sel = sm.astype(BF)
         sel_ref[rr, :] = sel
@@ -336,19 +353,14 @@
 
         @pl.when(i % per == per - 1)
         def _():
-            pool[i // per] = (acc[...] * (count**-0.5)).astype(BF)
-
-    micros = tok_ref.shape[0]
-    out = []
+            pool[gr] = (acc[...] * (count**-0.5)).astype(BF)
+
+            @pl.when(gi < micros * (m - 1))
+            def _():
+                token_copy(gi, gi % micros, j).start()
+
     for mi in range(micros):
-        for k in range(1, m):
-            j = lax.rem(me.map + k, m)
-            d = remote(
-                pool.at[mi * m + j, pl.ds(0, fm)], tok_ref.at[mi, me.map], tsend.at[mi * m + k], trecv.at[mi * m + k], (me.clip, j)
-            )
-            d.start()
-            out.append(d)
-        mine = pltpu.make_async_copy(pool.at[mi * m + me.map, pl.ds(0, fm)], tok_ref.at[mi, me.map], tsend.at[mi * m])
+        mine = pltpu.make_async_copy(pool.at[mi * m + me.map, pl.ds(0, fm)], tok_ref.at[mi, me.map], lsem.at[8 + mi])
         mine.start()
         mine.wait()
     for f in slots[blocks]:
@@ -369,22 +381,21 @@
         for s in range(q * each + 1, (q + 1) * each):
             t = t + pbg[s].astype(F32)
         fb_ref[:, q * wide : (q + 1) * wide] = t[8:9, :]
-    for mi in range(micros):
-        for k in range(1, m):
-            j = lax.rem(me.map + m - k, m)
-            remote(
-                pool.at[mi * m + j, pl.ds(0, fm)], tok_ref.at[mi, j], tsend.at[mi * m + k], trecv.at[mi * m + k], me.core_dev
-            ).wait_recv()
+    for gi in range(micros * (m - 1)):
+        token_copy(gi, gi % micros, lax.rem(me.map + 1 + gi // micros, m)).wait_send()
+        k = 1 + gi // micros
+        token_copy(gi, gi % micros, lax.rem(me.map + m - k, m), True).wait_recv()
     g.finish()
-    for d in small + out:
+    for d in small:
         d.wait_send()
+    local[0].wait()
 
 
 STEP = 1.0
 AHEAD = 3
 
 
-def forward(n, m, v, kx, b2rep, pa, pb, wq, wo, w1, w2, micros, frames, per, count):
+def forward(n, m, v, kx, b2rep, pa, pb, wq, wo, w1, micros, frames, per, count):
     rows, width = v.shape
     blocks = kx.shape[0]
     rb = rows // blocks
@@ -399,7 +410,6 @@
         functools.partial(forward_kernel, n, m, blocks, per, count),
         out_shape=(
             sds((8, width, width), BF),
-            sds((ff, width), BF),
             sds((micros, m, frames * MAPS, width), BF),
             sds((rows, LANES), F32),
             sds((rows, LANES), BF),
@@ -409,8 +419,8 @@
             sds((LANES, width), BF),
             sds((72, LANES), F32),
         ),
-        in_specs=[hb, vm, vm, vm, vm, hb, hb, hb, hb],
-        out_specs=(hb, hb, hb) + (vm,) * 7,
+        in_specs=[hb] + [vm] * 7,
+        out_specs=(hb, hb) + (vm,) * 7,
         scratch_shapes=[
             pltpu.VMEM((rows, width), BF),
             pltpu.VMEM((LANES, width), F32),
@@ -422,11 +432,12 @@
             pltpu.VMEM((width, LANES), BF),
             pltpu.VMEM((64, LANES), BF),
             pltpu.VMEM((8, LANES), F32),
+            pltpu.VMEM((8, width // n, width), BF),
             dma((blocks,)), dma((16,)), dma((copies,)), dma((copies,)), dma((2, n)), dma((2, n)),
             dma((micros * m,)), dma((micros * m,)),
         ],
         compiler_params=pltpu.CompilerParams(vmem_limit_bytes=VLIM, collective_id=0, has_side_effects=True),
-    )(v, kx, b2rep, pa, pb, wq, wo, w1, w2)
+    )(v, kx, b2rep, pa, pb, wq, wo, w1)
 
 
 def ln_stats(t):
@@ -437,12 +448,14 @@
 
 
 def token_kernel(
-    tok, cot, wa, w2, vec, b1,
-    out_ref, ga_ref, g2_ref, gtok_ref, gvec_ref, gb1_ref,
-    n1, joined, probs, att, mixed, n2, act, slope, gacc, gmix, gbr, gatt, gj, tr,
+    places, m, tok, cot, wa_hbm, w2s, vec, b1,
+    out_ref, ga_hbm, gtok_ref, gvec_ref, gb1_ref, ob_ref,
+    n1, joined, probs, att, mixed, n2, act, slope, gacc, gbr, tr, wa, w2, ga_ref, g2_ref,
+    own_b, rc_b, rx_b, ry_b, rz_b, rf_b, wsem, osem, lsem, gsend, grecv, rsend, rrecv,
 ):
     n, d = tok.shape
-    ff = w2.shape[0]
+    ff = g2_ref.shape[1]
+    fsh = ff // places
     per = d // 256
     seq = 256
     micros = n // seq
@@ -452,6 +465,51 @@
     chunks = n // ch
     lane = lax.broadcasted_iota(jnp.int32, (1, LANES), 1)
     first = lane < HEAD
+    me = Place(places, m)
+
+    def panel(q):
+        return pltpu.make_async_copy(wa_hbm.at[q], wa.at[q], wsem.at[q])
+
+    def panel_out(q):
+        return pltpu.make_async_copy(ga_ref.at[q], ga_hbm.at[q], osem.at[q])
+
+    for q in range(8):
+        panel(q).start()
+    own = pltpu.make_async_copy(w2s, w2.at[pl.ds(pl.multiple_of(me.clip * fsh, 8), fsh)], wsem.at[8])
+    own.start()
+    me.greet()
+    g = Gather(
+        me,
+        [(w2, None, fsh // 2, fsh, q * (fsh // 2), q == 0) for q in range(2)],
+        [w2s.at[pl.ds(q * (fsh // 2), fsh // 2)] for q in range(2)],
+        gsend,
+        grecv,
+    )
+    g.own(0)
+    g.own(1)
+    todo = [f for f in g.events() if f.func.__name__ != "own"]
+    early = [[] for _ in range(9 + micros * pairs + ff // cb)]
+    for at, f in enumerate(todo):
+        early[at * len(early) // len(todo)].append(f)
+
+    red = Reduce(
+        me, [(g2_ref, pl.ds(0, 1), fsh // 2, fsh, q * (fsh // 2), q == 0) for q in range(2)],
+        *([t.at[0], t.at[1]] for t in (own_b, rc_b, rx_b, ry_b, rz_b, rf_b)), lsem, rsend, rrecv,
+    )
+
+    def put_out(i, val):
+        ob_ref[i * (fsh // 2) : (i + 1) * (fsh // 2), :] = val[0]
+
+    steps = red.events(put_out)
+
+    def at_step(i, slots):
+        for at, fs in enumerate(slots):
+            if fs:
+
+                @pl.when(i == at)
+                def _():
+                    for f in fs:
+                        f()
 
     def rows_of(i):
         return pl.ds(pl.multiple_of(i * ch, ch), ch)
@@ -473,8 +531,11 @@
         n1[rows_of(i), :] = (xh * vec[0:1, :] + vec[1:2, :]).astype(BF)
 
     for blk in range(3):
+        panel(blk).wait()
+
         @pl.loop(0, d // cb)
         def _(j):
+            at_step(j, early[3 * blk : 3 * blk + 3])
             o = pl.multiple_of(blk * d + j * cb, cb)
             r = dot(n1[...], wa[blk, :, col(j * cb, cb)])
             if blk == 0:
@@ -497,6 +558,7 @@
 
     @pl.loop(0, micros * pairs)
     def _(i):
+        at_step(i, early[9 : 9 + micros * pairs])
         q = (heads_of(joined, i, 0).astype(F32) * (HEAD**-0.5)).astype(BF)
         k = heads_of(joined, i, d)
         v = heads_of(joined, i, 2 * d)
@@ -506,9 +568,13 @@
             s = dot_nt(jnp.where(mine, q, zero), k)
             ex = jnp.exp(s - jnp.max(s, axis=-1, keepdims=True))
             p = ex / jnp.sum(ex, axis=-1, keepdims=True)
-            probs[i * 2 + e] = p
-            total = total + dot(p.astype(BF), jnp.where(mine, v, zero))
+            low = p.astype(BF)
+            probs[i * 2 + e] = low
+            total = total + dot(low, jnp.where(mine, v, zero))
         put_heads(att, i, 0, total.astype(BF))
+
+    for q in range(3, 8):
+        panel(q).wait()
 
     @pl.loop(0, d // cb)
     def _(j):
@@ -522,6 +588,7 @@
 
     @pl.loop(0, ff // cb)
     def _(j):
+        at_step(j, early[9 + micros * pairs :])
         c = col(j * cb, cb)
         a, s = gelu_parts(dot(n2[...], wa[4 + j // per, :, col((j % per) * cb, cb)]) + b1[0:1, c])
         act[:, c] = a.astype(BF)
@@ -530,7 +597,12 @@
     @pl.loop(0, ff // cb)
     def _(j):
         c = col(j * cb, cb)
-        g2_ref[c, :] = dot_tn(act[:, c], cot[...]).astype(BF)
+        g2_ref[0, c, :] = dot_tn(act[:, c], cot[...]).astype(BF)
+
+    red.stage0(0)
+    red.stage0(1)
+    g.finish()
+    own.wait()
 
     @pl.loop(0, d // cb)
     def _(j):
@@ -538,6 +610,8 @@
         out_ref[:, c] = (mixed[:, c] + (dot(act[...], w2[:, c]) + vec[7:8, c])).astype(BF)
 
     transpose_into(n2)
+    for f in steps[:2]:
+        f()
 
     @pl.loop(0, ff // cb)
     def _(j):
@@ -547,6 +621,9 @@
         gb1_ref[0:1, c] = jnp.sum(g.astype(F32), axis=0, keepdims=True)
         ga_ref[4 + j // per, :, col((j % per) * cb, cb)] = dot(tr[...], g).astype(BF)
 
+    for q in range(4, 8):
+        panel_out(q).start()
+
     @pl.loop(0, d // cb)
     def _(j):
         c = col(j * cb, cb)
@@ -554,6 +631,9 @@
         for q in range(ff // d):
             total = total + dot_nt(act[:, q * d : (q + 1) * d], wa[4 + q, c, :])
         gacc[:, c] = total
+
+    for f in steps[2:4]:
+        f()
 
     @pl.loop(0, chunks)
     def _(i):
@@ -566,7 +646,7 @@
         back = eg - jnp.mean(eg, axis=-1, keepdims=True) - xh * jnp.mean(eg * xh, axis=-1, keepdims=True)
         c = cot[r, :].astype(F32)
         g = c + back * rstd
-        gmix[r, :] = g
+        mixed[r, :] = g
         low = g.astype(BF)
         gbr[r, :] = low
         add_row(4, low.astype(F32))
@@ -578,44 +658,55 @@
     def _(j):
         c = col(j * cb, cb)
         ga_ref[3, :, c] = dot(tr[...], gbr[:, c]).astype(BF)
-        gatt[:, c] = dot_nt(gbr[...], wa[3, c, :]).astype(BF)
+        att[:, c] = dot_nt(gbr[...], wa[3, c, :]).astype(BF)
+
+    panel_out(3).start()
+    late = [[] for _ in range(micros * pairs)]
+    late[len(late) // 4] = steps[4:6]
 
     @pl.loop(0, micros * pairs)
     def _(i):
+        at_step(i, late)
         q = (heads_of(joined, i, 0).astype(F32) * (HEAD**-0.5)).astype(BF)
         k = heads_of(joined, i, d)
         v = heads_of(joined, i, 2 * d)
-        ga = heads_of(gatt, i, 0)
+        ga = heads_of(att, i, 0)
         gq = jnp.zeros((seq, LANES), F32)
         gk = jnp.zeros((seq, LANES), F32)
         gv = jnp.zeros((seq, LANES), F32)
         for e in range(2):
             mine = first if e == 0 else jnp.logical_not(first)
-            p = probs[i * 2 + e]
+            low = probs[i * 2 + e]
+            p = low.astype(F32)
             ga_e = jnp.where(mine, ga, zero)
             gp = dot_nt(ga_e, v)
             pg = p * gp
             gs = (pg - p * jnp.sum(pg, axis=-1, keepdims=True)).astype(BF)
-            gv = gv + dot_tn(p.astype(BF), ga_e)
+            gv = gv + dot_tn(low, ga_e)
             gq = gq + dot(gs, jnp.where(mine, k, zero))
             gk = gk + dot_tn(gs, jnp.where(mine, q, zero))
-        put_heads(gj, i, 0, (gq * (HEAD**-0.5)).astype(BF))
-        put_heads(gj, i, d, gk.astype(BF))
-        put_heads(gj, i, 2 * d, gv.astype(BF))
+        put_heads(joined, i, 0, (gq * (HEAD**-0.5)).astype(BF))
+        put_heads(joined, i, d, gk.astype(BF))
+        put_heads(joined, i, 2 * d, gv.astype(BF))
 
     transpose_into(n1)
+    for f in steps[6:8]:
+        f()
 
     @pl.loop(0, 3 * d // cb)
     def _(j):
         c = col(j * cb, cb)
-        ga_ref[j // per, :, col((j % per) * cb, cb)] = dot(tr[...], gj[:, c]).astype(BF)
+        ga_ref[j // per, :, col((j % per) * cb, cb)] = dot(tr[...], joined[:, c]).astype(BF)
+
+    for q in range(3):
+        panel_out(q).start()
 
     @pl.loop(0, d // cb)
     def _(j):
         c = col(j * cb, cb)
         total = jnp.zeros((n, cb), F32)
         for q in range(3):
-            total = total + dot_nt(gj[:, q * d : (q + 1) * d], wa[q, c, :])
+            total = total + dot_nt(joined[:, q * d : (q + 1) * d], wa[q, c, :])
         gacc[:, c] = total
 
     @pl.loop(0, chunks)
@@ -625,45 +716,68 @@
         e = gacc[r, :]
         add_row(0, e * xh)
         add_row(1, e)
-        add_row(2, gj[r, 0:d].astype(F32))
-        add_row(3, gj[r, 2 * d : 3 * d].astype(F32))
+        add_row(2, joined[r, 0:d].astype(F32))
+        add_row(3, joined[r, 2 * d : 3 * d].astype(F32))
         eg = e * vec[0:1, :]
         back = eg - jnp.mean(eg, axis=-1, keepdims=True) - xh * jnp.mean(eg * xh, axis=-1, keepdims=True)
-        gtok_ref[r, :] = (gmix[r, :] + back * rstd).astype(BF)
-
-
-def token_layer(tok, cot, wa, w2, vec, b1):
+        gtok_ref[r, :] = (mixed[r, :] + back * rstd).astype(BF)
+
+    for f in steps[8:]:
+        f()
+    for q in range(8):
+        panel_out(q).wait()
+    red.finish()
+
+
+def token_layer(places, m, tok, cot, wa, w2s, vec, b1):
     n, d = tok.shape
-    ff = w2.shape[0]
+    fsh = w2s.shape[0]
+    ff = places * fsh
     vm = pl.BlockSpec(memory_space=pltpu.VMEM)
+    hb = pl.BlockSpec(memory_space=pltpu.HBM)
     sds = jax.ShapeDtypeStruct
     heads = (n // 256) * (d // HEAD)
+    na = places // 4
+    dma = pltpu.SemaphoreType.DMA
     return pl.pallas_call(
-        token_kernel,
+        functools.partial(token_kernel, places, m),
         out_shape=(
-            sds((n, d), BF), sds(wa.shape, BF), sds((ff, d), BF), sds((n, d), BF),
-            sds((8, d), F32), sds((1, ff), F32),
+            sds((n, d), BF), sds(wa.shape, BF), sds((n, d), BF), sds((8, d), F32), sds((1, ff), F32), sds((fsh, d), F32),
         ),
-        in_specs=[vm] * 6,
-        out_specs=(vm,) * 6,
+        in_specs=[vm, vm, hb, vm, vm, vm],
+        out_specs=(vm, hb, vm, vm, vm, vm),
         scratch_shapes=[
             pltpu.VMEM((n, d), BF),
             pltpu.VMEM((n, 3 * d), BF),
-            pltpu.VMEM((heads, 256, 256), F32),
+            pltpu.VMEM((heads, 256, 256), BF),
             pltpu.VMEM((n, d), BF),
             pltpu.VMEM((n, d), F32),
             pltpu.VMEM((n, d), BF),
             pltpu.VMEM((n, ff), BF),
             pltpu.VMEM((n, ff), BF),
             pltpu.VMEM((n, d), F32),
-            pltpu.VMEM((n, d), F32),
             pltpu.VMEM((n, d), BF),
-            pltpu.VMEM((n, d), BF),
-            pltpu.VMEM((n, 3 * d), BF),
             pltpu.VMEM((d, n), BF),
-        ],
-        compiler_params=pltpu.CompilerParams(vmem_limit_bytes=VLIM),
-    )(tok, cot, wa, w2, vec, b1)
+            pltpu.VMEM(wa.shape, BF),
+            pltpu.VMEM((ff, d), BF),
+            pltpu.VMEM(wa.shape, BF),
+            pltpu.VMEM((1, ff, d), BF),
+        ]
+        + reduce_buffers(na, 2, 1, fsh // 2, d)
+        + [dma((9,)), dma((8,)), dma((2, 2 * na)), dma((22 * na,)), dma((22 * na,)), dma((16 * na,)), dma((16 * na,))],
+        compiler_params=pltpu.CompilerParams(vmem_limit_bytes=VLIM, collective_id=2, has_side_effects=True),
+    )(tok, cot, wa, w2s, vec, b1)
+
+
+def reduce_buffers(na, chunks, panels, rows, width):
+    return [
+        pltpu.VMEM((chunks, 2 * na, panels, rows, width), BF),
+        pltpu.VMEM((chunks, 2 * na, panels, rows, width), BF),
+        pltpu.VMEM((chunks, 2 * na - 2, panels, rows, width // 2), BF),
+        pltpu.VMEM((chunks, na, panels, rows, width), BF),
+        pltpu.VMEM((chunks, na - 1, panels, rows, width // 2), BF),
+        pltpu.VMEM((chunks, panels, rows, width), BF),
+    ]
 
 
 class Reduce:
@@ -821,11 +935,11 @@
     def events(self, put):
         call, n = functools.partial, len(self.chunks)
         out = []
-        for t in range(n + 4):
+        for t in range(n // 2 + 4):
             for s in range(5, 0, -1):
-                i = t - (s - 1)
-                if 0 <= i < n:
-                    out.append(call(self.stage5, i, put) if s == 5 else call(getattr(self, "stage%d" % s), i))
+                for i in (2 * (t - s + 1), 2 * (t - s + 1) + 1):
+                    if 0 <= i < n:
+                        out.append(call(self.stage5, i, put) if s == 5 else call(getattr(self, "stage%d" % s), i))
         return out
 
     def finish(self):
@@ -837,17 +951,17 @@
 
 
 def backward_kernel(
-    n, m, blocks, per, count, v_ref, aux_hbm, der_hbm, gtok_ref, ga_ref, gb_ref, w1s_ref, w2_ref, vecs_ref,
-    co_hbm, gt_ref, oa_ref, ob_ref, win_ref, tot_ref,
+    n, m, blocks, per, count, v_ref, aux_hbm, der_hbm, gtok_ref, ga_ref, w1s_ref, w2_ref, vecs_ref,
+    co_hbm, gt_ref, oa_ref, win_ref, tot_ref,
     vbuf, aux_ref, der_ref, co_ref, gin, x_ref, w2g_ref, row_ref,
-    own_a, rc_a, rx_a, ry_a, rz_a, rf_a, own_b, rc_b, rx_b, ry_b, rz_b, rf_b,
+    own_a, rc_a, rx_a, ry_a, rz_a, rf_a,
     ms, mc, mx, my, mz, md, tc, tx, ty, tz, td, te,
     vsem, asem, dsem, csem, lsem, rsend, rrecv, tsend, trecv, ssend, srecv,
 ):
     rows, width = v_ref.shape
     rb = rows // blocks
     me = Place(n, m)
-    shard, fsh = width // n, gb_ref.shape[1] // n
+    shard = width // n
     micros, _, fm, _ = gtok_ref.shape
 
     def copies(i):
@@ -873,25 +987,16 @@
         out.append(pltpu.make_async_copy(gtok_ref.at[mi, me.map], gin.at[mi, me.map], tsend.at[mi * m]))
         out[-1].start()
 
-    chunks = [(gb_ref, pl.ds(0, 1), fsh // 2, fsh, q * (fsh // 2), q == 0) for q in range(2)]
-    chunks += [(ga_ref, pl.ds(2 * q, 2), shard, shard, 0, q % 2 == 0) for q in (2, 3, 0, 1)]
-
-    def both(b, a):
-        return [b.at[0], b.at[1]] + [a.at[q] for q in range(4)]
-
+    order = (2, 3, 0, 1)
+    chunks = [(ga_ref, pl.ds(2 * q, 2), shard, shard, 0, q % 2 == 0) for q in order]
     red = Reduce(
-        me, chunks, both(own_b, own_a), both(rc_b, rc_a), both(rx_b, rx_a), both(ry_b, ry_a), both(rz_b, rz_a),
-        both(rf_b, rf_a), lsem, rsend, rrecv,
+        me, chunks, *([t.at[q] for q in range(4)] for t in (own_a, rc_a, rx_a, ry_a, rz_a, rf_a)), lsem, rsend, rrecv
     )
-    for i in range(6):
+    for i in range(4):
         red.stage0(i)
 
     def put_out(i, val):
-        if i < 2:
-            ob_ref[i * (fsh // 2) : (i + 1) * (fsh // 2), :] = val[0]
-        else:
-            q = (2, 3, 0, 1)[i - 2]
-            oa_ref[2 * q : 2 * q + 2] = val
+        oa_ref[2 * order[i] : 2 * order[i] + 2] = val
 
     @pl.loop(0, blocks)
     def _(i):
@@ -1039,38 +1144,27 @@
     red.finish()
 
 
-RSTEP = 1.0
-
-
-def backward(n, m, v, aux, der, gtok, ga, gb, w1s, w2n, vecs, blocks, per, count):
+RSTEP = 1.6
+
+
+def backward(n, m, v, aux, der, gtok, ga, w1s, w2n, vecs, blocks, per, count):
     rows, width = v.shape
     rb = rows // blocks
-    na, shard, fsh = n // 4, width // n, gb.shape[1] // n
+    na, shard = n // 4, width // n
     micros, _, fm, _ = gtok.shape
     vm = pl.BlockSpec(memory_space=pltpu.VMEM)
     hb = pl.BlockSpec(memory_space=pltpu.HBM)
     sds = jax.ShapeDtypeStruct
     dma = pltpu.SemaphoreType.DMA
-    half = width // 2
-
-    def bufs(c, np, r):
-        return [
-            pltpu.VMEM((c, 2 * na, np, r, width), BF),
-            pltpu.VMEM((c, 2 * na, np, r, width), BF),
-            pltpu.VMEM((c, 2 * na - 2, np, r, half), BF),
-            pltpu.VMEM((c, na, np, r, width), BF),
-            pltpu.VMEM((c, na - 1, np, r, half), BF),
-            pltpu.VMEM((c, np, r, width), BF),
-        ]
 
     return pl.pallas_call(
         functools.partial(backward_kernel, n, m, blocks, per, count),
         out_shape=(
             sds((rows, LANES), BF), sds((micros * m, LANES, width), BF), sds((8, shard, width), F32),
-            sds((fsh, width), F32), sds((96, 256), F32), sds((80, LANES), F32),
+            sds((96, 256), F32), sds((80, LANES), F32),
         ),
-        in_specs=[hb] * 6 + [vm] * 3,
-        out_specs=(hb,) + (vm,) * 5,
+        in_specs=[hb] * 5 + [vm] * 3,
+        out_specs=(hb,) + (vm,) * 4,
         scratch_shapes=[
             pltpu.VMEM((rows, width), BF),
             pltpu.VMEM((rows, LANES), F32),
@@ -1081,8 +1175,7 @@
             pltpu.VMEM((64, LANES), F32),
             pltpu.VMEM((8, LANES), F32),
         ]
-        + bufs(4, 2, shard)
-        + bufs(2, 1, fsh // 2)
+        + reduce_buffers(na, 4, 2, shard, width)
         + [
             pltpu.VMEM((96, width), BF),
             pltpu.VMEM((96, width), BF),
@@ -1101,7 +1194,7 @@
         + [dma((6, 2 * na)), dma((6 * 8 * na,)), dma((6 * 8 * na,)), dma((micros * m,)), dma((micros * m,))]
         + [dma((2, na + 3)), dma((2, na + 3))],
         compiler_params=pltpu.CompilerParams(vmem_limit_bytes=VLIM, collective_id=1, has_side_effects=True),
-    )(v, aux, der, gtok, ga, gb, w1s, w2n, vecs)
+    )(v, aux, der, gtok, ga, w1s, w2n, vecs)
 
 
 def patch_out_kernel(v_ref, sel_ref, co_ref, gt_ref, bt_ref, o_ref):
@@ -1165,18 +1258,20 @@
     vecs = jnp.stack([ln1_gain, ln1_bias, qv_bias[0], qv_bias[1], out_bias, ln2_gain, ln2_bias, fc2_bias])
     pb = lax.dynamic_update_slice(jnp.zeros((16, wide), BF), vecs, (0, (me * shard) % wide))
     pb = lax.dynamic_update_slice(pb, fc1_bias[None], (8, (me * fsh) % wide))
-    wa, wb, tok, aux, sel, der, vec, fb, bt, small = forward(
-        n, m, v, kx, b2rep, pa, pb, qkv_weight, out_weight, fc1_weight, fc2_weight, micros, frames, per, count
+    wa, tok, aux, sel, der, vec, fb, bt, small = forward(
+        n, m, v, kx, b2rep, pa, pb, qkv_weight, out_weight, fc1_weight, micros, frames, per, count
     )
     tok = tok.reshape(-1, width)
     w1s = small[0:8]
     w2n = jnp.pad(small[8:72].astype(BF), ((0, 64), (0, 0)))
-    ff = wb.shape[0]
-    out, ga, gb, gtok, gvec, gb1 = token_layer(tok, cotangent.reshape(tok.shape), wa, wb, vec, fb)
+    ff = fc1_weight.shape[1]
+    out, ga, gtok, gvec, gb1, ob = token_layer(
+        n, m, tok, cotangent.reshape(tok.shape), wa, fc2_weight, vec, fb
+    )
     vecs = jnp.concatenate([gvec, jnp.swapaxes(gb1.reshape(n, -1, shard), 0, 1).reshape(-1, width)])
     vecs = jnp.pad(vecs, ((0, 16 - vecs.shape[0]), (0, 0)))
-    co, gts, oa, ob, win, tot = backward(
-        n, m, v, aux, der, gtok.reshape(micros, m, -1, width), ga, gb[None], w1s, w2n, vecs, blocks, per, count
+    co, gts, oa, win, tot = backward(
+        n, m, v, aux, der, gtok.reshape(micros, m, -1, width), ga, w1s, w2n, vecs, blocks, per, count
     )
     pg = patch_out(v, sel, co, gts, bt, blocks, per)
     pg = jnp.transpose(pg.reshape(micros, group, count, frames, width), (0, 1, 3, 2, 4))

time: 423 us -> 361 us (0.85)
  Pallas kernels: 390 us -> 326 us
    pallas_call x1, Pallas kernels: 156 us -> 93.2 us  [backward(): pl.pallas_call(functools.partial(backward_kernel, n, m, blocks, per, coun...]
    pallas_call x1, Pallas kernels: 127 us -> 102 us  [forward(): pl.pallas_call(functools.partial(forward_kernel, n, m, blocks, per, count...]
    pallas_call x1, Pallas kernels: 78.5 us -> 103 us  [token_layer(): pl.pallas_call(functools.partial(token_kernel, places, m), out_shape=(sds...]
where the time goes in v3:
time: 361 us; the launch traced here: 359 us
  Pallas kernels  326 us (90%)
  local copies, waits for them, and re-layouts  20.7 us (6%)
  other arithmetic  9.85 us (3%)
    pallas_call x1, Pallas kernels, token_layer(): pl.pallas_call(functools.partial(token_kernel, places, m), out_shape=(sds...  103 us
    pallas_call x1, Pallas kernels, forward(): pl.pallas_call(functools.partial(forward_kernel, n, m, blocks, per, count...  102 us
    pallas_call x1, Pallas kernels, backward(): pl.pallas_call(functools.partial(backward_kernel, n, m, blocks, per, coun...  93.2 us
    pallas_call x1, Pallas kernels, patch_out(): pl.pallas_call(patch_out_kernel, grid=(blocks,), out_shape=jax.ShapeDtype...  28.4 us

profile of v3, /device:TPU:0, one launch (start us, length us, event | category | flops | bytes accessed | tf_op | source)
XLA Modules:
  0.0 359.2 jit_solution(12379834286615948759)
XLA Ops:
  0.7 0.8 stack.28
  2.6 0.8 dynamic_update_slice.9
  3.4 0.8 copy.70
  5.7 0.7 tile.7
  6.6 0.7 maximum_maximum_fusion.pa_ref
  7.3 0.8 convert_bitcast_fusion
  9.0 0.7 pad.12.kx_ref
  10.9 102.2 %shard_map.356 = (bf16[8,768,768]{2,1,0:T(8,128)(2,1)}, bf16[2,2,128,768]{3,2,1,0:T(8,128)(2,1)}, f32[12544,128]{1,0:T(8,128)}, bf16[12544,128]{1,0:T(8,128)(2,1...) custom-call(bf16[12544,768]{1,0:T(8,128)(2,1)} %bitcast.72, ...), custom_call_target="tpu_custom_call" | custom-call | tf_op jit(solution)/shard_map/pallas_call | solution.py:409
  113.1 102.8 %shard_map.357 = (bf16[512,768]{1,0:T(8,128)(2,1)}, bf16[8,768,768]{2,1,0:T(8,128)(2,1)}, bf16[512,768]{1,0:T(8,128)(2,1)}, f32[8,768]{1,0:T(8,128)}, f32[1,3072]{1,0:T(1,128)}, /*index=5*/f32[192,768]{1,0:T(8,128)}) custom-call(bf16[512,768]{1,0:T(8,128)(2,1)} %bitcast.77, bf16[512,768]{1,0:T(8,128)(2,1)} %bitcast.76, ...), custom_call_target="tpu_custom_call" | custom-call | tf_op jit(solution)/shard_map/pallas_call | solution.py:742
  216.4 1.4 reduce.7
  218.0 1.4 select_maximum_fusion.vecs_ref
  220.6 93.2 %shard_map.358 = (bf16[12544,128]{1,0:T(8,128)(2,1)}, bf16[4,128,768]{2,1,0:T(8,128)(2,1)}, f32[8,48,768]{2,1,0:T(8,128)}, f32[96,256]{1,0:T(8,128)}, f32[80,128]{1,0:T(8,128)}) custom-call(bf16[12544,768]{1,0:T(8,128)(2,1)} %bitcast.73, f32[12544,128]{1,0:T(8,128)} %get-tuple-element.46.aux_hbm, bf16[12544,128]{1,0:T(8,128)(2,1)} %get-tuple-element.47.der_hbm, ...), custom_call_target="tpu_custom_call" | custom-call | tf_op jit(solution)/shard_map/pallas_call | solution.py:1160
  313.7 2.1 slice_bitcast_fusion.3
  315.8 0.9 pad_maximum_fusion
  316.7 0.8 pad_maximum_fusion.1
  318.1 1.4 multiply_add_fusion
  320.3 28.4 %shard_map.359 = bf16[12544,768]{1,0:T(8,128)(2,1)} custom-call(bf16[12544,768]{1,0:T(8,128)(2,1)} %bitcast.74, bf16[12544,128]{1,0:T(8,128)(2,1)} %get-tuple-element.45.sel_ref, bf16[12544,128]{1,0:T(8,128)(2,1)} %get-tuple-element.53.co_ref, bf16[4,128,768]{2,1,0:T(8,128)(2,1)} %get-tuple-element.54.gt_ref, bf16[128,768]{1,0:T(8,128)(2,1)} %get-tuple-element.55.bt_ref), custom_call_target="tpu_custom_call" | custom-call | tf_op jit(solution)/shard_map/pallas_call | solution.py:1218
  348.7 1.5 dynamic-slice_bitcast_fusion.1
  350.2 0.8 dynamic-slice.8
  351.6 1.3 dynamic-slice.4
  354.9 0.7 slice_reduce_fusion
  356.2 1.3 convolution_bitcast_fusion
  357.5 0.9 copy.83
  358.4 0.8 copy.84
  (46 shorter events, 11.3 us)
Async XLA Ops:
  2.6 8.3 %copy-start.2 = (bf16[16,384]{1,0:T(8,128)(2,1)}, bf16[16,384]{1,0:T(8,128)(2,1)S(1)}, u32[]{:S(2)}) copy-start(bf16[16,384]{1,0:T(8,128)(2,1)S(1)} %dynamic_update_slice.11.pb_ref) | copy-start | bytes 36868
  113.1 106.2 %copy-start.4 = (f32[72,128]{1,0:T(8,128)S(1)}, f32[72,128]{1,0:T(8,128)}, u32[]{:S(2)}) copy-start(f32[72,128]{1,0:T(8,128)} %get-tuple-element.50) | copy-start | bytes 110596
  320.3 35.9 %copy-start.3 = (bf16[48,64]{1,0:T(8,128)(2,1)S(1)}, bf16[48,64]{1,0:T(8,128)(2,1)}, u32[]{:S(2)}) copy-start(bf16[48,64]{1,0:T(8,128)(2,1)} %param.25) | copy-start | bytes 18436
  320.3 37.3 %copy-start = (bf16[512,768]{1,0:T(8,128)(2,1)S(1)}, bf16[512,768]{1,0:T(8,128)(2,1)}, u32[]{:S(2)}) copy-start(bf16[512,768]{1,0:T(8,128)(2,1)} %get-tuple-element.44) | copy-start | bytes 2359300
  320.3 38.1 %copy-start.1 = (f32[192,768]{1,0:T(8,128)S(1)}, f32[192,768]{1,0:T(8,128)}, u32[]{:S(2)}) copy-start(f32[192,768]{1,0:T(8,128)} %get-tuple-element.198) | copy-start | bytes 1769476

commit v4 on v3

--- a/solution.py
+++ b/solution.py
@@ -174,8 +174,8 @@
                 self.wait(i, self.at_core(p.na * side + k), s, p.half)
                 self.wait(i, self.at_core((2 + side) * p.na + k), s, 1 - p.half)
 
-    def finish(self):
-        for i in range(len(self.chunks)):
+    def finish(self, first=0):
+        for i in range(first, len(self.chunks)):
             self.from_core(i)
         for i, j, full in self.started:
             b = self.block(i, self.p.clip, None if full else self.p.half)
@@ -249,8 +249,8 @@
         small[-1].start()
     for d in local[1:]:
         d.wait()
-    chunks = [(wa_ref, pl.ds(2 * q, 2), shard, shard, 0, q != 2) for q in range(4)]
-    shards = [ws_ref.at[pl.ds(2 * q, 2)] for q in range(4)]
+    chunks = [(wa_ref, pl.ds(2 * q, 2), shard, shard, 0, q != 2) for q in range(3)]
+    shards = [ws_ref.at[pl.ds(2 * q, 2)] for q in range(3)]
     g = Gather(me, chunks, shards, gsend, grecv)
     todo = g.events()
     slots = [[] for _ in range(blocks + 1)]
@@ -391,8 +391,8 @@
     local[0].wait()
 
 
-STEP = 1.0
-AHEAD = 3
+STEP = 0.7
+AHEAD = 2
 
 
 def forward(n, m, v, kx, b2rep, pa, pb, wq, wo, w1, micros, frames, per, count):
@@ -448,10 +448,10 @@
 
 
 def token_kernel(
-    places, m, tok, cot, wa_hbm, w2s, vec, b1,
-    out_ref, ga_hbm, gtok_ref, gvec_ref, gb1_ref, ob_ref,
-    n1, joined, probs, att, mixed, n2, act, slope, gacc, gbr, tr, wa, w2, ga_ref, g2_ref,
-    own_b, rc_b, rx_b, ry_b, rz_b, rf_b, wsem, osem, lsem, gsend, grecv, rsend, rrecv,
+    places, m, tok, cot, wa_hbm, w1s, w2s, vec, b1,
+    out_ref, ga_hbm, gtok_ref, gvec_ref, gb1_ref, part_hbm,
+    n1, joined, probs, att, mixed, n2, act, slope, gacc, gbr, tr, wa, w2, ga_ref, g2_ref, wsv,
+    own_b, rc_b, rx_b, ry_b, wsem, osem, psem, lsem, gsend, grecv, rsend, rrecv,
 ):
     n, d = tok.shape
     ff = g2_ref.shape[1]
@@ -473,34 +473,46 @@
     def panel_out(q):
         return pltpu.make_async_copy(ga_ref.at[q], ga_hbm.at[q], osem.at[q])
 
-    for q in range(8):
+    for q in range(6):
         panel(q).start()
+    shard = w1s.shape[0]
+    for q in range(2):
+        wsv[q] = w1s[:, (2 + q) * d : (3 + q) * d]
+    own6 = pltpu.make_async_copy(
+        wsv, wa.at[pl.ds(6, 2), pl.ds(pl.multiple_of(me.clip * shard, 8), shard)], wsem.at[9]
+    )
+    own6.start()
     own = pltpu.make_async_copy(w2s, w2.at[pl.ds(pl.multiple_of(me.clip * fsh, 8), fsh)], wsem.at[8])
     own.start()
     me.greet()
     g = Gather(
         me,
-        [(w2, None, fsh // 2, fsh, q * (fsh // 2), q == 0) for q in range(2)],
-        [w2s.at[pl.ds(q * (fsh // 2), fsh // 2)] for q in range(2)],
+        [(wa, pl.ds(6, 2), shard, shard, 0, True)]
+        + [(w2, None, fsh // 2, fsh, q * (fsh // 2), q == 0) for q in range(2)],
+        [wsv] + [w2s.at[pl.ds(q * (fsh // 2), fsh // 2)] for q in range(2)],
         gsend,
         grecv,
     )
-    g.own(0)
-    g.own(1)
+    for i in range(3):
+        g.own(i)
     todo = [f for f in g.events() if f.func.__name__ != "own"]
-    early = [[] for _ in range(9 + micros * pairs + ff // cb)]
-    for at, f in enumerate(todo):
-        early[at * len(early) // len(todo)].append(f)
+    before, beside = 9 + micros * pairs, ff // cb
+    early = [[] for _ in range(before + beside)]
+    cut = 1 + max(at for at, f in enumerate(todo) if f.args[0] == 0)
+    for at, f in enumerate(todo[:cut]):
+        early[at * before // cut].append(f)
+    for at, f in enumerate(todo[cut:]):
+        early[before + at * beside // (len(todo) - cut)].append(f)
 
     red = Reduce(
         me, [(g2_ref, pl.ds(0, 1), fsh // 2, fsh, q * (fsh // 2), q == 0) for q in range(2)],
-        *([t.at[0], t.at[1]] for t in (own_b, rc_b, rx_b, ry_b, rz_b, rf_b)), lsem, rsend, rrecv,
+        *([t.at[0], t.at[1]] for t in (own_b, rc_b, rx_b, ry_b)), None, None, lsem, rsend, rrecv,
     )
 
-    def put_out(i, val):
-        ob_ref[i * (fsh // 2) : (i + 1) * (fsh // 2), :] = val[0]
-
-    steps = red.events(put_out)
+    steps = [functools.partial(f, i) for f in (red.stage1, red.stage2, red.add_second) for i in range(2)]
+
+    def part_out(i, k):
+        return pltpu.make_async_copy(red.own[i].at[2 * k], part_hbm.at[i, k], psem.at[i, k])
 
     def at_step(i, slots):
         for at, fs in enumerate(slots):
@@ -567,13 +579,12 @@
             mine = first if e == 0 else jnp.logical_not(first)
             s = dot_nt(jnp.where(mine, q, zero), k)
             ex = jnp.exp(s - jnp.max(s, axis=-1, keepdims=True))
-            p = ex / jnp.sum(ex, axis=-1, keepdims=True)
-            low = p.astype(BF)
+            low = (ex * (1.0 / jnp.sum(ex, axis=-1, keepdims=True))).astype(BF)
             probs[i * 2 + e] = low
             total = total + dot(low, jnp.where(mine, v, zero))
         put_heads(att, i, 0, total.astype(BF))
 
-    for q in range(3, 8):
+    for q in range(3, 6):
         panel(q).wait()
 
     @pl.loop(0, d // cb)
@@ -585,6 +596,9 @@
     def _(i):
         xh, _ = ln_stats(mixed[rows_of(i), :])
         n2[rows_of(i), :] = (xh * vec[5:6, :] + vec[6:7, :]).astype(BF)
+
+    g.from_core(0)
+    own6.wait()
 
     @pl.loop(0, ff // cb)
     def _(j):
@@ -601,7 +615,7 @@
 
     red.stage0(0)
     red.stage0(1)
-    g.finish()
+    g.finish(1)
     own.wait()
 
     @pl.loop(0, d // cb)
@@ -662,7 +676,7 @@
 
     panel_out(3).start()
     late = [[] for _ in range(micros * pairs)]
-    late[len(late) // 4] = steps[4:6]
+    late[len(late) // 2] = steps[4:6]
 
     @pl.loop(0, micros * pairs)
     def _(i):
@@ -690,8 +704,9 @@
         put_heads(joined, i, 2 * d, gv.astype(BF))
 
     transpose_into(n1)
-    for f in steps[6:8]:
-        f()
+    for i in range(2):
+        for k in range(me.na):
+            part_out(i, k).start()
 
     @pl.loop(0, 3 * d // cb)
     def _(j):
@@ -722,14 +737,15 @@
         back = eg - jnp.mean(eg, axis=-1, keepdims=True) - xh * jnp.mean(eg * xh, axis=-1, keepdims=True)
         gtok_ref[r, :] = (mixed[r, :] + back * rstd).astype(BF)
 
-    for f in steps[8:]:
-        f()
+    for i in range(2):
+        for k in range(me.na):
+            part_out(i, k).wait()
     for q in range(8):
         panel_out(q).wait()
-    red.finish()
-
-
-def token_layer(places, m, tok, cot, wa, w2s, vec, b1):
+    red.finish(second=False)
+
+
+def token_layer(places, m, tok, cot, wa, w1s, w2s, vec, b1):
     n, d = tok.shape
     fsh = w2s.shape[0]
     ff = places * fsh
@@ -742,10 +758,11 @@
     return pl.pallas_call(
         functools.partial(token_kernel, places, m),
         out_shape=(
-            sds((n, d), BF), sds(wa.shape, BF), sds((n, d), BF), sds((8, d), F32), sds((1, ff), F32), sds((fsh, d), F32),
+            sds((n, d), BF), sds(wa.shape, BF), sds((n, d), BF), sds((8, d), F32), sds((1, ff), F32),
+            sds((2, na, 1, fsh // 2, d), BF),
         ),
-        in_specs=[vm, vm, hb, vm, vm, vm],
-        out_specs=(vm, hb, vm, vm, vm, vm),
+        in_specs=[vm, vm, hb, vm, vm, vm, vm],
+        out_specs=(vm, hb, vm, vm, vm, hb),
         scratch_shapes=[
             pltpu.VMEM((n, d), BF),
             pltpu.VMEM((n, 3 * d), BF),
@@ -762,11 +779,12 @@
             pltpu.VMEM((ff, d), BF),
             pltpu.VMEM(wa.shape, BF),
             pltpu.VMEM((1, ff, d), BF),
+            pltpu.VMEM((2, w1s.shape[0], d), BF),
         ]
-        + reduce_buffers(na, 2, 1, fsh // 2, d)
-        + [dma((9,)), dma((8,)), dma((2, 2 * na)), dma((22 * na,)), dma((22 * na,)), dma((16 * na,)), dma((16 * na,))],
+        + reduce_buffers(na, 2, 1, fsh // 2, d)[:4]
+        + [dma((10,)), dma((8,)), dma((2, na)), dma((2, 2 * na)), dma((33 * na,)), dma((33 * na,)), dma((16 * na,)), dma((16 * na,))],
         compiler_params=pltpu.CompilerParams(vmem_limit_bytes=VLIM, collective_id=2, has_side_effects=True),
-    )(tok, cot, wa, w2s, vec, b1)
+    )(tok, cot, wa, w1s, w2s, vec, b1)
 
 
 def reduce_buffers(na, chunks, panels, rows, width):
@@ -912,11 +930,14 @@
             self.add_y(i)
             self.start(i, self.x_copies(i))
 
-    def stage3(self, i):
+    def add_second(self, i):
         if self.chunks[i][5]:
             self.add_y(i)
         else:
             self.add_x(i)
+
+    def stage3(self, i):
+        self.add_second(i)
         self.start(i, self.z_copies(i))
 
     def stage4(self, i):
@@ -942,21 +963,23 @@
                         out.append(call(self.stage5, i, put) if s == 5 else call(getattr(self, "stage%d" % s), i))
         return out
 
-    def finish(self):
+    def finish(self, first=True, second=True):
+        kinds = [self.core_copies, self.x_copies, self.y_copies] if first else []
+        kinds += [self.z_copies, self.last_copies] if second else []
         for i in range(len(self.chunks)):
-            for c in (self.core_copies, self.x_copies, self.y_copies, self.z_copies, self.last_copies):
+            for c in kinds:
                 for at, src, dst, dev in c(i):
                     s, r = self.sem(i, at)
                     remote(src, src, s, r, self.p.core_dev).wait_send()
 
 
 def backward_kernel(
-    n, m, blocks, per, count, v_ref, aux_hbm, der_hbm, gtok_ref, ga_ref, w1s_ref, w2_ref, vecs_ref,
-    co_hbm, gt_ref, oa_ref, win_ref, tot_ref,
+    n, m, blocks, per, count, v_ref, aux_hbm, der_hbm, gtok_ref, ga_ref, part_hbm, w1s_ref, w2_ref, vecs_ref,
+    co_hbm, gt_ref, oa_ref, ob_ref, win_ref, tot_ref,
     vbuf, aux_ref, der_ref, co_ref, gin, x_ref, w2g_ref, row_ref,
-    own_a, rc_a, rx_a, ry_a, rz_a, rf_a,
+    own_a, rc_a, rx_a, ry_a, rz_a, rf_a, own_b, rz_b, rf_b,
     ms, mc, mx, my, mz, md, tc, tx, ty, tz, td, te,
-    vsem, asem, dsem, csem, lsem, rsend, rrecv, tsend, trecv, ssend, srecv,
+    vsem, asem, dsem, csem, psem, lsem, rsend, rrecv, bsend, brecv, tsend, trecv, ssend, srecv,
 ):
     rows, width = v_ref.shape
     rb = rows // blocks
@@ -976,6 +999,12 @@
         r = pl.ds(i * rb, rb)
         return pltpu.make_async_copy(co_ref.at[r], co_hbm.at[r], csem.at[i])
 
+    def part_in(i, k):
+        return pltpu.make_async_copy(part_hbm.at[i, k], own_b.at[i, 2 * k], psem.at[i, k])
+
+    for i in range(2):
+        for k in range(me.na):
+            part_in(i, k).start()
     me.greet()
     out = []
     for mi in range(micros):
@@ -994,6 +1023,18 @@
     )
     for i in range(4):
         red.stage0(i)
+    half_fsh = ob_ref.shape[0] // 2
+    fin = Reduce(
+        me, [(ob_ref, None, half_fsh, half_fsh, 0, q == 0) for q in range(2)], [own_b.at[0], own_b.at[1]], None, None, None,
+        [rz_b.at[0], rz_b.at[1]], [rf_b.at[0], rf_b.at[1]], None, bsend, brecv,
+    )
+    for i in range(2):
+        for k in range(me.na):
+            part_in(i, k).wait()
+        fin.start(i, fin.z_copies(i))
+
+    def put_fc2(i, val):
+        ob_ref[i * half_fsh : (i + 1) * half_fsh, :] = val[0]
 
     def put_out(i, val):
         oa_ref[2 * order[i] : 2 * order[i] + 2] = val
@@ -1009,6 +1050,8 @@
     lane = lax.broadcasted_iota(jnp.int32, (rb, LANES), 1)
 
     todo = red.events(put_out)
+    todo[8:8] = [functools.partial(fin.stage4, i) for i in range(2)]
+    todo[16:16] = [functools.partial(fin.stage5, i, put_fc2) for i in range(2)]
     slots = [[] for _ in range(blocks + 1)]
     for at, f in enumerate(todo[2:]):
         slots[min(int(at * RSTEP * blocks / len(todo)), blocks)].append(f)
@@ -1142,12 +1185,13 @@
         put(i).wait()
 
     red.finish()
+    fin.finish(first=False)
 
 
 RSTEP = 1.6
 
 
-def backward(n, m, v, aux, der, gtok, ga, w1s, w2n, vecs, blocks, per, count):
+def backward(n, m, v, aux, der, gtok, ga, part, w1s, w2n, vecs, blocks, per, count):
     rows, width = v.shape
     rb = rows // blocks
     na, shard = n // 4, width // n
@@ -1161,10 +1205,10 @@
         functools.partial(backward_kernel, n, m, blocks, per, count),
         out_shape=(
             sds((rows, LANES), BF), sds((micros * m, LANES, width), BF), sds((8, shard, width), F32),
-            sds((96, 256), F32), sds((80, LANES), F32),
+            sds((2 * part.shape[3], width), F32), sds((96, 256), F32), sds((80, LANES), F32),
         ),
-        in_specs=[hb] * 5 + [vm] * 3,
-        out_specs=(hb,) + (vm,) * 4,
+        in_specs=[hb] * 6 + [vm] * 3,
+        out_specs=(hb,) + (vm,) * 5,
         scratch_shapes=[
             pltpu.VMEM((rows, width), BF),
             pltpu.VMEM((rows, LANES), F32),
@@ -1176,6 +1220,7 @@
             pltpu.VMEM((8, LANES), F32),
         ]
         + reduce_buffers(na, 4, 2, shard, width)
+        + [reduce_buffers(na, 2, 1, part.shape[3], width)[q] for q in (0, 4, 5)]
         + [
             pltpu.VMEM((96, width), BF),
             pltpu.VMEM((96, width), BF),
@@ -1191,10 +1236,10 @@
             pltpu.VMEM((40, LANES), F32),
         ]
         + [dma((blocks,))] * 4
-        + [dma((6, 2 * na)), dma((6 * 8 * na,)), dma((6 * 8 * na,)), dma((micros * m,)), dma((micros * m,))]
+        + [dma((2, na)), dma((6, 2 * na)), dma((6 * 8 * na,)), dma((6 * 8 * na,)), dma((16 * na,)), dma((16 * na,)), dma((micros * m,)), dma((micros * m,))]
         + [dma((2, na + 3)), dma((2, na + 3))],
         compiler_params=pltpu.CompilerParams(vmem_limit_bytes=VLIM, collective_id=1, has_side_effects=True),
-    )(v, aux, der, gtok, ga, w1s, w2n, vecs)
+    )(v, aux, der, gtok, ga, part, w1s, w2n, vecs)
 
 
 def patch_out_kernel(v_ref, sel_ref, co_ref, gt_ref, bt_ref, o_ref):
@@ -1265,15 +1310,15 @@
     w1s = small[0:8]
     w2n = jnp.pad(small[8:72].astype(BF), ((0, 64), (0, 0)))
     ff = fc1_weight.shape[1]
-    out, ga, gtok, gvec, gb1, ob = token_layer(
-        n, m, tok, cotangent.reshape(tok.shape), wa, fc2_weight, vec, fb
+    out, ga, gtok, gvec, gb1, part = token_layer(
+        n, m, tok, cotangent.reshape(tok.shape), wa, fc1_weight, fc2_weight, vec, fb
     )
     vecs = jnp.concatenate([gvec, jnp.swapaxes(gb1.reshape(n, -1, shard), 0, 1).reshape(-1, width)])
     vecs = jnp.pad(vecs, ((0, 16 - vecs.shape[0]), (0, 0)))
-    co, gts, oa, win, tot = backward(
-        n, m, v, aux, der, gtok.reshape(micros, m, -1, width), ga, w1s, w2n, vecs, blocks, per, count
+    co, gts, oa, ob, win, tot = backward(
+        n, m, v, aux, der, gtok.reshape(micros, m, -1, width), ga, part, w1s, w2n, vecs, blocks, per, count
     )
-    pg = patch_out(v, sel, co, gts, bt, blocks, per)
+    pg = patch_out(v, sel, co, gts, bt, groups * 2, 2)
     pg = jnp.transpose(pg.reshape(micros, group, count, frames, width), (0, 1, 3, 2, 4))
     if m > 2:
         oa, ob, win, tot = (lax.psum(t, "map") * 0.5 for t in (oa, ob, win, tot))

time: 361 us -> 348 us (0.964)
  Pallas kernels: 326 us -> 315 us
    pallas_call x1, Pallas kernels: 28.4 us -> 21.1 us  [patch_out(): pl.pallas_call(patch_out_kernel, grid=(blocks,), out_shape=jax.ShapeDtype...]
    pallas_call x1, Pallas kernels: 102 us -> 95.3 us  [forward(): pl.pallas_call(functools.partial(forward_kernel, n, m, blocks, per, count...]
where the time goes in v4:
time: 348 us
  Pallas kernels  315 us (91%)
  local copies, waits for them, and re-layouts  20.1 us (6%)
  other arithmetic  9.85 us (3%)
    pallas_call x1, Pallas kernels, token_layer(): pl.pallas_call(functools.partial(token_kernel, places, m), out_shape=(sds...  104 us
    pallas_call x1, Pallas kernels, backward(): pl.pallas_call(functools.partial(backward_kernel, n, m, blocks, per, coun...  95.4 us
    pallas_call x1, Pallas kernels, forward(): pl.pallas_call(functools.partial(forward_kernel, n, m, blocks, per, count...  95.3 us
    pallas_call x1, Pallas kernels, patch_out(): pl.pallas_call(patch_out_kernel, grid=(blocks,), out_shape=jax.ShapeDtype...  21.1 us

profile of v4, /device:TPU:0, one launch (start us, length us, event | category | flops | bytes accessed | tf_op | source)
XLA Modules:
  0.0 347.5 jit_solution(15678692673111123118)
XLA Ops:
  0.7 0.8 stack.28
  2.6 0.8 dynamic_update_slice.9
  3.4 0.8 copy.70
  5.7 0.7 tile.7
  6.6 0.7 maximum_maximum_fusion.pa_ref
  7.3 0.8 convert_bitcast_fusion
  9.0 0.7 pad.12.kx_ref
  10.3 95.3 %shard_map.356 = (bf16[8,768,768]{2,1,0:T(8,128)(2,1)}, bf16[2,2,128,768]{3,2,1,0:T(8,128)(2,1)}, f32[12544,128]{1,0:T(8,128)}, bf16[12544,128]{1,0:T(8,128)(2,1...) custom-call(bf16[12544,768]{1,0:T(8,128)(2,1)} %bitcast.72, ...), custom_call_target="tpu_custom_call" | custom-call | tf_op jit(solution)/shard_map/pallas_call | solution.py:409
  105.6 103.7 %shard_map.357 = (bf16[512,768]{1,0:T(8,128)(2,1)}, bf16[8,768,768]{2,1,0:T(8,128)(2,1)}, bf16[512,768]{1,0:T(8,128)(2,1)}, f32[8,768]{1,0:T(8,128)}, f32[1,3072...) custom-call(bf16[512,768]{1,0:T(8,128)(2,1)} %bitcast.79, bf16[512,768]{1,0:T(8,128)(2,1)} %bitcast.77, ...), custom_call_target="tpu_custom_call" | custom-call | tf_op jit(solution)/shard_map/pallas_call | solution.py:758
  209.8 1.4 reduce.7
  211.4 1.4 select_maximum_fusion.vecs_ref
  214.0 95.4 %shard_map.358 = (bf16[12544,128]{1,0:T(8,128)(2,1)}, bf16[4,128,768]{2,1,0:T(8,128)(2,1)}, f32[8,48,768]{2,1,0:T(8,128)}, f32[192,768]{1,0:T(8,128)}, f32[96,256]{1,0:T(8,128)}, /*index=5*/f32[80,128]{1,0:T(8,128)}) custom-call(bf16[12544,768]{1,0:T(8,128)(2,1)} %bitcast.73, f32[12544,128]{1,0:T(8,128)} %get-tuple-element.47.aux_hbm, ...), custom_call_target="tpu_custom_call" | custom-call | tf_op jit(solution)/shard_map/pallas_call | solution.py:1204
  309.4 2.1 slice_bitcast_fusion.3
  311.4 0.9 pad_maximum_fusion
  312.3 0.8 pad_maximum_fusion.1
  313.8 1.4 multiply_add_fusion
  315.9 21.1 %shard_map.359 = bf16[12544,768]{1,0:T(8,128)(2,1)} custom-call(bf16[12544,768]{1,0:T(8,128)(2,1)} %bitcast.74, bf16[12544,128]{1,0:T(8,128)(2,1)} %get-tuple-element.46.sel_ref, bf16[12544,128]{1,0:T(8,128)(2,1)} %get-tuple-element.55.co_ref, bf16[4,128,768]{2,1,0:T(8,128)(2,1)} %get-tuple-element.56.gt_ref, bf16[128,768]{1,0:T(8,128)(2,1)} %get-tuple-element.57.bt_ref), custom_call_target="tpu_custom_call" | custom-call | tf_op jit(solution)/shard_map/pallas_call | solution.py:1263
  337.0 1.5 dynamic-slice_bitcast_fusion.1
  338.5 0.8 dynamic-slice.8
  339.9 1.3 dynamic-slice.4
  343.2 0.7 slice_reduce_fusion
  344.5 1.3 convolution_bitcast_fusion
  345.8 0.9 copy.83
  346.7 0.8 copy.84
  (48 shorter events, 10.7 us)
Async XLA Ops:
  0.7 9.0 %copy-start.5 = (bf16[8]{0:T(256)(128)(2,1)S(1)}, bf16[8]{0:T(256)(128)(2,1)}, u32[]{:S(2)}) copy-start(bf16[8]{0:T(256)(128)(2,1)} %param.28) | copy-start | bytes 52
  2.6 7.7 %copy-start.2 = (bf16[16,384]{1,0:T(8,128)(2,1)}, bf16[16,384]{1,0:T(8,128)(2,1)S(1)}, u32[]{:S(2)}) copy-start(bf16[16,384]{1,0:T(8,128)(2,1)S(1)} %dynamic_update_slice.11.pb_ref) | copy-start | bytes 36868
  105.6 107.2 %copy-start.4 = (f32[72,128]{1,0:T(8,128)S(1)}, f32[72,128]{1,0:T(8,128)}, u32[]{:S(2)}) copy-start(f32[72,128]{1,0:T(8,128)} %get-tuple-element.52) | copy-start | bytes 110596
  315.9 28.6 %copy-start.3 = (bf16[48,64]{1,0:T(8,128)(2,1)S(1)}, bf16[48,64]{1,0:T(8,128)(2,1)}, u32[]{:S(2)}) copy-start(bf16[48,64]{1,0:T(8,128)(2,1)} %param.25) | copy-start | bytes 18436
  315.9 30.0 %copy-start = (bf16[512,768]{1,0:T(8,128)(2,1)S(1)}, bf16[512,768]{1,0:T(8,128)(2,1)}, u32[]{:S(2)}) copy-start(bf16[512,768]{1,0:T(8,128)(2,1)} %get-tuple-element.45) | copy-start | bytes 2359300
  315.9 30.8 %copy-start.1 = (f32[192,768]{1,0:T(8,128)S(1)}, f32[192,768]{1,0:T(8,128)}, u32[]{:S(2)}) copy-start(f32[192,768]{1,0:T(8,128)} %get-tuple-element.200) | copy-start | bytes 1769476
